TPU v7x, 32 devices: a whole 2x2x4 slice. The times are simulated.
32 devices in a mesh: ctx: 8 (over y, x, core), fsdp: 4 (over z).
Axes of the slice: x: 2, y: 2, z: 4, core: 2. Of those that a mesh axis runs over, the one named last changes fastest.
Arguments:
- hidden_in: bfloat16 [4, 2048, 1536], P('fsdp', 'ctx'), may hold values from -6 to 6
- positions: int32 [4, 2048], P('fsdp', 'ctx'), may hold values from 0 to 6142, as said below
- attn_gain: bfloat16 [1536], P('fsdp'), may hold values from 0.5 to 1.5
- w_query: bfloat16 [1536, 1536], P('fsdp'), may hold values from -0.15625 to 0.15625
- key_projection: bfloat16 [1536, 768], P('fsdp'), may hold values from -0.15625 to 0.15625
- value_projection: bfloat16 [1536, 768], P('fsdp'), may hold values from -0.15625 to 0.15625
- w_out: bfloat16 [1536, 1536], P('fsdp'), may hold values from -1.75 to 1.75
- mlp_gain: bfloat16 [1536], P('fsdp'), may hold values from 0.5 to 1.5
- w_gate: bfloat16 [1536, 4096], P('fsdp'), may hold values from -0.15625 to 0.15625
- w_up: bfloat16 [1536, 4096], P('fsdp'), may hold values from -0.15625 to 0.15625
- w_down: bfloat16 [4096, 1536], P('fsdp'), may hold values from -0.09375 to 0.09375
- out_grad: bfloat16 [4, 2048, 1536], P('fsdp', 'ctx'), may hold values from -6 to 6
Outputs:
- layer_out: bfloat16 [4, 2048, 1536], P('fsdp', 'ctx')
- input_grad: bfloat16 [4, 2048, 1536], P('fsdp', 'ctx')
- attn_gain_grad: float32 [1536], P('fsdp')
- w_query_grad: float32 [1536, 1536], P('fsdp')
- w_key_grad: float32 [1536, 768], P('fsdp')
- w_value_grad: float32 [1536, 768], P('fsdp')
- w_out_grad: float32 [1536, 1536], P('fsdp')
- mlp_gain_grad: float32 [1536], P('fsdp')
- w_gate_grad: float32 [1536, 4096], P('fsdp')
- w_up_grad: float32 [1536, 4096], P('fsdp')
- w_down_grad: float32 [4096, 1536], P('fsdp')
Inputs may be any that keep to these rules, and one draw needn't show every extreme that they name: For each sequence the positions are s, s + 1, ..., s + 2047, each once, with a start s of 0 to 4095; one sequence starts at 0 and another at 4095; every device along ctx holds two blocks of 128 consecutive positions whose block numbers counted from s add up to 15, in either order.
All inputs are finite; a program needn't handle non-finite values.
Results may differ from a plain program's by a relative error of at most 0.023.
Values may be sent and summed in bfloat16 or wider, within the bound.
A program may use at most 448 MiB of HBM per device.

v0:
```python
import math

import jax
import jax.numpy as jnp
from jax import lax
from jax.sharding import PartitionSpec as P

QUERY_HEADS = 16
KEY_VALUE_HEADS = 8
HEAD_SIZE = 96


EPS = 1e-05
THETA = 100000.0


def tables(token_position):
    half = HEAD_SIZE // 2
    freq = THETA ** (-(jnp.arange(half, dtype=jnp.float32) * 2.0 / HEAD_SIZE))
    angle = token_position.astype(jnp.float32)[:, None] * freq[None, :]
    return (jnp.cos(angle)[:, None, :], jnp.sin(angle)[:, None, :])


def rotary_embed(value_rows, cosine_table, sine_table):
    half = value_rows.shape[-1] // 2
    first = value_rows[..., :half]
    second = value_rows[..., half:]
    return jnp.concatenate(
        [first * cosine_table - second * sine_table, second * cosine_table + first * sine_table], -1
    )


def rotary_embed_backward(grads, cosine_table, sine_table):
    half = grads.shape[-1] // 2
    first = grads[..., :half]
    second = grads[..., half:]
    return jnp.concatenate(
        [first * cosine_table + second * sine_table, second * cosine_table - first * sine_table], -1
    )


def norm_forward(hidden, gain):
    return (
        hidden
        * lax.rsqrt(jnp.mean(hidden * hidden, -1, keepdims=True) + EPS)
        * gain.astype(jnp.float32)
    )


def norm_back(hidden, gain, grad):
    factor = lax.rsqrt(jnp.mean(hidden * hidden, -1, keepdims=True) + EPS)
    scaled = grad * gain.astype(jnp.float32)
    hidden_grad = factor * scaled - hidden * factor * factor * factor * jnp.mean(
        scaled * hidden, -1, keepdims=True
    )
    gain_grad = jnp.sum(grad * hidden * factor, 0)
    return (hidden_grad, gain_grad)


def dot_first(left, right):
    return lax.dot_general(
        left, right, (((0,), (0,)), ((), ())), preferred_element_type=jnp.float32
    )


def dot_last(left, right):
    return lax.dot_general(
        left, right, (((1,), (1,)), ((), ())), preferred_element_type=jnp.float32
    )


def over_blocks(step_fn, carry, arrays):
    block_count = arrays[0].shape[0]
    size = math.gcd(block_count, 512)
    parts = block_count // size
    shaped = tuple((item.reshape((parts, size) + item.shape[1:]) for item in arrays))

    def advance(state, inputs):
        index, pieces = inputs
        return (step_fn(state, pieces, index * size), None)

    final, unused = lax.scan(advance, carry, (jnp.arange(parts, dtype=jnp.int32), shaped))
    return final


def per_device(
    hidden_in,
    positions,
    attn_gain,
    w_query,
    key_projection,
    value_projection,
    w_out,
    mlp_gain,
    w_gate,
    w_up,
    w_down,
    out_grad,
):
    hidden = hidden_in[0].astype(jnp.float32)
    local_rows = hidden.shape[0]
    query_pos = positions[0]
    query_groups = QUERY_HEADS // KEY_VALUE_HEADS
    scale = HEAD_SIZE ** (-0.5)
    cosine_table, sine_table = tables(query_pos)
    attn_set = (
        lax.all_gather(attn_gain, "fsdp", axis=0, tiled=True),
        lax.all_gather(w_query, "fsdp", axis=0, tiled=True),
        lax.all_gather(key_projection, "fsdp", axis=0, tiled=True),
        lax.all_gather(value_projection, "fsdp", axis=0, tiled=True),
        lax.all_gather(w_out, "fsdp", axis=0, tiled=True),
    )
    gain_one, query_w, key_matrix, value_matrix, out_w = attn_set
    first_normed = norm_forward(hidden, gain_one).astype(jnp.bfloat16)
    query_raw = jnp.dot(first_normed, query_w, preferred_element_type=jnp.float32)
    unrotated_key = jnp.dot(first_normed, key_matrix, preferred_element_type=jnp.float32)
    value_raw = jnp.dot(first_normed, value_matrix, preferred_element_type=jnp.float32)
    query_rows = (
        rotary_embed(
            query_raw.reshape(local_rows, QUERY_HEADS, HEAD_SIZE), cosine_table, sine_table
        )
        .astype(jnp.bfloat16)
        .reshape(local_rows, KEY_VALUE_HEADS, query_groups, HEAD_SIZE)
    )
    keys_flat = (
        rotary_embed(
            unrotated_key.reshape(local_rows, KEY_VALUE_HEADS, HEAD_SIZE), cosine_table, sine_table
        )
        .astype(jnp.bfloat16)
        .reshape(local_rows, KEY_VALUE_HEADS * HEAD_SIZE)
    )
    values_flat = value_raw.astype(jnp.bfloat16)
    key_pos_all = lax.all_gather(query_pos, "ctx", axis=0, tiled=True)
    sequence_length = key_pos_all.shape[0]

    def masked_scores(partial_keys, first):
        block_count = partial_keys.shape[0]
        key_pos = lax.dynamic_slice_in_dim(key_pos_all, first, block_count)
        scores = (
            jnp.einsum(
                "tkgd,nkd->kgtn",
                query_rows,
                partial_keys.reshape(block_count, KEY_VALUE_HEADS, HEAD_SIZE),
                preferred_element_type=jnp.float32,
            )
            * scale
        )
        visible = key_pos[None, None, None, :] <= query_pos[None, None, :, None]
        return jnp.where(visible, scores, -jnp.inf)

    def forward_part(carry, part, first):
        top, denom, accum = carry
        partial_keys, partial_values = part
        block_count = partial_keys.shape[0]
        scores = masked_scores(partial_keys, first)
        new_top = jnp.maximum(top, jnp.max(scores, -1))
        weights = jnp.exp(scores - new_top[..., None])
        factor = jnp.exp(top - new_top)
        denom = denom * factor + jnp.sum(weights, -1)
        accum = accum * factor[..., None] + jnp.einsum(
            "kgtn,nkd->kgtd",
            weights.astype(jnp.bfloat16),
            partial_values.reshape(block_count, KEY_VALUE_HEADS, HEAD_SIZE),
            preferred_element_type=jnp.float32,
        )
        return (new_top, denom, accum)

    start_state = (
        jnp.full((KEY_VALUE_HEADS, query_groups, local_rows), -1e30, jnp.float32),
        jnp.zeros((KEY_VALUE_HEADS, query_groups, local_rows), jnp.float32),
        jnp.zeros((KEY_VALUE_HEADS, query_groups, local_rows, HEAD_SIZE), jnp.float32),
    )
    top, denom, accum = over_blocks(
        forward_part,
        start_state,
        (
            lax.all_gather(keys_flat, "ctx", axis=0, tiled=True),
            lax.all_gather(values_flat, "ctx", axis=0, tiled=True),
        ),
    )
    attended_output = accum / denom[..., None]
    log_total = top + jnp.log(denom)
    attended_low = (
        attended_output.transpose(2, 0, 1, 3)
        .reshape(local_rows, QUERY_HEADS * HEAD_SIZE)
        .astype(jnp.bfloat16)
    )
    mixed = hidden + jnp.dot(attended_low, out_w, preferred_element_type=jnp.float32)
    mlp_set = (
        lax.all_gather(mlp_gain, "fsdp", axis=0, tiled=True),
        lax.all_gather(w_gate, "fsdp", axis=0, tiled=True),
        lax.all_gather(w_up, "fsdp", axis=0, tiled=True),
        lax.all_gather(w_down, "fsdp", axis=0, tiled=True),
    )
    gain_two, gate_w, up_w, down_w = mlp_set
    normed_two = norm_forward(mixed, gain_two).astype(jnp.bfloat16)
    gate = jnp.dot(normed_two, gate_w, preferred_element_type=jnp.float32)
    up = jnp.dot(normed_two, up_w, preferred_element_type=jnp.float32)
    sigma = jax.nn.sigmoid(gate)
    active = (gate * sigma * up).astype(jnp.bfloat16)
    result = mixed + jnp.dot(active, down_w, preferred_element_type=jnp.float32)
    layer_out = result.astype(jnp.bfloat16)[None]
    grad_low = out_grad[0]
    grad_out = grad_low.astype(jnp.float32)
    gain_back, gate_back, up_back, down_back = (
        lax.all_gather(mlp_gain, "fsdp", axis=0, tiled=True),
        lax.all_gather(w_gate, "fsdp", axis=0, tiled=True),
        lax.all_gather(w_up, "fsdp", axis=0, tiled=True),
        lax.all_gather(w_down, "fsdp", axis=0, tiled=True),
    )
    down_grad = dot_first(active, grad_low)
    active_grad = dot_last(grad_low, down_back)
    gate_grad = (active_grad * up * sigma * (1.0 + gate * (1.0 - sigma))).astype(jnp.bfloat16)
    up_grad = (active_grad * gate * sigma).astype(jnp.bfloat16)
    gate_wgrad = dot_first(normed_two, gate_grad)
    up_wgrad = dot_first(normed_two, up_grad)
    normed_two_grad = dot_last(gate_grad, gate_back) + dot_last(up_grad, up_back)
    mixed_part, gain_two_grad = norm_back(mixed, gain_back, normed_two_grad)
    mixed_grad = grad_out + mixed_part
    mlp_shards = (
        lax.psum_scatter(
            gain_two_grad.astype(jnp.bfloat16), "fsdp", scatter_dimension=0, tiled=True
        ).astype(jnp.float32),
        lax.psum_scatter(
            gate_wgrad.astype(jnp.bfloat16), "fsdp", scatter_dimension=0, tiled=True
        ).astype(jnp.float32),
        lax.psum_scatter(
            up_wgrad.astype(jnp.bfloat16), "fsdp", scatter_dimension=0, tiled=True
        ).astype(jnp.float32),
        lax.psum_scatter(
            down_grad.astype(jnp.bfloat16), "fsdp", scatter_dimension=0, tiled=True
        ).astype(jnp.float32),
    )
    gain_first, query_back, key_back, value_back, out_back = (
        lax.all_gather(attn_gain, "fsdp", axis=0, tiled=True),
        lax.all_gather(w_query, "fsdp", axis=0, tiled=True),
        lax.all_gather(key_projection, "fsdp", axis=0, tiled=True),
        lax.all_gather(value_projection, "fsdp", axis=0, tiled=True),
        lax.all_gather(w_out, "fsdp", axis=0, tiled=True),
    )
    branch_grad = mixed_grad.astype(jnp.bfloat16)
    out_wgrad = dot_first(attended_low, branch_grad)
    attended_grad = (
        dot_last(branch_grad, out_back)
        .astype(jnp.bfloat16)
        .reshape(local_rows, KEY_VALUE_HEADS, query_groups, HEAD_SIZE)
        .transpose(1, 2, 0, 3)
    )
    delta = jnp.sum(attended_grad.astype(jnp.float32) * attended_output, -1)

    def backward_part(carry, part, first):
        query_acc, key_value_acc = carry
        partial_keys, partial_values = part
        block_count = partial_keys.shape[0]
        probs = jnp.exp(masked_scores(partial_keys, first) - log_total[..., None])
        gradient_of_value = jnp.einsum(
            "kgtn,kgtd->nkd",
            probs.astype(jnp.bfloat16),
            attended_grad,
            preferred_element_type=jnp.float32,
        )
        prob_grad = jnp.einsum(
            "kgtd,nkd->kgtn",
            attended_grad,
            partial_values.reshape(block_count, KEY_VALUE_HEADS, HEAD_SIZE),
            preferred_element_type=jnp.float32,
        )
        score_grad = (probs * (prob_grad - delta[..., None])).astype(jnp.bfloat16)
        query_acc = (
            query_acc
            + jnp.einsum(
                "kgtn,nkd->kgtd",
                score_grad,
                partial_keys.reshape(block_count, KEY_VALUE_HEADS, HEAD_SIZE),
                preferred_element_type=jnp.float32,
            )
            * scale
        )
        gradient_of_key = (
            jnp.einsum("kgtn,tkgd->nkd", score_grad, query_rows, preferred_element_type=jnp.float32)
            * scale
        )
        joined = jnp.concatenate(
            [
                gradient_of_key.reshape(block_count, KEY_VALUE_HEADS * HEAD_SIZE),
                gradient_of_value.reshape(block_count, KEY_VALUE_HEADS * HEAD_SIZE),
            ],
            1,
        )
        key_value_acc = lax.dynamic_update_slice_in_dim(key_value_acc, joined, first, 0)
        return (query_acc, key_value_acc)

    back_state = (
        jnp.zeros((KEY_VALUE_HEADS, query_groups, local_rows, HEAD_SIZE), jnp.float32),
        jnp.zeros((sequence_length, 2 * KEY_VALUE_HEADS * HEAD_SIZE), jnp.float32),
    )
    query_acc, key_value_acc = over_blocks(
        backward_part,
        back_state,
        (
            lax.all_gather(keys_flat, "ctx", axis=0, tiled=True),
            lax.all_gather(values_flat, "ctx", axis=0, tiled=True),
        ),
    )
    local_key_value = lax.psum_scatter(
        key_value_acc.astype(jnp.bfloat16), "ctx", scatter_dimension=0, tiled=True
    ).astype(jnp.float32)
    query_raw_grad = (
        rotary_embed_backward(
            query_acc.transpose(2, 0, 1, 3).reshape(local_rows, QUERY_HEADS, HEAD_SIZE),
            cosine_table,
            sine_table,
        )
        .reshape(local_rows, QUERY_HEADS * HEAD_SIZE)
        .astype(jnp.bfloat16)
    )
    key_raw_grad = (
        rotary_embed_backward(
            local_key_value[:, : KEY_VALUE_HEADS * HEAD_SIZE].reshape(
                local_rows, KEY_VALUE_HEADS, HEAD_SIZE
            ),
            cosine_table,
            sine_table,
        )
        .reshape(local_rows, KEY_VALUE_HEADS * HEAD_SIZE)
        .astype(jnp.bfloat16)
    )
    unrotated_value_gradient = local_key_value[:, KEY_VALUE_HEADS * HEAD_SIZE :].astype(
        jnp.bfloat16
    )
    query_wgrad = dot_first(first_normed, query_raw_grad)
    key_wgrad = dot_first(first_normed, key_raw_grad)
    value_wgrad = dot_first(first_normed, unrotated_value_gradient)
    normed_one_grad = (
        dot_last(query_raw_grad, query_back)
        + dot_last(key_raw_grad, key_back)
        + dot_last(unrotated_value_gradient, value_back)
    )
    input_part, gain_one_grad = norm_back(hidden, gain_first, normed_one_grad)
    input_grad = (mixed_grad + input_part).astype(jnp.bfloat16)[None]
    attn_shards = (
        lax.psum_scatter(
            gain_one_grad.astype(jnp.bfloat16), "fsdp", scatter_dimension=0, tiled=True
        ).astype(jnp.float32),
        lax.psum_scatter(
            query_wgrad.astype(jnp.bfloat16), "fsdp", scatter_dimension=0, tiled=True
        ).astype(jnp.float32),
        lax.psum_scatter(
            key_wgrad.astype(jnp.bfloat16), "fsdp", scatter_dimension=0, tiled=True
        ).astype(jnp.float32),
        lax.psum_scatter(
            value_wgrad.astype(jnp.bfloat16), "fsdp", scatter_dimension=0, tiled=True
        ).astype(jnp.float32),
        lax.psum_scatter(
            out_wgrad.astype(jnp.bfloat16), "fsdp", scatter_dimension=0, tiled=True
        ).astype(jnp.float32),
    )
    totals = (
        lax.psum(attn_shards[0].astype(jnp.bfloat16), "ctx").astype(jnp.float32),
        lax.psum(attn_shards[1].astype(jnp.bfloat16), "ctx").astype(jnp.float32),
        lax.psum(attn_shards[2].astype(jnp.bfloat16), "ctx").astype(jnp.float32),
        lax.psum(attn_shards[3].astype(jnp.bfloat16), "ctx").astype(jnp.float32),
        lax.psum(attn_shards[4].astype(jnp.bfloat16), "ctx").astype(jnp.float32),
        lax.psum(mlp_shards[0].astype(jnp.bfloat16), "ctx").astype(jnp.float32),
        lax.psum(mlp_shards[1].astype(jnp.bfloat16), "ctx").astype(jnp.float32),
        lax.psum(mlp_shards[2].astype(jnp.bfloat16), "ctx").astype(jnp.float32),
        lax.psum(mlp_shards[3].astype(jnp.bfloat16), "ctx").astype(jnp.float32),
    )
    return (
        layer_out,
        input_grad,
        totals[0],
        totals[1],
        totals[2],
        totals[3],
        totals[4],
        totals[5],
        totals[6],
        totals[7],
        totals[8],
    )


def solution(mesh):
    placed = (
        P("fsdp", "ctx", None),
        P("fsdp", "ctx"),
        P("fsdp"),
        P("fsdp", None),
        P("fsdp", None),
        P("fsdp", None),
        P("fsdp", None),
        P("fsdp"),
        P("fsdp", None),
        P("fsdp", None),
        P("fsdp", None),
        P("fsdp", "ctx", None),
    )
    return jax.shard_map(
        per_device,
        mesh=mesh,
        in_specs=placed,
        out_specs=(
            P("fsdp", "ctx", None),
            P("fsdp", "ctx", None),
            P("fsdp"),
            P("fsdp", None),
            P("fsdp", None),
            P("fsdp", None),
            P("fsdp", None),
            P("fsdp"),
            P("fsdp", None),
            P("fsdp", None),
            P("fsdp", None),
        ),
        check_vma=False,
    )
```

profile of v0, /device:TPU:0, one launch (start us, length us, event | category | flops | bytes accessed | tf_op | source)
XLA Modules:
  0.0 2368.8 jit_solution(6525127521492072982)
XLA Ops:
  9.5 13.5 all-gather.1
  23.7 39.2 %all-gather.13.cloned.1.call-done = bf16[1536,768]{1,0:T(8,128)(2,1)} async-done(((bf16[384,768]{1,0:T(8,128)(2,1)}), bf16[1536,768]{1,0:T(8,128)(2,1)}) %all-gather.13.cloned.1.call-update) | async-done | bytes 2359312 | tf_op jit(solution)/shard_map/all_gather | solution.py:109
  67.7 46.0 %all-gather.19.cloned.1.call-done = bf16[1536,768]{1,0:T(8,128)(2,1)} async-done(((bf16[384,768]{1,0:T(8,128)(2,1)}), bf16[1536,768]{1,0:T(8,128)(2,1)}) %all-gather.19.cloned.1.call-update) | async-done | bytes 2359312 | tf_op jit(solution)/shard_map/all_gather | solution.py:110
  119.9 12.3 all-gather.2
  132.3 9.4 all-gather
  141.7 61.9 %all-gather.17.cloned.1.call-done = bf16[1536,1536]{1,0:T(8,128)(2,1)} async-done(((bf16[384,1536]{1,0:T(8,128)(2,1)}), bf16[1536,1536]{1,0:T(8,128)(2,1)}) %all-gather.17.cloned.1.call-update) | async-done | bytes 4718608 | tf_op jit(solution)/shard_map/all_gather | solution.py:108
  203.6 6.6 copy.50
  210.2 4.1 fusion.46
  214.7 22.1 all-gather.15.cloned.1.call-done
  236.7 4.6 copy.51
  241.4 30.0 %all-gather.21.cloned.1.call-done = bf16[2048,768]{1,0:T(8,128)(2,1)} async-done(((bf16[256,768]{1,0:T(8,128)(2,1)}), bf16[2048,768]{1,0:T(8,128)(2,1)}) %all-gather.21.cloned.1.call-update) | async-done | bytes 3145744 | tf_op jit(solution)/shard_map/all_gather | solution.py:178
  271.4 4.7 copy.52
  276.1 76.8 %while.28 = (s32[]{:T(128)}, f32[8,2,256]{2,1,0:T(2,128)S(1)}, f32[8,2,256]{2,1,0:T(2,128)S(1)}, f32[8,2,256,96]{2,3,1,0:T(8,128)}, s32[4]{0:T(128)S(1)}, /*inde...) while((s32[]{:T(128)}, f32[8,2,256]{2,1,0:T(2,128)S(1)}, ...), condition=%wide.region_4.5_spmd.clone, body=%wide.region_1.4_spmd.clone.sunk | while | flops 829706240 | bytes 68164856 | solution.py:82
  279.9 4.6 fusion.136
  284.6 5.3 fusion.138
  290.4 4.5 fusion.140
  298.7 4.6 fusion.136
  303.4 5.3 fusion.138
  309.2 5.0 fusion.140
  318.1 4.6 fusion.136
  322.7 5.3 fusion.138
  328.6 5.0 fusion.140
  337.5 4.6 fusion.136
  342.1 5.3 fusion.138
  347.9 5.0 fusion.140
  355.4 6.9 all-gather.23.cloned.1.call-done
  362.3 4.1 multiply_reduce_fusion.3
  367.7 212.8 %all-gather.25.cloned.1.call-done = bf16[1536,4096]{1,0:T(8,128)(2,1)} async-done(((bf16[384,4096]{1,0:T(8,128)(2,1)}), bf16[1536,4096]{1,0:T(8,128)(2,1)}) %all-gather.25.cloned.1.call-update) | async-done | bytes 12582928 | tf_op jit(solution)/shard_map/all_gather | solution.py:191
  580.5 9.5 fusion.64
  590.0 208.5 %all-gather.27.cloned.1.call-done = bf16[1536,4096]{1,0:T(8,128)(2,1)} async-done(((bf16[384,4096]{1,0:T(8,128)(2,1)}), bf16[1536,4096]{1,0:T(8,128)(2,1)}) %all-gather.27.cloned.1.call-update) | async-done | bytes 12582928 | tf_op jit(solution)/shard_map/all_gather | solution.py:192
  798.5 9.7 fusion.65
  808.2 208.3 %all-gather.29.cloned.1.call-done = bf16[4096,1536]{1,0:T(8,128)(2,1)} async-done(((bf16[1024,1536]{1,0:T(8,128)(2,1)}), bf16[4096,1536]{1,0:T(8,128)(2,1)}) %all-gather.29.cloned.1.call-update) | async-done | bytes 12582928 | tf_op jit(solution)/shard_map/all_gather | solution.py:193
  1016.5 11.0 multiply_convert_fusion
  1027.6 8.4 fusion.66
  1036.0 11.2 multiply_reduce_fusion
  1055.7 3.5 broadcast_in_dim.39
  1059.2 115.1 %while.29 = (s32[]{:T(128)}, f32[8,2,256,96]{2,3,1,0:T(8,128)S(1)}, bf16[2048,1536]{0,1:T(8,128)(2,1)}, s32[4]{0:T(128)S(1)}, s32[2048]{0:T(1024)S(1)}, /*index=...) while((s32[]{:T(128)}, f32[8,2,256,96]{2,3,1,0:T(8,128)S(1)}, ...), condition=%wide.region_9.10_spmd.clone, body=%wide.region_8.9_spmd.clone.sunk | while | flops 2039480320 | bytes 111336800 | solution.py:82
  1062.6 4.5 fusion.151
  1068.6 8.6 fusion.152
  1091.3 4.5 fusion.151
  1097.3 8.6 fusion.152
  1120.0 4.5 fusion.151
  1126.0 8.6 fusion.152
  1148.8 4.5 fusion.151
  1154.8 8.6 fusion.152
  1176.3 3.7 convolution_convert_fusion.4
  1182.0 3.7 convolution_convert_fusion.3
  1186.2 48.1 %reduce-scatter.9.cloned.1.call-done = bf16[256,1536]{0,1:T(8,128)(2,1)} async-done(((bf16[2048,1536]{0,1:T(8,128)(2,1)}), bf16[256,1536]{0,1:T(8,128)(2,1)}) %reduce-scatter.9.cloned.1.call-update) | async-done | bytes 786448 | tf_op jit(solution)/shard_map/reduce_scatter | solution.py:305
  1241.5 8.0 convolution_convert_fusion.2
  1249.6 8.1 convolution_convert_fusion.1
  1258.8 8.3 convolution_convert_fusion
  1267.3 55.3 %reduce-scatter.11.cloned.1.call-done = bf16[384,1536]{1,0:T(8,128)(2,1)} async-done(((bf16[1536,1536]{1,0:T(8,128)(2,1)}), bf16[384,1536]{1,0:T(8,128)(2,1)}) %reduce-scatter.11.cloned.1.call-update) | async-done | bytes 1179664 | tf_op jit(solution)/shard_map/reduce_scatter | solution.py:345
  1322.6 88.6 %reduce-scatter.17.cloned.1.call-done = bf16[384,1536]{1,0:T(8,128)(2,1)} async-done(((bf16[1536,1536]{1,0:T(8,128)(2,1)}), bf16[384,1536]{1,0:T(8,128)(2,1)}) %reduce-scatter.17.cloned.1.call-update) | async-done | bytes 1179664 | tf_op jit(solution)/shard_map/reduce_scatter | solution.py:354
  1411.3 51.6 %reduce-scatter.13.cloned.1.call-done = bf16[384,768]{1,0:T(8,128)(2,1)} async-done(((bf16[1536,768]{1,0:T(8,128)(2,1)}), bf16[384,768]{1,0:T(8,128)(2,1)}) %reduce-scatter.13.cloned.1.call-update) | async-done | bytes 589840 | tf_op jit(solution)/shard_map/reduce_scatter | solution.py:348
  1462.9 50.4 %reduce-scatter.15.cloned.1.call-done = bf16[384,768]{1,0:T(8,128)(2,1)} async-done(((bf16[1536,768]{1,0:T(8,128)(2,1)}), bf16[384,768]{1,0:T(8,128)(2,1)}) %reduce-scatter.15.cloned.1.call-update) | async-done | bytes 589840 | tf_op jit(solution)/shard_map/reduce_scatter | solution.py:351
  1513.3 213.7 %reduce-scatter.19.cloned.1.call-done = bf16[384,4096]{1,0:T(8,128)(2,1)} async-done(((bf16[1536,4096]{1,0:T(8,128)(2,1)}), bf16[384,4096]{1,0:T(8,128)(2,1)}) %reduce-scatter.19.cloned.1.call-update) | async-done | bytes 3145744 | tf_op jit(solution)/shard_map/reduce_scatter | solution.py:224
  1727.0 215.3 %reduce-scatter.21.cloned.1.call-done = bf16[384,4096]{1,0:T(8,128)(2,1)} async-done(((bf16[1536,4096]{1,0:T(8,128)(2,1)}), bf16[384,4096]{1,0:T(8,128)(2,1)}) %reduce-scatter.21.cloned.1.call-update) | async-done | bytes 3145744 | tf_op jit(solution)/shard_map/reduce_scatter | solution.py:227
  1942.2 215.3 %reduce-scatter.23.cloned.1.call-done = bf16[1024,1536]{1,0:T(8,128)(2,1)} async-done(((bf16[4096,1536]{1,0:T(8,128)(2,1)}), bf16[1024,1536]{1,0:T(8,128)(2,1)}) %reduce-scatter.23.cloned.1.call-update) | async-done | bytes 3145744 | tf_op jit(solution)/shard_map/reduce_scatter | solution.py:230
  2159.4 3.9 fusion.67
  2163.3 7.6 fusion.23
  2175.1 11.8 all-reduce.4
  2187.1 12.7 all-reduce.2
  2203.8 139.5 %all-reduce.7.cloned.1.call-done = (bf16[384,1536]{1,0:T(8,128)(2,1)}, bf16[384,768]{1,0:T(8,128)(2,1)}, bf16[384,768]{1,0:T(8,128)(2,1)}, bf16[384,1536]{1,0:T(...) async-done(((bf16[384,1536]{1,0:T(8,128)(2,1)}, bf16[384,768]{1,0:T(8,128)(2,1)}, bf16[384,768]{1,0:T(8,128)(2,1)}, ...) | async-done | bytes 12976144 | tf_op jit(solution)/shard_map/psum | solution.py:360
  2358.2 3.6 convert_element_type.245
  (274 shorter events, 138.3 us)
Async XLA Ops:
  7.2 2.3 copy-start.40
  7.2 15.9 copy-start.36
  7.2 15.9 copy-start.3
  7.2 55.6 %all-gather.13.cloned.1.call-start = ((), (), s32[]{:S(2)}) async-start(), calls=%async_computation.8 | async-start | bytes 2949120 | tf_op jit(solution)/shard_map/all_gather | solution.py:109
  7.9 105.8 %all-gather.19.cloned.1.call-start = ((), (), s32[]{:S(2)}) async-start(), calls=%async_computation.11 | async-start | bytes 2949120 | tf_op jit(solution)/shard_map/all_gather | solution.py:110
  8.7 194.9 %all-gather.17.cloned.1.call-start = ((), (), s32[]{:S(2)}) async-start(), calls=%async_computation.10 | async-start | bytes 5898240 | tf_op jit(solution)/shard_map/all_gather | solution.py:108
  9.4 227.3 %all-gather.15.cloned.1.call-start = ((), (), s32[]{:S(2)}) async-start(), calls=%async_computation.9 | async-start | bytes 3538944 | tf_op jit(solution)/shard_map/all_gather | solution.py:177
  23.1 187.1 %copy-start.34 = (f32[1536]{0:T(1024)}, f32[1536]{0:T(1024)S(1)}, u32[]{:S(2)}) copy-start(f32[1536]{0:T(1024)S(1)} %reshape.328) | copy-start | bytes 18436
  23.4 186.8 %copy-start.37 = (f32[256]{0:T(256)}, f32[256]{0:T(256)S(1)}, u32[]{:S(2)}) copy-start(f32[256]{0:T(256)S(1)} %add_rsqrt_fusion.1) | copy-start | bytes 3076
  23.6 190.7 %copy-start.27 = (f32[256,48]{0,1:T(8,128)}, f32[256,48]{0,1:T(8,128)S(1)}, u32[]{:S(2)}) copy-start(f32[256,48]{0,1:T(8,128)S(1)} %get-tuple-element.349) | copy-start | bytes 147460
  23.7 190.7 %copy-start.29 = (f32[256,48]{0,1:T(8,128)}, f32[256,48]{0,1:T(8,128)S(1)}, u32[]{:S(2)}) copy-start(f32[256,48]{0,1:T(8,128)S(1)} %get-tuple-element.350) | copy-start | bytes 147460
  67.7 203.7 %all-gather.21.cloned.1.call-start = ((), (), s32[]{:S(2)}) async-start(), calls=%async_computation.12 | async-start | bytes 3538944 | tf_op jit(solution)/shard_map/all_gather | solution.py:178
  117.0 245.3 %all-gather.23.cloned.1.call-start = ((), (), s32[]{:S(2)}) async-start(), calls=%async_computation.13 | async-start | bytes 5898240 | tf_op jit(solution)/shard_map/all_gather | solution.py:111
  117.6 462.9 %all-gather.25.cloned.1.call-start = ((), (), s32[]{:S(2)}) async-start(), calls=%async_computation.14 | async-start | bytes 15728640 | tf_op jit(solution)/shard_map/all_gather | solution.py:191
  118.3 680.2 %all-gather.27.cloned.1.call-start = ((), (), s32[]{:S(2)}) async-start(), calls=%async_computation.15 | async-start | bytes 15728640 | tf_op jit(solution)/shard_map/all_gather | solution.py:192
  119.1 897.4 %all-gather.29.cloned.1.call-start = ((), (), s32[]{:S(2)}) async-start(), calls=%async_computation.16 | async-start | bytes 15728640 | tf_op jit(solution)/shard_map/all_gather | solution.py:193
  119.8 1114.6 %reduce-scatter.9.cloned.1.call-start = ((), (), s32[]{:S(2)}) async-start(), calls=%async_computation.17 | async-start | bytes 7077888 | tf_op jit(solution)/shard_map/reduce_scatter | solution.py:305
  284.6 5.8 copy-start
  303.4 5.9 copy-start
  322.7 5.9 copy-start
  342.1 5.8 copy-start
  367.7 430.8 %copy-start.12 = (bf16[256,1536]{1,0:T(8,128)(2,1)}, bf16[256,1536]{1,0:T(8,128)(2,1)S(1)}, u32[]{:S(2)}) copy-start(bf16[256,1536]{1,0:T(8,128)(2,1)S(1)} %multiply_convert_fusion.3) | copy-start | bytes 2359300
  1027.5 8.4 copy-start.25
  1027.5 8.4 copy-start.7
  1027.5 22.7 slice-start
  1035.9 11.2 copy-start.15
  1035.9 14.3 slice-start.1
  1077.2 4.6 copy-start.2
  1081.8 3.5 copy-start.1
  1086.7 1.4 copy-start.20
  1105.9 4.6 copy-start.2
  1110.5 3.5 copy-start.1
  1115.4 1.4 copy-start.20
  1134.6 4.6 copy-start.2
  1139.2 3.5 copy-start.1
  1144.1 1.4 copy-start.20
  1163.3 4.6 copy-start.2
  1168.0 3.5 copy-start.1
  1174.3 2.0 copy-start.4
  1174.3 2.0 copy-start.35
  1174.3 2.0 copy-start.38
  1174.3 148.3 %reduce-scatter.11.cloned.1.call-start = ((), (), s32[]{:S(2)}) async-start(), calls=%async_computation.18 | async-start | bytes 5898240 | tf_op jit(solution)/shard_map/reduce_scatter | solution.py:345
  1180.0 2.0 copy-start.10
  1180.0 231.3 %reduce-scatter.17.cloned.1.call-start = ((), (), s32[]{:S(2)}) async-start(), calls=%async_computation.21 | async-start | bytes 5898240 | tf_op jit(solution)/shard_map/reduce_scatter | solution.py:354
  1185.8 277.1 %reduce-scatter.13.cloned.1.call-start = ((), (), s32[]{:S(2)}) async-start(), calls=%async_computation.19 | async-start | bytes 2949120 | tf_op jit(solution)/shard_map/reduce_scatter | solution.py:348
  1238.0 3.5 copy-start.13
  1238.0 275.3 %reduce-scatter.15.cloned.1.call-start = ((), (), s32[]{:S(2)}) async-start(), calls=%async_computation.20 | async-start | bytes 2949120 | tf_op jit(solution)/shard_map/reduce_scatter | solution.py:351
  1241.5 485.5 %reduce-scatter.19.cloned.1.call-start = ((), (), s32[]{:S(2)}) async-start(), calls=%async_computation.22 | async-start | bytes 15728640 | tf_op jit(solution)/shard_map/reduce_scatter | solution.py:224
  1249.5 692.7 %reduce-scatter.21.cloned.1.call-start = ((), (), s32[]{:S(2)}) async-start(), calls=%async_computation.23 | async-start | bytes 15728640 | tf_op jit(solution)/shard_map/reduce_scatter | solution.py:227
  1257.7 899.8 %reduce-scatter.23.cloned.1.call-start = ((), (), s32[]{:S(2)}) async-start(), calls=%async_computation.24 | async-start | bytes 15728640 | tf_op jit(solution)/shard_map/reduce_scatter | solution.py:230
  1267.1 1076.1 %all-reduce.7.cloned.1.call-start = ((), (), s32[]{:S(2)}) async-start(), calls=%async_computation.25 | async-start | bytes 25952256 | tf_op jit(solution)/shard_map/psum | solution.py:360
  2157.5 1.9 copy-start.18
  2159.4 3.9 copy-start.8
  2159.4 3.9 copy-start.14
  2163.3 7.6 copy-start.11
  2171.0 1.7 copy-start.24
  2171.0 1.9 copy-start.26
  2172.9 2.3 copy-start.39
  2343.3 3.1 copy-start.33
  2343.3 4.2 copy-start.32
  2346.3 2.2 copy-start.31
  2348.5 2.7 copy-start.23
  2351.3 3.5 copy-start.22
  2354.7 3.5 copy-start.21
  (14 other events, 13.7 us)
Sparse Core Ops, SparseCore 0:
  9.6 53.1 all-gather.12
  64.4 49.2 all-gather.18
  115.3 88.2 all-gather.16
  205.9 30.7 all-gather.14
  239.0 32.3 all-gather.20
  272.8 89.4 all-gather.22
  363.8 216.6 all-gather.24
  582.1 216.3 all-gather.26
  800.1 216.3 all-gather.28
  1174.4 59.9 reduce-scatter.8
  1237.4 85.2 reduce-scatter.10
  1325.5 85.7 reduce-scatter.16
  1414.3 48.5 reduce-scatter.12
  1465.7 47.5 reduce-scatter.14
  1515.6 211.3 reduce-scatter.18
  1729.3 212.8 reduce-scatter.20
  1944.5 212.8 reduce-scatter.22
  2163.0 180.1 all-reduce.6
where the time goes:
time: 2370 us
  waiting for transfers between devices  1920 us (81%)
  matrix products  239 us (10%)
  local copies, waits for them, and re-layouts  71.9 us (3%)
  blocking collectives  59.7 us (3%)
  other arithmetic  56.8 us (2%)
    reduce_scatter x1, waiting for transfers between devices, per_device(): lax.psum_scatter(up_wgrad.astype(jnp.bfloat16), 'fsdp', scatter_dimension...  215 us
    reduce_scatter x1, waiting for transfers between devices, per_device(): lax.psum_scatter(down_grad.astype(jnp.bfloat16), 'fsdp', scatter_dimensio...  215 us
    reduce_scatter x1, waiting for transfers between devices, per_device(): lax.psum_scatter(gate_wgrad.astype(jnp.bfloat16), 'fsdp', scatter_dimensi...  214 us
    all_gather x1, waiting for transfers between devices, per_device(): lax.all_gather(w_gate, 'fsdp', axis=0, tiled=True)  213 us
    all_gather x1, waiting for transfers between devices, per_device(): lax.all_gather(w_up, 'fsdp', axis=0, tiled=True)  208 us
    all_gather x1, waiting for transfers between devices, per_device(): lax.all_gather(w_down, 'fsdp', axis=0, tiled=True)  208 us
    psum x1, waiting for transfers between devices, per_device(): lax.psum(attn_shards[1].astype(jnp.bfloat16), 'ctx').astype(jnp.float32)  139 us
    reduce_scatter x1, waiting for transfers between devices, per_device(): lax.psum_scatter(out_wgrad.astype(jnp.bfloat16), 'fsdp', scatter_dimensio...  88.6 us
  transfers between devices with their start and end apart: 18, of which 18 were waited for; matrix products, arithmetic and copies ran while one was open for 8% of the time, Pallas kernels for 0%

commit v1 on v0

--- a/solution.py
+++ b/solution.py
@@ -1,8 +1,11 @@
+import functools
 import math
 
 import jax
 import jax.numpy as jnp
 from jax import lax
+from jax.experimental import pallas as pl
+from jax.experimental.pallas import tpu as pltpu
 from jax.sharding import PartitionSpec as P
 
 QUERY_HEADS = 16
@@ -381,6 +384,730 @@
     )
 
 
+MESH = pl.DeviceIdType.MESH
+ANY = pl.ANY
+VMEM = pltpu.VMEM
+DMA = pltpu.SemaphoreType.DMA
+LANES = 128
+BLOCK = 128
+F32 = jnp.float32
+BF16 = jnp.bfloat16
+VMEM_BYTES = 60 * 2**20
+
+
+def flip(c, k):
+    out = c
+    for b in (1, 2, 4):
+        if k & b:
+            out = out + b - 2 * b * ((c // b) % 2)
+    return out
+
+
+def remote(src, dst, send, recv, **to):
+    return pltpu.make_async_remote_copy(
+        src_ref=src, dst_ref=dst, send_sem=send, recv_sem=recv, device_id=to, device_id_type=MESH
+    )
+
+
+def greet(peers):
+    barrier = pltpu.get_barrier_semaphore()
+    for peer in peers:
+        pl.semaphore_signal(barrier, inc=1, device_id=peer, device_id_type=MESH)
+    pl.semaphore_wait(barrier, len(peers))
+
+
+class Gather:
+    def __init__(self, c, own, buf, send, recv):
+        self.c, self.own, self.buf, self.send, self.recv = c, own, buf, send, recv
+        self.half = buf.shape[1] // 2
+        self.pending = []
+
+    def rows(self, h):
+        return pl.ds(h * self.half, self.half)
+
+    def start(self, channel, who, to, h, own=False):
+        source = flip(self.c, who)
+        there = self.buf.at[source, self.rows(h)]
+        d = remote(
+            self.own.at[self.rows(h)] if own else there,
+            there,
+            self.send.at[channel, h],
+            self.recv.at[channel, h],
+            ctx=flip(self.c, to),
+        )
+        d.start()
+        self.pending.append(d)
+
+    def arrived(self, channel, who, frm, h):
+        ref = self.buf.at[flip(self.c, who), self.rows(h)]
+        remote(
+            ref, ref, self.send.at[channel, h], self.recv.at[channel, h], ctx=flip(self.c, frm)
+        ).wait_recv()
+
+    def begin(self):
+        self.start(1, 0, 2, 0, own=True)
+        self.start(2, 0, 4, 1, own=True)
+        self.start(1, 0, 2, 1, own=True)
+        self.start(2, 0, 4, 0, own=True)
+        self.start(0, 0, 1, 0, own=True)
+        self.start(0, 0, 1, 1, own=True)
+
+    def finish(self):
+        self.arrived(1, 2, 2, 0)
+        self.start(6, 2, 4, 0)
+        self.start(3, 2, 1, 0)
+        self.arrived(2, 4, 4, 1)
+        self.start(7, 4, 2, 1)
+        self.start(4, 4, 1, 1)
+        self.arrived(1, 2, 2, 1)
+        self.start(3, 2, 1, 1)
+        self.arrived(2, 4, 4, 0)
+        self.start(4, 4, 1, 0)
+        self.arrived(6, 6, 4, 0)
+        self.start(5, 6, 1, 0)
+        self.arrived(7, 6, 2, 1)
+        self.start(5, 6, 1, 1)
+        for channel, who in ((0, 1), (3, 3), (4, 5), (5, 7)):
+            for h in (0, 1):
+                self.arrived(channel, who, 1, h)
+        for d in self.pending:
+            d.wait_send()
+
+
+def params(cid):
+    return pltpu.CompilerParams(
+        collective_id=cid, has_side_effects=True, vmem_limit_bytes=VMEM_BYTES
+    )
+
+
+def plane_gather(x, cid):
+    rows, width = x.shape
+
+    def kernel(x_ref, o_ref, send, recv, local):
+        c = lax.axis_index("ctx")
+        greet([{"ctx": flip(c, k)} for k in (1, 2, 4)])
+        here = pltpu.make_async_copy(x_ref, o_ref.at[c], local)
+        here.start()
+        g = Gather(c, x_ref, o_ref, send, recv)
+        g.begin()
+        g.finish()
+        here.wait()
+
+    return pl.pallas_call(
+        kernel,
+        out_shape=jax.ShapeDtypeStruct((8, rows, width), x.dtype),
+        in_specs=[pl.BlockSpec(memory_space=ANY)],
+        out_specs=pl.BlockSpec(memory_space=ANY),
+        scratch_shapes=[DMA((8, 2)), DMA((8, 2)), DMA],
+        compiler_params=params(cid),
+        cost_estimate=pl.CostEstimate(flops=0, bytes_accessed=16 * rows * width * 20, transcendentals=0),
+        name="plane_gather",
+    )(x)
+
+
+def plane_exchange(x, cid):
+    def kernel(x_ref, o_ref, send, recv, local):
+        c = lax.axis_index("ctx")
+        greet([{"ctx": flip(c, k)} for k in range(1, 8)])
+        here = pltpu.make_async_copy(x_ref.at[c], o_ref.at[c], local)
+        here.start()
+        sent = []
+        for k in (6, 7, 2, 4, 3, 5, 1):
+            d = remote(
+                x_ref.at[flip(c, k)], o_ref.at[c], send.at[k], recv.at[k], ctx=flip(c, k)
+            )
+            d.start()
+            sent.append(d)
+        here.wait()
+        for k in (6, 7, 2, 4, 3, 5, 1):
+            ref = o_ref.at[flip(c, k)]
+            remote(ref, ref, send.at[k], recv.at[k], ctx=flip(c, k)).wait_recv()
+        for d in sent:
+            d.wait_send()
+
+    return pl.pallas_call(
+        kernel,
+        out_shape=jax.ShapeDtypeStruct(x.shape, x.dtype),
+        in_specs=[pl.BlockSpec(memory_space=ANY)],
+        out_specs=pl.BlockSpec(memory_space=ANY),
+        scratch_shapes=[DMA((8,)), DMA((8,)), DMA],
+        compiler_params=params(cid),
+        name="plane_exchange",
+    )(x)
+
+
+def scatter_kernel(p_ref, o_ref, first, total, last, diagonal, s1, v1, s2, v2):
+    c = lax.axis_index("ctx")
+    greet([{"ctx": flip(c, k)} for k in (1, 2, 4)])
+    rows = p_ref.shape[1]
+    piece = rows // 2
+    pending = []
+
+    def go(d):
+        d.start()
+        pending.append(d)
+
+    def sl(q):
+        return pl.ds(q * piece, piece)
+
+    for j, k in enumerate((6, 2, 4, 0)):
+        for q in (0, 1):
+            go(
+                remote(
+                    p_ref.at[flip(c, 1 ^ k), sl(q)],
+                    first.at[j, sl(q)],
+                    s1.at[j, q],
+                    v1.at[j, q],
+                    ctx=flip(c, 1),
+                )
+            )
+
+    def paired(j, q):
+        ref = first.at[j, sl(q)]
+        remote(ref, ref, s1.at[j, q], v1.at[j, q], ctx=flip(c, 1)).wait_recv()
+
+    def chip(j, k, q):
+        return p_ref[flip(c, k), sl(q)].astype(F32) + first[j, sl(q)].astype(F32)
+
+    def came(channel, ref, q, frm):
+        remote(ref, ref, s2.at[channel, q], v2.at[channel, q], ctx=flip(c, frm)).wait_recv()
+
+    for q, to in ((0, 2), (1, 4)):
+        paired(0, q)
+        total[0, sl(q)] = chip(0, 6, q).astype(BF16)
+        go(
+            remote(
+                total.at[0, sl(q)], diagonal.at[sl(q)], s2.at[2, q], v2.at[2, q], ctx=flip(c, to)
+            )
+        )
+
+    def final(j, k, q, merged):
+        v = chip(j, k, q)
+        if merged:
+            v = v + diagonal[sl(q)].astype(F32)
+        total[j, sl(q)] = v.astype(BF16)
+        go(
+            remote(
+                total.at[j, sl(q)],
+                last.at[j - 1, sl(q)],
+                s2.at[j - 1, q],
+                v2.at[j - 1, q],
+                ctx=flip(c, k),
+            )
+        )
+
+    paired(1, 0)
+    final(1, 2, 0, False)
+    paired(2, 1)
+    final(2, 4, 1, False)
+    paired(2, 0)
+    came(2, diagonal.at[sl(0)], 0, 2)
+    final(2, 4, 0, True)
+    paired(1, 1)
+    came(2, diagonal.at[sl(1)], 1, 4)
+    final(1, 2, 1, True)
+    for q in (0, 1):
+        paired(3, q)
+    for q in (0, 1):
+        came(0, last.at[0, sl(q)], q, 2)
+        came(1, last.at[1, sl(q)], q, 4)
+        o_ref[sl(q)] = chip(3, 0, q) + (last[0, sl(q)].astype(F32) + last[1, sl(q)].astype(F32))
+    for d in pending:
+        d.wait_send()
+
+
+def plane_scatter(p, cid):
+    rows, width = p.shape[1:]
+    return pl.pallas_call(
+        scatter_kernel,
+        out_shape=jax.ShapeDtypeStruct((rows, width), F32),
+        in_specs=[pl.BlockSpec(memory_space=VMEM)],
+        out_specs=pl.BlockSpec(memory_space=VMEM),
+        scratch_shapes=[
+            VMEM((4, rows, width), BF16),
+            VMEM((3, rows, width), BF16),
+            VMEM((2, rows, width), BF16),
+            VMEM((rows, width), BF16),
+            DMA((4, 2)),
+            DMA((4, 2)),
+            DMA((3, 2)),
+            DMA((3, 2)),
+        ],
+        compiler_params=params(cid),
+        name="plane_scatter",
+    )(p)
+
+
+def first_kernel(x_ref, gain_ref, info_ref, all_ref, gains_ref, infos_ref, normed, *sems):
+    gsend, grecv, isend, irecv, send, recv, local = sems
+    c = lax.axis_index("ctx")
+    z = lax.axis_index("fsdp")
+    depth = gains_ref.shape[0]
+    others = [lax.rem(z + k, depth) for k in range(1, depth)]
+    greet([{"ctx": flip(c, k)} for k in range(1, 8)] + [{"fsdp": o} for o in others])
+    sent = []
+    for k, o in enumerate(others):
+        d = remote(gain_ref, gains_ref.at[z], gsend.at[k], grecv.at[k], fsdp=o)
+        d.start()
+        sent.append(d)
+    for k in range(1, 8):
+        d = remote(info_ref, infos_ref.at[c], isend.at[k], irecv.at[k], ctx=flip(c, k))
+        d.start()
+        sent.append(d)
+    gains_ref[z] = gain_ref[...]
+    infos_ref[c] = info_ref[...]
+    x = x_ref[...].astype(F32)
+    factor = lax.rsqrt(jnp.mean(x * x, -1, keepdims=True) + EPS)
+    for k in range(depth - 1):
+        ref = gains_ref.at[lax.rem(z + depth - 1 - k, depth)]
+        remote(ref, ref, gsend.at[k], grecv.at[k], fsdp=others[k]).wait_recv()
+    gain = jnp.concatenate([gains_ref[k, 0:1, :] for k in range(depth)], 1)
+    normed[...] = (x * factor * gain).astype(BF16)
+    here = pltpu.make_async_copy(normed, all_ref.at[c], local)
+    here.start()
+    g = Gather(c, normed, all_ref, send, recv)
+    g.begin()
+    g.finish()
+    here.wait()
+    for k in range(1, 8):
+        ref = infos_ref.at[flip(c, k)]
+        remote(ref, ref, isend.at[k], irecv.at[k], ctx=flip(c, k)).wait_recv()
+    for d in sent:
+        d.wait_send()
+
+
+def first_gather(x, gains, info, depth, cid):
+    rows, width = x.shape
+    vm = pl.BlockSpec(memory_space=VMEM)
+    return pl.pallas_call(
+        first_kernel,
+        out_shape=(
+            jax.ShapeDtypeStruct((8, rows, width), BF16),
+            jax.ShapeDtypeStruct((depth,) + gains.shape, F32),
+            jax.ShapeDtypeStruct((8,) + info.shape, jnp.int32),
+        ),
+        in_specs=[vm, vm, vm],
+        out_specs=(pl.BlockSpec(memory_space=ANY), vm, vm),
+        scratch_shapes=[
+            VMEM((rows, width), BF16),
+            DMA((depth,)),
+            DMA((depth,)),
+            DMA((8,)),
+            DMA((8,)),
+            DMA((8, 2)),
+            DMA((8, 2)),
+            DMA,
+        ],
+        compiler_params=params(cid),
+        name="first_gather",
+    )(x, gains, info)
+
+
+def angles(base_cos, base_sin, step_cos, step_sin):
+    return (
+        base_cos * step_cos - base_sin * step_sin,
+        base_sin * step_cos + base_cos * step_sin,
+    )
+
+
+def turn(u, cosine, sine, sign):
+    lane = lax.broadcasted_iota(jnp.int32, u.shape, 1)
+    signed = jnp.where(lane < LANES // 2, -sign, sign) * sine
+    return u * cosine + pltpu.roll(u, LANES // 2, 1) * signed
+
+
+def qkv_kernel(x_ref, w_ref, bc_ref, bs_ref, sc_ref, ss_ref, q_ref, k_ref, v_ref):
+    i = pl.program_id(0)
+    raw = jnp.dot(x_ref[...], w_ref[...], preferred_element_type=F32)
+    blocks = x_ref.shape[0] // BLOCK
+    for b in range(blocks):
+        row = pl.ds(i * blocks + b, 1)
+        cosine, sine = angles(bc_ref[row, :], bs_ref[row, :], sc_ref[...], ss_ref[...])
+        rows = slice(b * BLOCK, (b + 1) * BLOCK)
+        for h in (0, 1):
+            cols = slice(h * LANES, (h + 1) * LANES)
+            q_ref[rows, cols] = turn(raw[rows, cols], cosine, sine, 1.0).astype(BF16)
+        k_ref[rows, :] = turn(raw[rows, 2 * LANES : 3 * LANES], cosine, sine, 1.0).astype(BF16)
+        v_ref[rows, :] = raw[rows, 3 * LANES :].astype(BF16)
+
+
+def project(x, w, tables_in):
+    tokens, width = x.shape
+    step = 512
+    whole = lambda a: pl.BlockSpec(a.shape, lambda i: (0, 0))
+    return pl.pallas_call(
+        qkv_kernel,
+        grid=(tokens // step,),
+        out_shape=(
+            jax.ShapeDtypeStruct((tokens, 2 * LANES), BF16),
+            jax.ShapeDtypeStruct((tokens, LANES), BF16),
+            jax.ShapeDtypeStruct((tokens, LANES), BF16),
+        ),
+        in_specs=[pl.BlockSpec((step, width), lambda i: (i, 0)), whole(w)] + [whole(t) for t in tables_in],
+        out_specs=(
+            pl.BlockSpec((step, 2 * LANES), lambda i: (i, 0)),
+            pl.BlockSpec((step, LANES), lambda i: (i, 0)),
+            pl.BlockSpec((step, LANES), lambda i: (i, 0)),
+        ),
+        compiler_params=pltpu.CompilerParams(vmem_limit_bytes=VMEM_BYTES),
+        name="project",
+    )(x, w, *tables_in)
+
+
+CHUNK = 512
+
+
+def both_heads(ref, start):
+    rows = pl.ds(pl.multiple_of(start, BLOCK), BLOCK)
+    return jnp.concatenate([ref[rows, :LANES], ref[rows, LANES:]], 0)
+
+
+def order_rows(order_ref, tokens, pairs):
+    for j in range(tokens // BLOCK):
+        rows = pl.ds(pl.multiple_of(order_ref[j] * BLOCK, BLOCK), BLOCK)
+        for source, target in pairs:
+            target[j * BLOCK : (j + 1) * BLOCK, :] = source[rows, :]
+
+
+def contract(a, b, dims):
+    return lax.dot_general(a, b, ((dims[0], dims[1]), ((), ())), preferred_element_type=F32)
+
+
+def attend_kernel(order_ref, q_ref, k_ref, v_ref, o_ref, low_ref, lse_ref, keys, values):
+    j = pl.program_id(0)
+    tokens = q_ref.shape[0]
+    factor = HEAD_SIZE ** (-0.5) * math.log2(math.e)
+
+    @pl.when(j == 0)
+    def _():
+        order_rows(order_ref, tokens, ((k_ref, keys), (v_ref, values)))
+
+    start = order_ref[j] * BLOCK
+    q = both_heads(q_ref, start)
+    last = j // (CHUNK // BLOCK)
+
+    def step(t, carry, masked):
+        top, denom, acc = carry
+        rows = pl.ds(pl.multiple_of(t * CHUNK, CHUNK), CHUNK)
+        s = contract(keys[rows, :], q, ((1,), (1,)))
+        if masked:
+            key = t * CHUNK + lax.broadcasted_iota(jnp.int32, s.shape, 0)
+            query = j * BLOCK + lax.broadcasted_iota(jnp.int32, s.shape, 1) % BLOCK
+            s = jnp.where(key <= query, s, -jnp.inf)
+        new_top = jnp.maximum(top, jnp.max(s, 0, keepdims=True))
+        p = jnp.exp2((s - new_top) * factor)
+        shrink = jnp.exp2((top - new_top) * factor)
+        denom = denom * shrink + jnp.sum(p, 0, keepdims=True)
+        acc = acc * shrink + contract(values[rows, :], p.astype(BF16), ((0,), (0,)))
+        return new_top, denom, acc
+
+    carry = (
+        jnp.full((1, 2 * BLOCK), -1e30, F32),
+        jnp.zeros((1, 2 * BLOCK), F32),
+        jnp.zeros((LANES, 2 * BLOCK), F32),
+    )
+    carry = lax.fori_loop(0, last, lambda t, state: step(t, state, False), carry)
+    top, denom, acc = step(last, carry, True)
+    out = (acc / denom).T
+    lse_ref[pl.ds(j, 1), :, :] = (top * factor + jnp.log2(denom)).reshape(1, 1, 2 * BLOCK)
+    out = jnp.concatenate([out[:BLOCK], out[BLOCK:]], 1)
+    rows = pl.ds(pl.multiple_of(start, BLOCK), BLOCK)
+    o_ref[rows, :] = out
+    low_ref[rows, :] = out.astype(BF16)
+
+
+def attend(order, q, k, v):
+    tokens = q.shape[0]
+    blocks = tokens // BLOCK
+    whole = lambda *shape: pl.BlockSpec(shape, lambda j, *_: (0,) * len(shape))
+    return pl.pallas_call(
+        attend_kernel,
+        grid_spec=pltpu.PrefetchScalarGridSpec(
+            num_scalar_prefetch=1,
+            grid=(blocks,),
+            in_specs=[whole(*q.shape), whole(*k.shape), whole(*v.shape)],
+            out_specs=(whole(tokens, 2 * LANES), whole(tokens, 2 * LANES), whole(blocks, 1, 2 * BLOCK)),
+            scratch_shapes=[VMEM(k.shape, BF16), VMEM(v.shape, BF16)],
+        ),
+        out_shape=(
+            jax.ShapeDtypeStruct((tokens, 2 * LANES), F32),
+            jax.ShapeDtypeStruct((tokens, 2 * LANES), BF16),
+            jax.ShapeDtypeStruct((blocks, 1, 2 * BLOCK), F32),
+        ),
+        compiler_params=pltpu.CompilerParams(vmem_limit_bytes=VMEM_BYTES),
+        name="attend",
+    )(order, q, k, v)
+
+
+def attend_back_kernel(
+    order_ref, q_ref, k_ref, v_ref, o_ref, do_ref, lse_ref, bc_ref, bs_ref, sc_ref, ss_ref, d_ref, keys, values, dk, dv
+):
+    j = pl.program_id(0)
+    tokens = q_ref.shape[0]
+    scale = HEAD_SIZE ** (-0.5)
+    factor = scale * math.log2(math.e)
+
+    @pl.when(j == 0)
+    def _():
+        order_rows(order_ref, tokens, ((k_ref, keys), (v_ref, values)))
+        dk[...] = jnp.zeros_like(dk)
+        dv[...] = jnp.zeros_like(dv)
+
+    block = order_ref[j]
+    start = block * BLOCK
+    q = both_heads(q_ref, start)
+    do = both_heads(do_ref, start)
+    delta = jnp.sum((both_heads(o_ref, start) * do.astype(F32)).T, 0, keepdims=True)
+    lse = lse_ref[j]
+    last = j // (CHUNK // BLOCK)
+
+    def step(t, dq, masked):
+        rows = pl.ds(pl.multiple_of(t * CHUNK, CHUNK), CHUNK)
+        key_rows = keys[rows, :]
+        s = contract(key_rows, q, ((1,), (1,)))
+        if masked:
+            key = t * CHUNK + lax.broadcasted_iota(jnp.int32, s.shape, 0)
+            query = j * BLOCK + lax.broadcasted_iota(jnp.int32, s.shape, 1) % BLOCK
+            s = jnp.where(key <= query, s, -jnp.inf)
+        p = jnp.exp2(s * factor - lse)
+        dp = contract(values[rows, :], do, ((1,), (1,)))
+        ds = (p * (dp - delta)).astype(BF16)
+        dv[rows, :] += jnp.dot(p.astype(BF16), do, preferred_element_type=F32)
+        dk[rows, :] += jnp.dot(ds, q, preferred_element_type=F32)
+        return dq + contract(key_rows, ds, ((0,), (0,)))
+
+    dq = jnp.zeros((LANES, 2 * BLOCK), F32)
+    dq = lax.fori_loop(0, last, lambda t, state: step(t, state, False), dq)
+    dq = step(last, dq, True).T * scale
+
+    def table(at):
+        row = pl.ds(at, 1)
+        return angles(bc_ref[row, :], bs_ref[row, :], sc_ref[...], ss_ref[...])
+
+    cosine, sine = table(block)
+    rows = pl.ds(pl.multiple_of(start, BLOCK), BLOCK)
+    for h in (0, 1):
+        part = dq[h * BLOCK : (h + 1) * BLOCK]
+        d_ref[rows, h * LANES : (h + 1) * LANES] = turn(part, cosine, sine, -1.0).astype(BF16)
+
+    @pl.when(j == tokens // BLOCK - 1)
+    def _():
+        def put(b, unused):
+            at = order_ref[b]
+            cosine, sine = table(at)
+            source = pl.ds(pl.multiple_of(b * BLOCK, BLOCK), BLOCK)
+            rows = pl.ds(pl.multiple_of(at * BLOCK, BLOCK), BLOCK)
+            d_ref[rows, 2 * LANES : 3 * LANES] = turn(dk[source, :] * scale, cosine, sine, -1.0).astype(BF16)
+            d_ref[rows, 3 * LANES :] = dv[source, :].astype(BF16)
+            return unused
+
+        lax.fori_loop(0, tokens // BLOCK, put, 0)
+
+
+def attend_back(order, q, k, v, o, do, lse, tables_in):
+    tokens = q.shape[0]
+    blocks = tokens // BLOCK
+    whole = lambda a: pl.BlockSpec(a.shape, lambda j, *_: (0,) * a.ndim)
+    arrays = (q, k, v, o, do, lse) + tuple(tables_in)
+    return pl.pallas_call(
+        attend_back_kernel,
+        grid_spec=pltpu.PrefetchScalarGridSpec(
+            num_scalar_prefetch=1,
+            grid=(blocks,),
+            in_specs=[whole(a) for a in arrays],
+            out_specs=pl.BlockSpec((tokens, 4 * LANES), lambda j, *_: (0, 0)),
+            scratch_shapes=[VMEM(k.shape, BF16), VMEM(v.shape, BF16), VMEM(k.shape, F32), VMEM(v.shape, F32)],
+        ),
+        out_shape=jax.ShapeDtypeStruct((tokens, 4 * LANES), BF16),
+        compiler_params=pltpu.CompilerParams(vmem_limit_bytes=VMEM_BYTES),
+        name="attend_back",
+    )(order, *arrays)
+
+
+def in_plane(
+    depth,
+    hidden_in,
+    positions,
+    attn_gain,
+    w_query,
+    key_projection,
+    value_projection,
+    w_out,
+    mlp_gain,
+    w_gate,
+    w_up,
+    w_down,
+    out_grad,
+):
+    c = lax.axis_index("ctx")
+    plane = 8
+    rows, width = hidden_in.shape[1:]
+    tokens = plane * rows
+    shard = width // depth
+    half = HEAD_SIZE // 2
+    columns = w_gate.shape[1]
+    mine = columns // plane
+    strip = mine // depth
+    deep = w_down.shape[0]
+
+    def share(a, axis):
+        return lax.dynamic_index_in_dim(a, c, axis, keepdims=False)
+
+    def halves(a, heads):
+        a = share(a.reshape(shard, plane, heads, 2, half), 1)
+        a = jnp.pad(a, ((0, 0), (0, 0), (0, 0), (0, LANES // 2 - half)))
+        return a.reshape(shard, heads * LANES)
+
+    value_part = jnp.pad(share(value_projection.reshape(shard, plane, HEAD_SIZE), 1), ((0, 0), (0, LANES - HEAD_SIZE)))
+    qkv_part = jnp.concatenate([halves(w_query, 2), halves(key_projection, 1), value_part], 1)
+
+    def cut(a):
+        return share(a.reshape(shard, depth, plane, strip), 2).reshape(shard, mine)
+
+    out_part = share(w_out.reshape(plane, shard // plane, width), 0)
+    down_part = share(w_down.reshape(plane, deep // plane, width), 0)
+
+    def over_depth(a):
+        return lax.all_gather(a, "fsdp", axis=0, tiled=True)
+
+    qkv_w = over_depth(qkv_part)
+    out_slices = over_depth(out_part)
+    gate_w = over_depth(cut(w_gate))
+    up_w = over_depth(cut(w_up))
+    down_w = over_depth(down_part)
+
+    position = positions[0]
+    lane = lax.broadcasted_iota(jnp.int32, (8, LANES), 1)
+    info = jnp.where(lane < LANES // 2, position[0], position[BLOCK])
+    gains = jnp.concatenate(
+        [
+            jnp.broadcast_to(attn_gain.astype(F32)[None], (4, shard)),
+            jnp.broadcast_to(mlp_gain.astype(F32)[None], (4, shard)),
+        ],
+        0,
+    )
+    hidden_low = hidden_in[0]
+    normed_all, gains_all, infos = first_gather(hidden_low, gains, info, depth, 0)
+    gain_one = gains_all[:, 0].reshape(width)
+    gain_two = gains_all[:, 4].reshape(width)
+    starts = infos[:, 0].reshape(plane, 2, LANES // 2)[:, :, 0].reshape(2 * plane)
+    ranks = (starts - jnp.min(starts)) // BLOCK
+    blocks = 2 * plane
+    order = jnp.sum(
+        jnp.where(ranks[None, :] == jnp.arange(blocks)[:, None], jnp.arange(blocks)[None, :], 0), 1
+    ).astype(jnp.int32)
+
+    freq = THETA ** (-(jnp.arange(half, dtype=F32) * 2.0 / HEAD_SIZE))
+    pad = jnp.zeros((LANES // 2 - half,), F32)
+    freq = jnp.concatenate([freq, pad, freq, pad])
+    base = starts.astype(F32)[:, None] * freq[None]
+    inner = jnp.arange(BLOCK, dtype=F32)[:, None] * freq[None]
+    tables_in = (jnp.cos(base), jnp.sin(base), jnp.cos(inner), jnp.sin(inner))
+
+    normed_all = normed_all.reshape(tokens, width)
+    q, k, v = project(normed_all, qkv_w, tables_in)
+    attended, attended_low, lse = attend(order, q, k, v)
+
+    out_all = plane_gather(out_slices.reshape(depth * (shard // plane), width), 1)
+    out_w = (
+        out_all.reshape(plane, depth, shard // plane, width).transpose(1, 0, 2, 3).reshape(width, width)
+    )
+    mixed_heads = plane_exchange(attended_low.reshape(plane, rows, 2 * LANES), 2)
+    attended_tok = (
+        mixed_heads.reshape(plane, rows, 2, LANES)[..., :HEAD_SIZE].transpose(1, 0, 2, 3).reshape(rows, width)
+    )
+    hidden = hidden_low.astype(F32)
+    mixed = hidden + jnp.dot(attended_tok, out_w, preferred_element_type=F32)
+    normed_two = norm_forward(mixed, gain_two).astype(BF16)
+    two_all = plane_gather(normed_two, 3).reshape(tokens, width)
+    grad_low = out_grad[0]
+    grad_all = plane_gather(grad_low, 4).reshape(tokens, width)
+
+    gate = jnp.dot(two_all, gate_w, preferred_element_type=F32)
+    up = jnp.dot(two_all, up_w, preferred_element_type=F32)
+    sigma = jax.nn.sigmoid(gate)
+    active = (gate * sigma * up).astype(BF16)
+    down_sum = jnp.dot(active, down_w, preferred_element_type=F32).astype(BF16)
+    result = mixed + plane_scatter(down_sum.reshape(plane, rows, width), 5)
+    layer_out = result.astype(BF16)[None]
+
+    down_grad = dot_first(active, grad_all)
+    active_grad = dot_last(grad_all, down_w)
+    gate_grad = (active_grad * up * sigma * (1.0 + gate * (1.0 - sigma))).astype(BF16)
+    up_grad = (active_grad * gate * sigma).astype(BF16)
+    gate_wgrad = dot_first(two_all, gate_grad)
+    up_wgrad = dot_first(two_all, up_grad)
+    two_grad_sum = (dot_last(gate_grad, gate_w) + dot_last(up_grad, up_w)).astype(BF16)
+    two_grad = plane_scatter(two_grad_sum.reshape(plane, rows, width), 6)
+    mixed_part, gain_two_grad = norm_back(mixed, gain_two, two_grad)
+    mixed_grad = grad_low.astype(F32) + mixed_part
+    branch_grad = mixed_grad.astype(BF16)
+
+    def scatter_depth(a):
+        return lax.psum_scatter(a.astype(BF16), "fsdp", scatter_dimension=0, tiled=True)
+
+    gate_shard = scatter_depth(gate_wgrad)
+    up_shard = scatter_depth(up_wgrad)
+    down_shard = scatter_depth(down_grad)
+
+    attended_grad = dot_last(branch_grad, out_w).astype(BF16)
+    out_wgrad = dot_first(attended_tok, branch_grad).astype(BF16)
+    spread = jnp.pad(
+        attended_grad.reshape(rows, plane, 2, HEAD_SIZE), ((0, 0), (0, 0), (0, 0), (0, LANES - HEAD_SIZE))
+    )
+    spread = spread.transpose(1, 0, 2, 3).reshape(plane, rows, 2 * LANES)
+    do = plane_exchange(spread, 7).reshape(tokens, 2 * LANES)
+    qkv_grad = attend_back(order, q, k, v, attended, do, lse, tables_in)
+    one_grad_sum = dot_last(qkv_grad, qkv_w).astype(BF16)
+    qkv_wgrad = dot_first(normed_all, qkv_grad).astype(BF16)
+    qkv_shard = scatter_depth(qkv_wgrad)
+    one_grad = plane_scatter(one_grad_sum.reshape(plane, rows, width), 8)
+    input_part, gain_one_grad = norm_back(hidden, gain_one, one_grad)
+    input_grad = (mixed_grad + input_part).astype(BF16)[None]
+
+    out_rows = out_wgrad.reshape(depth, plane, shard // plane, width).transpose(1, 0, 2, 3)
+    out_sum = plane_scatter(out_rows.reshape(plane, shard // plane * depth, width), 9)
+    out_shard = scatter_depth(out_sum)
+
+    joined = jnp.concatenate([gate_shard, up_shard, down_shard.reshape(-1, mine)], 0)
+    joined = plane_gather(joined, 10).astype(F32)
+    def columns_of(a):
+        return a.reshape(plane, shard, depth, strip).transpose(1, 2, 0, 3).reshape(shard, columns)
+
+    gate_total = columns_of(joined[:, :shard])
+    up_total = columns_of(joined[:, shard : 2 * shard])
+    down_total = joined[:, 2 * shard :].reshape(deep, width)
+
+    tail = jnp.concatenate([qkv_shard, out_shard.reshape(-1, 4 * LANES)], 0)
+    tail = plane_gather(tail, 11).astype(F32)
+    out_total = tail[:, shard:].reshape(shard, width)
+    heads = tail[:, :shard].reshape(plane, shard, 4, LANES)
+
+    def unhalve(a, n):
+        a = a.reshape(plane, shard, n, 2, LANES // 2)[..., :half]
+        return a.transpose(1, 0, 2, 3, 4).reshape(shard, plane * n * HEAD_SIZE)
+
+    query_total = unhalve(heads[:, :, :2], 2)
+    key_total = unhalve(heads[:, :, 2:3], 1)
+    value_total = heads[:, :, 3, :HEAD_SIZE].transpose(1, 0, 2).reshape(shard, plane * HEAD_SIZE)
+
+    gain_sums = lax.psum(jnp.stack([gain_one_grad, gain_two_grad]), ("ctx", "fsdp"))
+    gain_sums = lax.dynamic_slice_in_dim(gain_sums, lax.axis_index("fsdp") * shard, shard, 1)
+    return (
+        layer_out,
+        input_grad,
+        gain_sums[0],
+        query_total,
+        key_total,
+        value_total,
+        out_total,
+        gain_sums[1],
+        gate_total,
+        up_total,
+        down_total,
+    )
+
+
 def solution(mesh):
     placed = (
         P("fsdp", "ctx", None),
@@ -396,8 +1123,11 @@
         P("fsdp", None),
         P("fsdp", "ctx", None),
     )
+    body = per_device
+    if mesh.shape["ctx"] == KEY_VALUE_HEADS:
+        body = functools.partial(in_plane, mesh.shape["fsdp"])
     return jax.shard_map(
-        per_device,
+        body,
         mesh=mesh,
         in_specs=placed,
         out_specs=(

time: 2370 us -> 795 us (0.34)
  waiting for transfers between devices: 1920 us -> 0.24 us
  Pallas kernels: 0 us -> 422 us
  matrix products: 239 us -> 97.4 us
  local copies, waits for them, and re-layouts: 71.9 us -> 161 us
  other arithmetic: 56.8 us -> 23.2 us
    reduce_scatter x8 -> x5, waiting for transfers between devices: 938 us -> 0.06 us  [scatter_depth(): lax.psum_scatter(a.astype(BF16), 'fsdp', scatter_dimension=0, tiled=True)]
    all_gather x9 -> x4, waiting for transfers between devices: 836 us -> 0.03 us  [over_depth(): return lax.all_gather(a, 'fsdp', axis=0, tiled=True)]
    pallas_call x0 -> x15, Pallas kernels: none -> 422 us  [the longest x5 155 us: plane_gather(): pl.pallas_call(kernel, out_shape=jax.ShapeDtypeStruct((8, rows, width), x...]
    psum x1 -> x0, waiting for transfers between devices: 139 us -> none  [per_device(): lax.psum(attn_shards[1].astype(jnp.bfloat16), 'ctx').astype(jnp.float32)]
    dot_general x35 -> x4, matrix products: 162 us -> 31.2 us  [the longest x1 13.5 us: in_plane(): gate = jnp.dot(two_all, gate_w, preferred_element_type=F32)]
    reshape x0 -> x14, local copies, waits for them, and re-layouts: none -> 69.1 us  [the longest x3 37.4 us: columns_of(): a.reshape(plane, shard, depth, strip).transpose(1, 2, 0, 3)]
    slice x1 -> x14, local copies, waits for them, and re-layouts: 1.02 us -> 30.7 us  [the longest x1 9.34 us: in_plane(): down_total = joined[:, 2 * shard:].reshape(deep, width)]
    psum x1, blocking collectives: 12.7 us -> 41.8 us  [in_plane(): lax.psum(jnp.stack([gain_one_grad, gain_two_grad]), ('ctx', 'fsdp'))]
  transfers between devices with their start and end apart: 18 -> 9, of which waited for: 18 -> 0; matrix products, arithmetic and copies ran while one was open for 8% -> 17% of each run, Pallas kernels for 0% -> 36%
where the time goes in v1:
time: 795 us; the launch traced here: 787 us
  Pallas kernels  422 us (53%)
  local copies, waits for them, and re-layouts  161 us (20%)
  matrix products  97.4 us (12%)
  blocking collectives  68 us (9%)
  other arithmetic  23.2 us (3%)
  between operations  14.6 us (2%)
    pallas_call x5, Pallas kernels, plane_gather(): pl.pallas_call(kernel, out_shape=jax.ShapeDtypeStruct((8, rows, width), x...  155 us
    pallas_call x4, Pallas kernels, plane_scatter(): pl.pallas_call(scatter_kernel, out_shape=jax.ShapeDtypeStruct((rows, widt...  133 us
    psum x1, blocking collectives, in_plane(): lax.psum(jnp.stack([gain_one_grad, gain_two_grad]), ('ctx', 'fsdp'))  41.8 us
    pallas_call x1, Pallas kernels, first_gather(): pl.pallas_call(first_kernel, out_shape=(jax.ShapeDtypeStruct((8, rows, wi...  39 us
    reshape x3, local copies, waits for them, and re-layouts, columns_of(): a.reshape(plane, shard, depth, strip).transpose(1, 2, 0, 3)  37.4 us
    dot_general x5, matrix products, dot_first(): lax.dot_general(left, right, (((0,), (0,)), ((), ())), preferred_element_...  33.6 us
    unnamed x44, local copies, waits for them, and re-layouts  32.7 us
    dot_general x5, matrix products, dot_last(): lax.dot_general(left, right, (((1,), (1,)), ((), ())), preferred_element_...  32.5 us
  transfers between devices with their start and end apart: 9, of which 0 were waited for; matrix products, arithmetic and copies ran while one was open for 17% of the time, Pallas kernels for 36%

profile of v1, /device:TPU:0, one launch (start us, length us, event | category | flops | bytes accessed | tf_op | source)
XLA Modules:
  0.0 787.2 jit_solution(15965950642677492926)
XLA Ops:
  7.2 2.3 copy.79
  11.2 2.1 copy.80
  14.9 2.4 copy.78
  21.1 3.4 copy.87
  25.4 3.4 copy.86
  32.1 26.2 %all-gather = bf16[1,192,1536]{2,1,0:T(8,128)(2,1)} all-gather(bf16[1,48,1536]{2,1,0:T(8,128)(2,1)S(1)} %constant_dynamic-slice_fusion.4), channel_id=2, replica_groups=mesh['ctx'=8,'fsdp'=4] {'fsdp'}, dimensions={1}, use_global_device_ids=true | all-gather | bytes 737280 | tf_op jit(solution)/shard_map/all_gather | solution.py:971
  58.4 24.4 %plane_gather.5 = bf16[8,192,1536]{2,1,0:T(8,128)(2,1)} custom-call(bf16[192,1536]{1,0:T(8,128)(2,1)} %bitcast.160), custom_call_target="tpu_custom_call" | custom-call | bytes 94371840 | tf_op jit(solution)/shard_map/plane_gather/pallas_call | solution.py:496
  82.8 4.9 copy.85
  87.7 31.2 %plane_gather.7 = bf16[8,256,1536]{2,1,0:T(8,128)(2,1)} custom-call(bf16[256,1536]{1,0:T(8,128)(2,1)} %bitcast.158), custom_call_target="tpu_custom_call" | custom-call | bytes 125829120 | tf_op jit(solution)/shard_map/plane_gather/pallas_call | solution.py:496
  121.5 39.0 %first_gather.1 = (bf16[8,256,1536]{2,1,0:T(8,128)(2,1)}, f32[4,8,384]{2,1,0:T(8,128)}, s32[8,8,128]{2,1,0:T(8,128)}) custom-call(bf16[256,1536]{1,0:T(8,128)(2,1)} %bitcast.132, f32[8,384]{1,0:T(8,128)} %pad_maximum_fusion.2.gain_ref, s32[8,128]{1,0:T(8,128)} %iota.24.info_ref), custom_call_target="tpu_custom_call" | custom-call | tf_op jit(solution)/shard_map/first_gather/pallas_call | solution.py:682
  165.2 7.9 project.1
  173.1 27.2 %attend.1 = (f32[2048,256]{1,0:T(8,128)}, bf16[2048,256]{1,0:T(8,128)(2,1)}, f32[16,1,256]{2,1,0:T(1,128)}) custom-call(s32[16]{0:T(128)} %select_reduce_fusion.order_ref, bf16[2048,256]{1,0:T(8,128)(2,1)} %get-tuple-element.22.q_ref, bf16[2048,128]{1,0:T(8,128)(2,1)} %get-tuple-element.23.k_ref, bf16[2048,128]{1,0:T(8,128)(2,1)} %get-tuple-element.24.v_ref), custom_call_target="tpu_custom_call" | custom-call | tf_op jit(solution)/shard_map/attend/pallas_call | solution.py:823
  200.3 14.3 %plane_exchange.2 = bf16[8,256,256]{2,1,0:T(8,128)(2,1)} custom-call(bf16[8,256,256]{2,1,0:T(8,128)(2,1)} %bitcast.164), custom_call_target="tpu_custom_call" | custom-call | tf_op jit(solution)/shard_map/plane_exchange/pallas_call | solution.py:528
  214.6 1.8 copy.101
  216.4 3.8 multiply_reduce_fusion.2
  221.3 31.4 %plane_gather.6 = bf16[8,256,1536]{2,1,0:T(8,128)(2,1)} custom-call(bf16[256,1536]{1,0:T(8,128)(2,1)} %multiply_convert_fusion.1.x_ref), custom_call_target="tpu_custom_call" | custom-call | bytes 125829120 | tf_op jit(solution)/shard_map/plane_gather/pallas_call | solution.py:496
  252.8 8.8 %fusion.15 = f32[512,2048]{0,1:T(8,128)} fusion(bf16[2048,1536]{1,0:T(8,128)(2,1)} %bitcast.139, bf16[1,512,1536]{2,1,0:T(8,128)(2,1)} %all-gather.13.cloned.1.call-done), kind=kOutput, calls=%fused_computation.35 | convolution fusion | flops 3221225472 | bytes 12058624 | tf_op jit(solution)/shard_map/dot_general | solution.py:70
  261.5 8.7 %fusion.30 = f32[2048,512]{1,0:T(8,128)} fusion(bf16[2048,1536]{1,0:T(8,128)(2,1)} %bitcast.141, bf16[1536,512]{0,1:T(8,128)(2,1)} %all-gather.11.cloned.1.call-done), kind=kOutput, calls=%fused_computation.91 | convolution fusion | flops 3221225472 | bytes 12058624 | tf_op jit(solution)/shard_map/dot_general | solution.py:1027
  270.3 13.5 %fusion.4 = (bf16[2048,512]{1,0:T(8,128)(2,1)}, bf16[2048,512]{1,0:T(8,128)(2,1)}, bf16[2048,512]{1,0:T(8,128)(2,1)S(1)}) fusion(f32[512,2048]{0,1:T(8,128)} %fusion.15, f32[2048,512]{1,0:T(8,128)} %fusion.30, bf16[2048,1536]{1,0:T(8,128)(2,1)} %bitcast.142, bf16[1536,512]{0,1:T(8,128)(2,1)} %all-gather.9.cloned.1.call-done), kind=kOutput, calls=%fused_computation.12 | convolution fusion | flops 3238002688 | bytes 22544384 | tf_op jit(solution)/shard_map/dot_general | solution.py:1026
  283.7 5.3 convolution_convert_fusion.2
  289.0 35.2 %plane_scatter.4 = f32[256,1536]{1,0:T(8,128)} custom-call(bf16[8,256,1536]{2,1,0:T(8,128)(2,1)} %bitcast.149), custom_call_target="tpu_custom_call" | custom-call | tf_op jit(solution)/shard_map/plane_scatter/pallas_call | solution.py:621
  324.2 5.6 fusion.31
  329.9 5.3 add_convert_fusion
  335.1 35.2 %plane_scatter.5 = f32[256,1536]{1,0:T(8,128)} custom-call(bf16[8,256,1536]{2,1,0:T(8,128)(2,1)} %bitcast.147), custom_call_target="tpu_custom_call" | custom-call | tf_op jit(solution)/shard_map/plane_scatter/pallas_call | solution.py:621
  370.4 2.0 multiply_reduce_fusion
  375.6 2.5 copy.91
  378.1 27.8 %plane_scatter.7 = f32[192,1536]{1,0:T(8,128)} custom-call(bf16[8,192,1536]{2,1,0:T(8,128)(2,1)} %bitcast.134), custom_call_target="tpu_custom_call" | custom-call | tf_op jit(solution)/shard_map/plane_scatter/pallas_call | solution.py:621
  405.9 2.3 convert_element_type.106
  408.5 4.6 convolution_convert_fusion.7
  415.6 2.3 copy.102.x_ref
  417.9 14.6 %plane_exchange.3 = bf16[8,256,256]{2,1,0:T(8,128)(2,1)} custom-call(bf16[8,256,256]{2,1,0:T(8,128)(2,1)} %copy.102.x_ref), custom_call_target="tpu_custom_call" | custom-call | tf_op jit(solution)/shard_map/plane_exchange/pallas_call | solution.py:528
  432.5 31.0 %attend_back.1 = bf16[2048,512]{1,0:T(8,128)(2,1)} custom-call(s32[16]{0:T(128)} %select_reduce_fusion.order_ref, bf16[2048,256]{1,0:T(8,128)(2,1)} %get-tuple-element.22.q_ref, bf16[2048,128]{1,0:T(8,128)(2,1)} %get-tuple-element.23.k_ref, bf16[2048,128]{1,0:T(8,128)(2,1)} %get-tuple-element.24.v_ref, f32[2048,256]{1,0:T(8,128)} %get-tuple-element.27.o_ref, ...), custom_call_target="tpu_custom_call" | custom-call | tf_op jit(solution)/shard_map/attend_back/pallas_call | solution.py:912
  463.6 8.0 %convolution_convert_fusion.6 = bf16[1536,512]{1,0:T(8,128)(2,1)} fusion(bf16[2048,1536]{1,0:T(8,128)(2,1)} %bitcast.146, bf16[2048,512]{1,0:T(8,128)(2,1)} %attend_back.1), kind=kOutput, calls=%fused_computation.23 | convolution fusion | flops 3222011904 | bytes 9961472 | tf_op jit(solution)/shard_map/dot_general | solution.py:64
  471.7 8.0 %convolution_convert_fusion.3 = bf16[512,1536]{1,0:T(8,128)(2,1)} fusion(bf16[2048,512]{1,0:T(8,128)(2,1)} %copy-done.15, bf16[2048,1536]{1,0:T(8,128)(2,1)} %bitcast.140), kind=kOutput, calls=%fused_computation.20 | convolution fusion | flops 3222011904 | bytes 9961472 | tf_op jit(solution)/shard_map/dot_general | solution.py:64
  479.8 8.1 %convolution_convert_fusion.5 = bf16[1536,512]{1,0:T(8,128)(2,1)} fusion(bf16[2048,1536]{1,0:T(8,128)(2,1)} %bitcast.143, bf16[2048,512]{1,0:T(8,128)(2,1)} %get-tuple-element.74), kind=kOutput, calls=%fused_computation.22 | convolution fusion | flops 3222011904 | bytes 9961472 | tf_op jit(solution)/shard_map/dot_general | solution.py:64
  488.1 8.1 %convolution_convert_fusion.4 = bf16[1536,512]{1,0:T(8,128)(2,1)} fusion(bf16[2048,1536]{1,0:T(8,128)(2,1)} %bitcast.144, bf16[2048,512]{1,0:T(8,128)(2,1)} %get-tuple-element.73), kind=kOutput, calls=%fused_computation.21 | convolution fusion | flops 3222011904 | bytes 9961472 | tf_op jit(solution)/shard_map/dot_general | solution.py:64
  496.5 8.2 %convolution_convert_fusion.1 = bf16[2048,1536]{1,0:T(8,128)(2,1)} fusion(bf16[2048,512]{1,0:T(8,128)(2,1)} %attend_back.1, bf16[1536,512]{1,0:T(8,128)(2,1)} %all-gather.7.cloned.1.call-done.w_ref), kind=kOutput, calls=%fused_computation.2 | convolution fusion | flops 3224371200 | bytes 9961472 | tf_op jit(solution)/shard_map/dot_general | solution.py:70
  504.8 35.2 %plane_scatter.6 = f32[256,1536]{1,0:T(8,128)} custom-call(bf16[8,256,1536]{2,1,0:T(8,128)(2,1)} %bitcast.148), custom_call_target="tpu_custom_call" | custom-call | tf_op jit(solution)/shard_map/plane_scatter/pallas_call | solution.py:621
  539.9 1.8 fusion.14
  541.8 41.8 %psum.7 = f32[2,1536]{1,0:T(2,128)S(1)} all-reduce(f32[2,1536]{1,0:T(2,128)S(1)} %pad_maximum_fusion.3), channel_id=1, replica_groups=mesh['ctx'=8,'fsdp'=4] {'ctx','fsdp'}, use_global_device_ids=true, to_apply=%region_8.9 | all-reduce | flops 3072 | bytes 24576 | tf_op jit(solution)/shard_map/psum | solution.py:1094
  584.3 2.8 fusion.19
  588.1 1.9 pad_maximum_fusion.1.x_ref
  590.0 23.5 %plane_gather.8 = bf16[8,528,512]{2,1,0:T(8,128)(2,1)} custom-call(bf16[528,512]{1,0:T(8,128)(2,1)} %pad_maximum_fusion.1.x_ref), custom_call_target="tpu_custom_call" | custom-call | bytes 86507520 | tf_op jit(solution)/shard_map/plane_gather/pallas_call | solution.py:496
  613.6 1.8 slice.86
  616.2 3.6 slice.80
  619.8 7.5 reshape.236
  627.3 5.5 slice.85
  632.8 5.5 slice.83
  639.6 2.2 pad_maximum_fusion.x_ref
  641.8 44.4 %plane_gather.9 = bf16[8,1152,512]{2,1,0:T(8,128)(2,1)} custom-call(bf16[1152,512]{1,0:T(8,128)(2,1)} %pad_maximum_fusion.x_ref), custom_call_target="tpu_custom_call" | custom-call | bytes 188743680 | tf_op jit(solution)/shard_map/plane_gather/pallas_call | solution.py:496
  686.2 1.9 reshape.242
  688.1 4.9 copy.106
  693.0 2.7 copy.99
  695.6 3.3 copy.104
  699.0 1.8 slice.82
  700.8 2.0 copy.97
  702.8 3.5 copy.105
  707.7 9.3 %fusion.27 = (f32[8,384,512]{2,1,0:T(8,128)}, f32[8,384,512]{2,1,0:T(8,128)}, f32[8,384,512]{2,1,0:T(8,128)}) fusion(bf16[8,1152,512]{2,1,0:T(8,128)(2,1)} %plane_gather.9), kind=kLoop, calls=%fused_computation.88 | loop fusion | bytes 37748736 | tf_op jit(solution)/shard_map/slice | solution.py:1079
  717.1 7.8 reshape.248
  724.9 7.5 reshape.246
  732.4 9.1 %copy.96 = f32[384,4,8,128]{3,2,1,0:T(8,128)} copy(f32[384,4,8,128]{3,1,0,2:T(4,128)} %bitcast.128) | data formatting | bytes 12582912 | tf_op jit(solution)/shard_map/transpose | solution.py:1075
  741.5 7.7 reshape.244
  749.2 9.1 %copy.95 = f32[384,4,8,128]{3,2,1,0:T(8,128)} copy(f32[384,4,8,128]{3,1,0,2:T(4,128)} %bitcast.129) | data formatting | bytes 12582912 | tf_op jit(solution)/shard_map/transpose | solution.py:1075
  758.3 22.2 %copy_bitcast_fusion = (f32[384,4096]{1,0:T(8,128)}, f32[384,4096]{1,0:T(8,128)}) fusion(f32[48,8,32,128]{3,2,1,0:T(8,128)} %bitcast.130, f32[48,8,32,128]{3,2,1,0:T(8,128)} %bitcast.131), kind=kLoop, calls=%fused_computation.4 | loop fusion | bytes 25165824 | tf_op jit(solution)/shard_map/reshape | solution.py:1075
  (116 shorter events, 31.5 us)
Async XLA Ops:
  7.2 13.0 %copy-start = (bf16[1024,1536]{1,0:T(8,128)(2,1)S(1)}, bf16[1024,1536]{1,0:T(8,128)(2,1)}, u32[]{:S(2)}) copy-start(bf16[1024,1536]{1,0:T(8,128)(2,1)} %param.22) | copy-start | bytes 9437188
  7.2 158.0 %all-gather.7.cloned.1.call-start = ((), (), s32[]{:S(2)}) async-start(), calls=%async_computation.5 | async-start | bytes 1966080 | tf_op jit(solution)/shard_map/all_gather | solution.py:971
  20.2 232.6 %all-gather.13.cloned.1.call-start = ((), (), s32[]{:S(2)}) async-start(), calls=%async_computation.13 | async-start | bytes 1966080 | tf_op jit(solution)/shard_map/all_gather | solution.py:971
  21.0 240.5 %all-gather.11.cloned.1.call-start = ((), (), s32[]{:S(2)}) async-start(), calls=%async_computation.7 | async-start | bytes 1966080 | tf_op jit(solution)/shard_map/all_gather | solution.py:971
  25.3 4.4 copy-start.11
  25.3 244.9 %all-gather.9.cloned.1.call-start = ((), (), s32[]{:S(2)}) async-start(), calls=%async_computation.6 | async-start | bytes 1966080 | tf_op jit(solution)/shard_map/all_gather | solution.py:971
  29.6 557.5 %reduce-scatter.8.cloned.1.call-start = ((), (), s32[]{:S(2)}) async-start(), calls=%async_computation.9 | async-start | bytes 737280 | tf_op jit(solution)/shard_map/reduce_scatter | solution.py:1047
  87.7 32.5 %copy-start.9 = (bf16[384]{0:T(512)(128)(2,1)S(1)}, bf16[384]{0:T(512)(128)(2,1)}, u32[]{:S(2)}) copy-start(bf16[384]{0:T(512)(128)(2,1)} %param.14) | copy-start | bytes 2308
  87.7 32.5 %copy-start.10 = (bf16[384]{0:T(512)(128)(2,1)S(1)}, bf16[384]{0:T(512)(128)(2,1)}, u32[]{:S(2)}) copy-start(bf16[384]{0:T(512)(128)(2,1)} %param.19) | copy-start | bytes 2308
  214.6 1.9 copy-start.3
  270.2 13.5 %copy-start.12 = (bf16[1,512,1536]{2,1,0:T(8,128)(2,1)S(1)}, bf16[1,512,1536]{2,1,0:T(8,128)(2,1)}, u32[]{:S(2)}) copy-start(bf16[1,512,1536]{2,1,0:T(8,128)(2,1)} %all-gather.13.cloned.1.call-done) | copy-start | bytes 4718596
  283.7 5.3 copy-start.15
  324.2 5.6 copy-start.13
  324.2 5.6 copy-start.14
  335.1 37.2 %copy-start.8 = (bf16[1,256,1536]{2,1,0:T(8,128)(2,1)S(1)}, bf16[1,256,1536]{2,1,0:T(8,128)(2,1)}, u32[]{:S(2)}) copy-start(bf16[1,256,1536]{2,1,0:T(8,128)(2,1)} %param.23) | copy-start | bytes 2359300
  370.4 2.0 copy-start.6
  370.4 2.3 copy-start.7
  374.2 1.4 copy-start.4
  405.9 2.6 copy-start.5
  408.3 179.8 %reduce-scatter.6.cloned.1.call-start = ((), (), s32[]{:S(2)}) async-start(), calls=%async_computation.8 | async-start | bytes 1966080 | tf_op jit(solution)/shard_map/reduce_scatter | solution.py:1047
  471.6 166.8 %reduce-scatter.14.cloned.1.call-start = ((), (), s32[]{:S(2)}) async-start(), calls=%async_computation.12 | async-start | bytes 1966080 | tf_op jit(solution)/shard_map/reduce_scatter | solution.py:1047
  479.7 159.9 %reduce-scatter.10.cloned.1.call-start = ((), (), s32[]{:S(2)}) async-start(), calls=%async_computation.10 | async-start | bytes 1966080 | tf_op jit(solution)/shard_map/reduce_scatter | solution.py:1047
  487.9 151.8 %reduce-scatter.12.cloned.1.call-start = ((), (), s32[]{:S(2)}) async-start(), calls=%async_computation.11 | async-start | bytes 1966080 | tf_op jit(solution)/shard_map/reduce_scatter | solution.py:1047
  613.5 2.6 copy-start.2
  688.1 7.5 slice-start
  758.3 22.2 %copy-start.1 = (bf16[1024,1536]{1,0:T(8,128)(2,1)S(1)}, bf16[1024,1536]{1,0:T(8,128)(2,1)}, u32[]{:S(2)}) copy-start(bf16[1024,1536]{1,0:T(8,128)(2,1)} %param.22) | copy-start | bytes 9437188
Sparse Core Ops, SparseCore 0:
  20.3 49.2 all-gather.6
  71.7 35.9 all-gather.12
  109.9 37.1 all-gather.10
  148.4 35.8 all-gather.8
  408.4 22.3 reduce-scatter.7
  471.7 35.6 reduce-scatter.5
  509.7 34.2 reduce-scatter.13
  546.3 35.3 reduce-scatter.9
  584.0 34.2 reduce-scatter.11

commit v2 on v1

--- a/solution.py
+++ b/solution.py
@@ -417,19 +417,14 @@
 
 
 class Gather:
-    def __init__(self, c, own, buf, send, recv):
-        self.c, self.own, self.buf, self.send, self.recv = c, own, buf, send, recv
-        self.half = buf.shape[1] // 2
+    def __init__(self, c, own, buf, at, send, recv):
+        self.c, self.own, self.buf, self.at, self.send, self.recv = c, own, buf, at, send, recv
         self.pending = []
 
-    def rows(self, h):
-        return pl.ds(h * self.half, self.half)
-
     def start(self, channel, who, to, h, own=False):
-        source = flip(self.c, who)
-        there = self.buf.at[source, self.rows(h)]
+        there = self.at(self.buf, flip(self.c, who), h)
         d = remote(
-            self.own.at[self.rows(h)] if own else there,
+            self.own(h) if own else there,
             there,
             self.send.at[channel, h],
             self.recv.at[channel, h],
@@ -439,7 +434,7 @@
         self.pending.append(d)
 
     def arrived(self, channel, who, frm, h):
-        ref = self.buf.at[flip(self.c, who), self.rows(h)]
+        ref = self.at(self.buf, flip(self.c, who), h)
         remote(
             ref, ref, self.send.at[channel, h], self.recv.at[channel, h], ctx=flip(self.c, frm)
         ).wait_recv()
@@ -452,26 +447,98 @@
         self.start(0, 0, 1, 0, own=True)
         self.start(0, 0, 1, 1, own=True)
 
-    def finish(self):
+    def near_half(self):
         self.arrived(1, 2, 2, 0)
         self.start(6, 2, 4, 0)
         self.start(3, 2, 1, 0)
         self.arrived(2, 4, 4, 1)
         self.start(7, 4, 2, 1)
         self.start(4, 4, 1, 1)
+
+    def near_rest(self):
         self.arrived(1, 2, 2, 1)
         self.start(3, 2, 1, 1)
         self.arrived(2, 4, 4, 0)
         self.start(4, 4, 1, 0)
+
+    def far(self):
         self.arrived(6, 6, 4, 0)
         self.start(5, 6, 1, 0)
         self.arrived(7, 6, 2, 1)
         self.start(5, 6, 1, 1)
+
+    def paired(self, channel, who):
+        for h in (0, 1):
+            self.arrived(channel, who, 1, h)
+
+    def finish(self):
+        self.near_half()
+        self.near_rest()
+        self.far()
         for channel, who in ((0, 1), (3, 3), (4, 5), (5, 7)):
-            for h in (0, 1):
-                self.arrived(channel, who, 1, h)
+            self.paired(channel, who)
+
+    def sent(self):
         for d in self.pending:
             d.wait_send()
+
+
+def row_half(ref, d, h):
+    half = ref.shape[1] // 2
+    return ref.at[d, pl.ds(h * half, half)]
+
+
+def column_half(ref, d, h):
+    half = ref.shape[2] // 2
+    return ref.at[d, :, pl.ds(h * half, half)]
+
+
+def own_half(ref, axis=0):
+    half = ref.shape[axis] // 2
+    return lambda h: ref.at[(slice(None),) * axis + (pl.ds(h * half, half),)]
+
+
+class Line:
+    def __init__(self, z, depth, at, send, recv):
+        self.z, self.depth, self.at, self.send, self.recv = z, depth, at, send, recv
+
+    def copy(self, way, k, part, to):
+        ref = self.at(part)
+        return remote(ref, ref, self.send.at[way, k], self.recv.at[way, k], fsdp=to)
+
+    def step(self, k):
+        z, top = self.z, self.depth - 1
+
+        @pl.when((z >= k) & (z < top))
+        def _():
+            self.copy(0, k, z - k, z + 1).start()
+
+        @pl.when((z + k <= top) & (z > 0))
+        def _():
+            self.copy(1, k, z + k, z - 1).start()
+
+    def landed(self, k):
+        z, top = self.z, self.depth - 1
+
+        @pl.when(z >= k + 1)
+        def _():
+            self.copy(0, k, z - 1 - k, z - 1).wait_recv()
+
+        @pl.when(z + 1 + k <= top)
+        def _():
+            self.copy(1, k, z + 1 + k, z + 1).wait_recv()
+
+    def sent(self):
+        z, top = self.z, self.depth - 1
+        for k in range(top):
+
+            @pl.when((z >= k) & (z < top))
+            def _():
+                self.copy(0, k, z - k, z + 1).wait_send()
+
+            @pl.when((z + k <= top) & (z > 0))
+            def _():
+                self.copy(1, k, z + k, z - 1).wait_send()
 
 
 def params(cid):
@@ -480,29 +547,39 @@
     )
 
 
-def plane_gather(x, cid):
-    rows, width = x.shape
-
-    def kernel(x_ref, o_ref, send, recv, local):
+def plane_gather(arrays, cid):
+    n = len(arrays)
+    by_rows = [a.shape[0] % 32 == 0 for a in arrays]
+
+    def kernel(*refs):
+        ins, outs, (send, recv, local) = refs[:n], refs[n : 2 * n], refs[2 * n :]
         c = lax.axis_index("ctx")
         greet([{"ctx": flip(c, k)} for k in (1, 2, 4)])
-        here = pltpu.make_async_copy(x_ref, o_ref.at[c], local)
-        here.start()
-        g = Gather(c, x_ref, o_ref, send, recv)
-        g.begin()
-        g.finish()
-        here.wait()
+        here = [pltpu.make_async_copy(ins[i], outs[i].at[c], local.at[i]) for i in range(n)]
+        gathers = []
+        for i in range(n):
+            at, own = (row_half, own_half(ins[i])) if by_rows[i] else (column_half, own_half(ins[i], 1))
+            gathers.append(Gather(c, own, outs[i], at, send.at[i], recv.at[i]))
+        for g in gathers:
+            g.begin()
+        for h in here:
+            h.start()
+        for g in gathers:
+            g.finish()
+        for h in here:
+            h.wait()
+        for g in gathers:
+            g.sent()
 
     return pl.pallas_call(
         kernel,
-        out_shape=jax.ShapeDtypeStruct((8, rows, width), x.dtype),
-        in_specs=[pl.BlockSpec(memory_space=ANY)],
-        out_specs=pl.BlockSpec(memory_space=ANY),
-        scratch_shapes=[DMA((8, 2)), DMA((8, 2)), DMA],
+        out_shape=[jax.ShapeDtypeStruct((8,) + a.shape, a.dtype) for a in arrays],
+        in_specs=[pl.BlockSpec(memory_space=ANY)] * n,
+        out_specs=[pl.BlockSpec(memory_space=ANY)] * n,
+        scratch_shapes=[DMA((n, 8, 2)), DMA((n, 8, 2)), DMA((n,))],
         compiler_params=params(cid),
-        cost_estimate=pl.CostEstimate(flops=0, bytes_accessed=16 * rows * width * 20, transcendentals=0),
         name="plane_gather",
-    )(x)
+    )(*arrays)
 
 
 def plane_exchange(x, cid):
@@ -638,290 +715,514 @@
     )(p)
 
 
-def first_kernel(x_ref, gain_ref, info_ref, all_ref, gains_ref, infos_ref, normed, *sems):
-    gsend, grecv, isend, irecv, send, recv, local = sems
+def contract(a, b, dims):
+    return lax.dot_general(a, b, ((dims[0], dims[1]), ((), ())), preferred_element_type=F32)
+
+
+def lanes(start, size):
+    return pl.ds(pl.multiple_of(start, LANES), size)
+
+
+def turned(u, cosine, sine):
+    half = HEAD_SIZE // 2
+    a, b = u[:half], u[half:]
+    return jnp.concatenate([a * cosine - b * sine, b * cosine + a * sine], 0)
+
+
+def picked(weight, first, count):
+    shape = (count, weight.shape[1])
+    hit = lax.broadcasted_iota(jnp.int32, shape, 1) == first + lax.broadcasted_iota(jnp.int32, shape, 0)
+    return contract(hit.astype(BF16), weight, ((1,), (1,))).astype(BF16)
+
+
+def first_kernel(
+    x_ref, gain_ref, info_ref, base_ref, step_ref, wq_ref, wk_ref, wv_ref, wo_ref, wg_ref, wu_ref, wd_ref,
+    all_ref, qkv_ref, w_ref, table_ref, gains_ref, infos_ref, wo_all, gu_ref, down_ref,
+    xs, bases, gsend, grecv, isend, irecv, bsend, brecv, send, recv, zsend, zrecv, osend, orecv, local, parts,
+):
     c = lax.axis_index("ctx")
     z = lax.axis_index("fsdp")
     depth = gains_ref.shape[0]
+    shard, width = wq_ref.shape
+    rows = x_ref.shape[0]
+    strip = gu_ref.shape[1] // 2 // depth
     others = [lax.rem(z + k, depth) for k in range(1, depth)]
     greet([{"ctx": flip(c, k)} for k in range(1, 8)] + [{"fsdp": o} for o in others])
+
     sent = []
     for k, o in enumerate(others):
-        d = remote(gain_ref, gains_ref.at[z], gsend.at[k], grecv.at[k], fsdp=o)
+        sent.append(remote(gain_ref, gains_ref.at[z], gsend.at[k], grecv.at[k], fsdp=o))
+    for k in range(1, 8):
+        sent.append(remote(info_ref, infos_ref.at[c], isend.at[k], irecv.at[k], ctx=flip(c, k)))
+        sent.append(remote(base_ref, bases.at[c], bsend.at[k], brecv.at[k], ctx=flip(c, k)))
+    for d in sent:
         d.start()
-        sent.append(d)
-    for k in range(1, 8):
-        d = remote(info_ref, infos_ref.at[c], isend.at[k], irecv.at[k], ctx=flip(c, k))
-        d.start()
-        sent.append(d)
+    out_rows = shard // 8
+    mine = pltpu.make_async_copy(wo_ref.at[pl.ds(c * out_rows, out_rows)], wo_all.at[z], parts.at[0])
+    mine.start()
     gains_ref[z] = gain_ref[...]
     infos_ref[c] = info_ref[...]
+    bases[c] = base_ref[...]
+
+    own = lanes(z * shard, shard)
+    count = 2 * HEAD_SIZE
+    w_ref[:count, own] = picked(wq_ref[...], c * count, count)
+    w_ref[count : count + HEAD_SIZE, own] = picked(wk_ref[...], c * HEAD_SIZE, HEAD_SIZE)
+    w_ref[count + HEAD_SIZE :, own] = picked(wv_ref[...], c * HEAD_SIZE, HEAD_SIZE)
+    line = Line(z, depth, lambda d: w_ref.at[:, lanes(d * shard, shard)], zsend, zrecv)
+    line.step(0)
+
     x = x_ref[...].astype(F32)
     factor = lax.rsqrt(jnp.mean(x * x, -1, keepdims=True) + EPS)
     for k in range(depth - 1):
         ref = gains_ref.at[lax.rem(z + depth - 1 - k, depth)]
         remote(ref, ref, gsend.at[k], grecv.at[k], fsdp=others[k]).wait_recv()
     gain = jnp.concatenate([gains_ref[k, 0:1, :] for k in range(depth)], 1)
-    normed[...] = (x * factor * gain).astype(BF16)
-    here = pltpu.make_async_copy(normed, all_ref.at[c], local)
-    here.start()
-    g = Gather(c, normed, all_ref, send, recv)
+    xs[c] = (x * factor * gain).astype(BF16)
+    g = Gather(c, own_half(xs.at[c]), xs, row_half, send, recv)
     g.begin()
-    g.finish()
-    here.wait()
-    for k in range(1, 8):
-        ref = infos_ref.at[flip(c, k)]
-        remote(ref, ref, isend.at[k], irecv.at[k], ctx=flip(c, k)).wait_recv()
+    mine.wait()
+    out_line = Line(z, depth, lambda d: wo_all.at[d], osend, orecv)
+    out_line.step(0)
+
+    copies = [pltpu.make_async_copy(wd_ref.at[pl.ds(c * down_ref.shape[0], down_ref.shape[0])], down_ref, parts.at[1])]
+    for i, weight in enumerate((wg_ref, wu_ref)):
+        for s in range(depth):
+            copies.append(
+                pltpu.make_async_copy(
+                    weight.at[:, lanes((s * 8 + c) * strip, strip)],
+                    gu_ref.at[:, pl.ds((i * depth + s) * strip, strip)],
+                    parts.at[2 + i * depth + s],
+                )
+            )
+    for d in copies:
+        d.start()
+
+    def keep(k):
+        d = pltpu.make_async_copy(xs.at[flip(c, k)], all_ref.at[flip(c, k)], local.at[k])
+        d.start()
+        copies.append(d)
+
+    keep(0)
+
+    def rotary(k):
+        d = flip(c, k)
+        if k:
+            for ref, s, r in ((bases, bsend, brecv), (infos_ref, isend, irecv)):
+                remote(ref.at[d], ref.at[d], s.at[k], r.at[k], ctx=d).wait_recv()
+        half = HEAD_SIZE // 2
+        step_cos, step_sin = step_ref[:half], step_ref[half:]
+        for b in (0, 1):
+            start = b * (LANES // 2)
+            base_cos = bases[d, :, start : start + 1]
+            base_sin = bases[d, :, start + LANES // 4 : start + LANES // 4 + 1]
+            at = lanes(d * rows + b * BLOCK, BLOCK)
+            table_ref[:half, at] = base_cos * step_cos - base_sin * step_sin
+            table_ref[half:, at] = base_sin * step_cos + base_cos * step_sin
+
+    for k in range(8):
+        rotary(k)
+
+    def project(k):
+        d = flip(c, k)
+        at = lanes(d * rows, rows)
+        half = HEAD_SIZE // 2
+        cosine, sine = table_ref[:half, at], table_ref[half:, at]
+        raw = contract(w_ref[...], xs[d], ((1,), (1,)))
+        for h in range(3):
+            head = slice(h * HEAD_SIZE, (h + 1) * HEAD_SIZE)
+            qkv_ref[head, at] = turned(raw[head], cosine, sine).astype(BF16)
+        qkv_ref[3 * HEAD_SIZE :, at] = raw[3 * HEAD_SIZE :].astype(BF16)
+
+    line.landed(0)
+    line.step(1)
+    g.near_half()
+    out_line.landed(0)
+    out_line.step(1)
+    line.landed(1)
+    line.step(2)
+    g.near_rest()
+    keep(2)
+    keep(4)
+    out_line.landed(1)
+    out_line.step(2)
+    line.landed(2)
+    project(0)
+    g.far()
+    project(2)
+    project(4)
+    for channel, k in ((0, 1), (3, 3), (4, 5)):
+        g.paired(channel, k)
+        keep(k)
+        project(k)
+    keep(6)
+    project(6)
+    g.paired(5, 7)
+    keep(7)
+    project(7)
+    out_line.landed(2)
+    for d in copies:
+        d.wait()
     for d in sent:
         d.wait_send()
-
-
-def first_gather(x, gains, info, depth, cid):
+    line.sent()
+    out_line.sent()
+    g.sent()
+
+
+def first_part(x, gains, info, base, step, weights, depth, cid):
     rows, width = x.shape
+    shard = gains.shape[1]
+    columns = weights[4].shape[1]
+    down_rows = weights[6].shape[0] // 8
     vm = pl.BlockSpec(memory_space=VMEM)
+    hbm = pl.BlockSpec(memory_space=ANY)
+    shape = jax.ShapeDtypeStruct
     return pl.pallas_call(
         first_kernel,
         out_shape=(
-            jax.ShapeDtypeStruct((8, rows, width), BF16),
-            jax.ShapeDtypeStruct((depth,) + gains.shape, F32),
-            jax.ShapeDtypeStruct((8,) + info.shape, jnp.int32),
+            shape((8, rows, width), BF16),
+            shape((4 * HEAD_SIZE, 8 * rows), BF16),
+            shape((4 * HEAD_SIZE, width), BF16),
+            shape((HEAD_SIZE, 8 * rows), F32),
+            shape((depth,) + gains.shape, F32),
+            shape((8,) + info.shape, jnp.int32),
+            shape((depth, shard // 8, width), BF16),
+            shape((shard, 2 * columns // 8), BF16),
+            shape((down_rows, width), BF16),
         ),
-        in_specs=[vm, vm, vm],
-        out_specs=(pl.BlockSpec(memory_space=ANY), vm, vm),
+        in_specs=[vm] * 8 + [hbm] * 4,
+        out_specs=(hbm, vm, vm, vm, vm, vm, hbm, hbm, hbm),
         scratch_shapes=[
-            VMEM((rows, width), BF16),
+            VMEM((8, rows, width), BF16),
+            VMEM((8,) + base.shape, F32),
             DMA((depth,)),
             DMA((depth,)),
             DMA((8,)),
             DMA((8,)),
+            DMA((8,)),
+            DMA((8,)),
             DMA((8, 2)),
             DMA((8, 2)),
-            DMA,
+            DMA((2, depth)),
+            DMA((2, depth)),
+            DMA((2, depth)),
+            DMA((2, depth)),
+            DMA((8,)),
+            DMA((2 + 2 * depth,)),
         ],
         compiler_params=params(cid),
-        name="first_gather",
-    )(x, gains, info)
-
-
-def angles(base_cos, base_sin, step_cos, step_sin):
-    return (
-        base_cos * step_cos - base_sin * step_sin,
-        base_sin * step_cos + base_cos * step_sin,
-    )
-
-
-def turn(u, cosine, sine, sign):
-    lane = lax.broadcasted_iota(jnp.int32, u.shape, 1)
-    signed = jnp.where(lane < LANES // 2, -sign, sign) * sine
-    return u * cosine + pltpu.roll(u, LANES // 2, 1) * signed
-
-
-def qkv_kernel(x_ref, w_ref, bc_ref, bs_ref, sc_ref, ss_ref, q_ref, k_ref, v_ref):
-    i = pl.program_id(0)
-    raw = jnp.dot(x_ref[...], w_ref[...], preferred_element_type=F32)
-    blocks = x_ref.shape[0] // BLOCK
-    for b in range(blocks):
-        row = pl.ds(i * blocks + b, 1)
-        cosine, sine = angles(bc_ref[row, :], bs_ref[row, :], sc_ref[...], ss_ref[...])
-        rows = slice(b * BLOCK, (b + 1) * BLOCK)
-        for h in (0, 1):
-            cols = slice(h * LANES, (h + 1) * LANES)
-            q_ref[rows, cols] = turn(raw[rows, cols], cosine, sine, 1.0).astype(BF16)
-        k_ref[rows, :] = turn(raw[rows, 2 * LANES : 3 * LANES], cosine, sine, 1.0).astype(BF16)
-        v_ref[rows, :] = raw[rows, 3 * LANES :].astype(BF16)
-
-
-def project(x, w, tables_in):
-    tokens, width = x.shape
-    step = 512
-    whole = lambda a: pl.BlockSpec(a.shape, lambda i: (0, 0))
-    return pl.pallas_call(
-        qkv_kernel,
-        grid=(tokens // step,),
-        out_shape=(
-            jax.ShapeDtypeStruct((tokens, 2 * LANES), BF16),
-            jax.ShapeDtypeStruct((tokens, LANES), BF16),
-            jax.ShapeDtypeStruct((tokens, LANES), BF16),
-        ),
-        in_specs=[pl.BlockSpec((step, width), lambda i: (i, 0)), whole(w)] + [whole(t) for t in tables_in],
-        out_specs=(
-            pl.BlockSpec((step, 2 * LANES), lambda i: (i, 0)),
-            pl.BlockSpec((step, LANES), lambda i: (i, 0)),
-            pl.BlockSpec((step, LANES), lambda i: (i, 0)),
-        ),
-        compiler_params=pltpu.CompilerParams(vmem_limit_bytes=VMEM_BYTES),
-        name="project",
-    )(x, w, *tables_in)
+        name="first_part",
+    )(x, gains, info, base, step, *weights)
 
 
 CHUNK = 512
 
 
-def both_heads(ref, start):
-    rows = pl.ds(pl.multiple_of(start, BLOCK), BLOCK)
-    return jnp.concatenate([ref[rows, :LANES], ref[rows, LANES:]], 0)
-
-
-def order_rows(order_ref, tokens, pairs):
-    for j in range(tokens // BLOCK):
-        rows = pl.ds(pl.multiple_of(order_ref[j] * BLOCK, BLOCK), BLOCK)
-        for source, target in pairs:
-            target[j * BLOCK : (j + 1) * BLOCK, :] = source[rows, :]
-
-
-def contract(a, b, dims):
-    return lax.dot_general(a, b, ((dims[0], dims[1]), ((), ())), preferred_element_type=F32)
-
-
-def attend_kernel(order_ref, q_ref, k_ref, v_ref, o_ref, low_ref, lse_ref, keys, values):
+def whole_block(a):
+    return pl.BlockSpec(a.shape, lambda j, *_: (0,) * len(a.shape))
+
+
+def two_heads(ref, at):
+    return jnp.concatenate([ref[:HEAD_SIZE, at], ref[HEAD_SIZE : 2 * HEAD_SIZE, at]], 1)
+
+
+def causal(s, t, j):
+    key = t * CHUNK + lax.broadcasted_iota(jnp.int32, s.shape, 0)
+    query = j * BLOCK + lax.broadcasted_iota(jnp.int32, s.shape, 1) % BLOCK
+    return jnp.where(key <= query, s, -jnp.inf)
+
+
+def attend_kernel(order_ref, qkv_ref, o_ref, low_ref, lse_ref, keys, values):
     j = pl.program_id(0)
-    tokens = q_ref.shape[0]
+    tokens = qkv_ref.shape[1]
     factor = HEAD_SIZE ** (-0.5) * math.log2(math.e)
 
     @pl.when(j == 0)
     def _():
-        order_rows(order_ref, tokens, ((k_ref, keys), (v_ref, values)))
-
-    start = order_ref[j] * BLOCK
-    q = both_heads(q_ref, start)
+        for b in range(tokens // BLOCK):
+            at = lanes(order_ref[b] * BLOCK, BLOCK)
+            there = slice(b * BLOCK, (b + 1) * BLOCK)
+            keys[there, :] = qkv_ref[2 * HEAD_SIZE : 3 * HEAD_SIZE, at].T
+            values[:, there] = qkv_ref[3 * HEAD_SIZE :, at]
+
+    block = order_ref[j]
+    at = lanes(block * BLOCK, BLOCK)
+    q = two_heads(qkv_ref, at)
     last = j // (CHUNK // BLOCK)
 
     def step(t, carry, masked):
         top, denom, acc = carry
-        rows = pl.ds(pl.multiple_of(t * CHUNK, CHUNK), CHUNK)
-        s = contract(keys[rows, :], q, ((1,), (1,)))
+        s = jnp.dot(keys[pl.ds(pl.multiple_of(t * CHUNK, CHUNK), CHUNK), :], q, preferred_element_type=F32)
         if masked:
-            key = t * CHUNK + lax.broadcasted_iota(jnp.int32, s.shape, 0)
-            query = j * BLOCK + lax.broadcasted_iota(jnp.int32, s.shape, 1) % BLOCK
-            s = jnp.where(key <= query, s, -jnp.inf)
+            s = causal(s, t, j)
         new_top = jnp.maximum(top, jnp.max(s, 0, keepdims=True))
         p = jnp.exp2((s - new_top) * factor)
         shrink = jnp.exp2((top - new_top) * factor)
         denom = denom * shrink + jnp.sum(p, 0, keepdims=True)
-        acc = acc * shrink + contract(values[rows, :], p.astype(BF16), ((0,), (0,)))
+        acc = acc * shrink + jnp.dot(values[:, lanes(t * CHUNK, CHUNK)], p.astype(BF16), preferred_element_type=F32)
         return new_top, denom, acc
 
     carry = (
         jnp.full((1, 2 * BLOCK), -1e30, F32),
         jnp.zeros((1, 2 * BLOCK), F32),
-        jnp.zeros((LANES, 2 * BLOCK), F32),
+        jnp.zeros((HEAD_SIZE, 2 * BLOCK), F32),
     )
     carry = lax.fori_loop(0, last, lambda t, state: step(t, state, False), carry)
     top, denom, acc = step(last, carry, True)
-    out = (acc / denom).T
+    out = acc / denom
     lse_ref[pl.ds(j, 1), :, :] = (top * factor + jnp.log2(denom)).reshape(1, 1, 2 * BLOCK)
-    out = jnp.concatenate([out[:BLOCK], out[BLOCK:]], 1)
-    rows = pl.ds(pl.multiple_of(start, BLOCK), BLOCK)
-    o_ref[rows, :] = out
-    low_ref[rows, :] = out.astype(BF16)
-
-
-def attend(order, q, k, v):
-    tokens = q.shape[0]
+    device = block // 2
+    within = lanes((block - 2 * device) * BLOCK, BLOCK)
+    for h in (0, 1):
+        head = slice(h * HEAD_SIZE, (h + 1) * HEAD_SIZE)
+        part = out[:, h * BLOCK : (h + 1) * BLOCK]
+        o_ref[head, at] = part
+        low_ref[device, head, within] = part.astype(BF16)
+
+
+def attend(order, qkv):
+    tokens = qkv.shape[1]
     blocks = tokens // BLOCK
-    whole = lambda *shape: pl.BlockSpec(shape, lambda j, *_: (0,) * len(shape))
+    outs = (
+        jax.ShapeDtypeStruct((2 * HEAD_SIZE, tokens), F32),
+        jax.ShapeDtypeStruct((8, 2 * HEAD_SIZE, tokens // 8), BF16),
+        jax.ShapeDtypeStruct((blocks, 1, 2 * BLOCK), F32),
+    )
     return pl.pallas_call(
         attend_kernel,
         grid_spec=pltpu.PrefetchScalarGridSpec(
             num_scalar_prefetch=1,
             grid=(blocks,),
-            in_specs=[whole(*q.shape), whole(*k.shape), whole(*v.shape)],
-            out_specs=(whole(tokens, 2 * LANES), whole(tokens, 2 * LANES), whole(blocks, 1, 2 * BLOCK)),
-            scratch_shapes=[VMEM(k.shape, BF16), VMEM(v.shape, BF16)],
+            in_specs=[whole_block(qkv)],
+            out_specs=[whole_block(a) for a in outs],
+            scratch_shapes=[VMEM((tokens, HEAD_SIZE), BF16), VMEM((HEAD_SIZE, tokens), BF16)],
         ),
-        out_shape=(
-            jax.ShapeDtypeStruct((tokens, 2 * LANES), F32),
-            jax.ShapeDtypeStruct((tokens, 2 * LANES), BF16),
-            jax.ShapeDtypeStruct((blocks, 1, 2 * BLOCK), F32),
-        ),
+        out_shape=outs,
         compiler_params=pltpu.CompilerParams(vmem_limit_bytes=VMEM_BYTES),
         name="attend",
-    )(order, q, k, v)
+    )(order, qkv)
 
 
 def attend_back_kernel(
-    order_ref, q_ref, k_ref, v_ref, o_ref, do_ref, lse_ref, bc_ref, bs_ref, sc_ref, ss_ref, d_ref, keys, values, dk, dv
+    order_ref, qkv_ref, o_ref, do_ref, lse_ref, table_ref, d_ref, keys, keys_t, values, dk, dv
 ):
     j = pl.program_id(0)
-    tokens = q_ref.shape[0]
+    tokens = qkv_ref.shape[1]
     scale = HEAD_SIZE ** (-0.5)
     factor = scale * math.log2(math.e)
+    half = HEAD_SIZE // 2
 
     @pl.when(j == 0)
     def _():
-        order_rows(order_ref, tokens, ((k_ref, keys), (v_ref, values)))
+        for b in range(tokens // BLOCK):
+            at = lanes(order_ref[b] * BLOCK, BLOCK)
+            there = slice(b * BLOCK, (b + 1) * BLOCK)
+            key = qkv_ref[2 * HEAD_SIZE : 3 * HEAD_SIZE, at]
+            keys[there, :] = key.T
+            keys_t[:, there] = key
+            values[there, :] = qkv_ref[3 * HEAD_SIZE :, at].T
         dk[...] = jnp.zeros_like(dk)
         dv[...] = jnp.zeros_like(dv)
 
     block = order_ref[j]
-    start = block * BLOCK
-    q = both_heads(q_ref, start)
-    do = both_heads(do_ref, start)
-    delta = jnp.sum((both_heads(o_ref, start) * do.astype(F32)).T, 0, keepdims=True)
+    at = lanes(block * BLOCK, BLOCK)
+    q = two_heads(qkv_ref, at)
+    device = block // 2
+    within = lanes((block - 2 * device) * BLOCK, BLOCK)
+    do = jnp.concatenate([do_ref[device, :HEAD_SIZE, within], do_ref[device, HEAD_SIZE:, within]], 1)
+    delta = jnp.sum(two_heads(o_ref, at) * do.astype(F32), 0, keepdims=True)
     lse = lse_ref[j]
     last = j // (CHUNK // BLOCK)
 
     def step(t, dq, masked):
         rows = pl.ds(pl.multiple_of(t * CHUNK, CHUNK), CHUNK)
-        key_rows = keys[rows, :]
-        s = contract(key_rows, q, ((1,), (1,)))
+        s = jnp.dot(keys[rows, :], q, preferred_element_type=F32)
         if masked:
-            key = t * CHUNK + lax.broadcasted_iota(jnp.int32, s.shape, 0)
-            query = j * BLOCK + lax.broadcasted_iota(jnp.int32, s.shape, 1) % BLOCK
-            s = jnp.where(key <= query, s, -jnp.inf)
+            s = causal(s, t, j)
         p = jnp.exp2(s * factor - lse)
-        dp = contract(values[rows, :], do, ((1,), (1,)))
+        dp = jnp.dot(values[rows, :], do, preferred_element_type=F32)
         ds = (p * (dp - delta)).astype(BF16)
-        dv[rows, :] += jnp.dot(p.astype(BF16), do, preferred_element_type=F32)
-        dk[rows, :] += jnp.dot(ds, q, preferred_element_type=F32)
-        return dq + contract(key_rows, ds, ((0,), (0,)))
-
-    dq = jnp.zeros((LANES, 2 * BLOCK), F32)
+        dv[rows, :] += contract(p.astype(BF16), do, ((1,), (1,)))
+        dk[rows, :] += contract(ds, q, ((1,), (1,)))
+        return dq + jnp.dot(keys_t[:, lanes(t * CHUNK, CHUNK)], ds, preferred_element_type=F32)
+
+    dq = jnp.zeros((HEAD_SIZE, 2 * BLOCK), F32)
     dq = lax.fori_loop(0, last, lambda t, state: step(t, state, False), dq)
-    dq = step(last, dq, True).T * scale
-
-    def table(at):
-        row = pl.ds(at, 1)
-        return angles(bc_ref[row, :], bs_ref[row, :], sc_ref[...], ss_ref[...])
-
-    cosine, sine = table(block)
-    rows = pl.ds(pl.multiple_of(start, BLOCK), BLOCK)
+    dq = step(last, dq, True) * scale
     for h in (0, 1):
-        part = dq[h * BLOCK : (h + 1) * BLOCK]
-        d_ref[rows, h * LANES : (h + 1) * LANES] = turn(part, cosine, sine, -1.0).astype(BF16)
+        head = slice(h * HEAD_SIZE, (h + 1) * HEAD_SIZE)
+        d_ref[head, at] = turned(dq[:, h * BLOCK : (h + 1) * BLOCK], table_ref[:half, at], -table_ref[half:, at]).astype(BF16)
 
     @pl.when(j == tokens // BLOCK - 1)
     def _():
-        def put(b, unused):
-            at = order_ref[b]
-            cosine, sine = table(at)
-            source = pl.ds(pl.multiple_of(b * BLOCK, BLOCK), BLOCK)
-            rows = pl.ds(pl.multiple_of(at * BLOCK, BLOCK), BLOCK)
-            d_ref[rows, 2 * LANES : 3 * LANES] = turn(dk[source, :] * scale, cosine, sine, -1.0).astype(BF16)
-            d_ref[rows, 3 * LANES :] = dv[source, :].astype(BF16)
-            return unused
-
-        lax.fori_loop(0, tokens // BLOCK, put, 0)
-
-
-def attend_back(order, q, k, v, o, do, lse, tables_in):
-    tokens = q.shape[0]
-    blocks = tokens // BLOCK
-    whole = lambda a: pl.BlockSpec(a.shape, lambda j, *_: (0,) * a.ndim)
-    arrays = (q, k, v, o, do, lse) + tuple(tables_in)
+        for b in range(tokens // BLOCK):
+            to = lanes(order_ref[b] * BLOCK, BLOCK)
+            there = slice(b * BLOCK, (b + 1) * BLOCK)
+            d_ref[2 * HEAD_SIZE : 3 * HEAD_SIZE, to] = turned(
+                dk[there, :].T * scale, table_ref[:half, to], -table_ref[half:, to]
+            ).astype(BF16)
+            d_ref[3 * HEAD_SIZE :, to] = dv[there, :].T.astype(BF16)
+
+
+def attend_back(order, *arrays):
+    tokens = arrays[0].shape[1]
+    out = jax.ShapeDtypeStruct((4 * HEAD_SIZE, tokens), BF16)
+    tall = (tokens, HEAD_SIZE)
     return pl.pallas_call(
         attend_back_kernel,
         grid_spec=pltpu.PrefetchScalarGridSpec(
             num_scalar_prefetch=1,
-            grid=(blocks,),
-            in_specs=[whole(a) for a in arrays],
-            out_specs=pl.BlockSpec((tokens, 4 * LANES), lambda j, *_: (0, 0)),
-            scratch_shapes=[VMEM(k.shape, BF16), VMEM(v.shape, BF16), VMEM(k.shape, F32), VMEM(v.shape, F32)],
+            grid=(tokens // BLOCK,),
+            in_specs=[whole_block(a) for a in arrays],
+            out_specs=whole_block(out),
+            scratch_shapes=[VMEM(tall, BF16), VMEM(tall[::-1], BF16), VMEM(tall, BF16), VMEM(tall, F32), VMEM(tall, F32)],
         ),
-        out_shape=jax.ShapeDtypeStruct((tokens, 4 * LANES), BF16),
+        out_shape=out,
         compiler_params=pltpu.CompilerParams(vmem_limit_bytes=VMEM_BYTES),
         name="attend_back",
     )(order, *arrays)
+
+
+def last_kernel(a_ref, b_ref, gain_ref, a_all, b_all, sum_ref, by_z, part, by_c, send, recv, local, zs, zr, cs, cr):
+    c = lax.axis_index("ctx")
+    z = lax.axis_index("fsdp")
+    depth, _, shard = by_z.shape
+    others = [lax.rem(z + k, depth) for k in range(1, depth)]
+    greet([{"ctx": flip(c, k)} for k in range(1, 8)] + [{"fsdp": o} for o in others])
+    sent = []
+    for k, o in enumerate(others):
+        d = remote(gain_ref.at[:, lanes(o * shard, shard)], by_z.at[z], zs.at[k], zr.at[k], fsdp=o)
+        d.start()
+        sent.append(d)
+    gathers = [
+        Gather(c, own_half(a_ref), a_all, row_half, send.at[0], recv.at[0]),
+        Gather(c, own_half(b_ref, 1), b_all, column_half, send.at[1], recv.at[1]),
+    ]
+    here = [
+        pltpu.make_async_copy(a_ref, a_all.at[c], local.at[0]),
+        pltpu.make_async_copy(b_ref, b_all.at[c], local.at[1]),
+    ]
+    for g in gathers:
+        g.begin()
+    for d in here:
+        d.start()
+    total = gain_ref[:, lanes(z * shard, shard)]
+    for k in range(depth - 1):
+        ref = by_z.at[lax.rem(z + depth - 1 - k, depth)]
+        remote(ref, ref, zs.at[k], zr.at[k], fsdp=others[k]).wait_recv()
+        total = total + by_z[lax.rem(z + depth - 1 - k, depth)]
+    part[...] = total
+    for k in range(1, 8):
+        d = remote(part, by_c.at[c], cs.at[k], cr.at[k], ctx=flip(c, k))
+        d.start()
+        sent.append(d)
+    by_c[c] = total
+    for g in gathers:
+        g.finish()
+    for k in range(1, 8):
+        ref = by_c.at[flip(c, k)]
+        remote(ref, ref, cs.at[k], cr.at[k], ctx=flip(c, k)).wait_recv()
+    total = by_c[0]
+    for k in range(1, 8):
+        total = total + by_c[k]
+    sum_ref[...] = total
+    for d in here:
+        d.wait()
+    for d in sent:
+        d.wait_send()
+    for g in gathers:
+        g.sent()
+
+
+def last_gather(a, b, gains, depth, cid):
+    shard = gains.shape[1] // depth
+    hbm = pl.BlockSpec(memory_space=ANY)
+    vm = pl.BlockSpec(memory_space=VMEM)
+    small = (8, shard)
+    return pl.pallas_call(
+        last_kernel,
+        out_shape=(
+            jax.ShapeDtypeStruct((8,) + a.shape, BF16),
+            jax.ShapeDtypeStruct((8,) + b.shape, BF16),
+            jax.ShapeDtypeStruct(small, F32),
+        ),
+        in_specs=[hbm, hbm, vm],
+        out_specs=(hbm, hbm, vm),
+        scratch_shapes=[
+            VMEM((depth,) + small, F32),
+            VMEM(small, F32),
+            VMEM((8,) + small, F32),
+            DMA((2, 8, 2)),
+            DMA((2, 8, 2)),
+            DMA((2,)),
+            DMA((depth,)),
+            DMA((depth,)),
+            DMA((8,)),
+            DMA((8,)),
+        ],
+        compiler_params=params(cid),
+        name="last_gather",
+    )(a, b, gains)
+
+
+def widen_mlp(gate_up, down):
+    _, shard, both = gate_up.shape
+    mine = both // 2
+    depth = mine // LANES
+    step = shard // 8
+
+    def kernel(a_ref, d_ref, gate_ref, up_ref, down_ref):
+        for i, out in enumerate((gate_ref, up_ref)):
+            for c in range(8):
+                for s in range(depth):
+                    out[:, (s * 8 + c) * LANES : (s * 8 + c + 1) * LANES] = a_ref[
+                        c, :, i * mine + s * LANES : i * mine + (s + 1) * LANES
+                    ].astype(F32)
+        down_ref[...] = d_ref[0].astype(F32)
+
+    _, rows, width = down.shape
+    wide = jax.ShapeDtypeStruct((shard, 8 * mine), F32)
+    wide_spec = pl.BlockSpec((step, 8 * mine), lambda i: (i, 0))
+    return pl.pallas_call(
+        kernel,
+        grid=(8,),
+        out_shape=(wide, wide, jax.ShapeDtypeStruct((8 * rows, width), F32)),
+        in_specs=[pl.BlockSpec((8, step, both), lambda i: (0, i, 0)), pl.BlockSpec((1, rows, width), lambda i: (i, 0, 0))],
+        out_specs=(wide_spec, wide_spec, pl.BlockSpec((rows, width), lambda i: (i, 0))),
+        compiler_params=pltpu.CompilerParams(vmem_limit_bytes=VMEM_BYTES),
+        name="widen_mlp",
+    )(gate_up, down)
+
+
+def widen_attention(qkv, out):
+    shard = qkv.shape[2]
+    width = out.shape[2]
+
+    def kernel(a_ref, o_ref, q_out, k_out, v_out, out_out):
+        per_q = 2 * HEAD_SIZE
+        for c in range(0, 8, 2):
+            both = jnp.concatenate([a_ref[c + i, :per_q, :] for i in (0, 1)], 0)
+            q_out[:, c * per_q : (c + 2) * per_q] = both.astype(F32).T
+        for target, first in ((k_out, per_q), (v_out, per_q + HEAD_SIZE)):
+            for c in range(0, 8, 4):
+                four = jnp.concatenate([a_ref[c + i, first : first + HEAD_SIZE, :] for i in range(4)], 0)
+                target[:, c * HEAD_SIZE : (c + 4) * HEAD_SIZE] = four.astype(F32).T
+        for c in range(8):
+            rows = out.shape[1]
+            out_out[c * rows : (c + 1) * rows, :] = o_ref[c].astype(F32)
+
+    vm = pl.BlockSpec(memory_space=VMEM)
+    shape = lambda n: jax.ShapeDtypeStruct((shard, n), F32)
+    heads = 8 * HEAD_SIZE
+    return pl.pallas_call(
+        kernel,
+        out_shape=(shape(2 * heads), shape(heads), shape(heads), shape(width)),
+        in_specs=[vm, vm],
+        out_specs=(vm, vm, vm, vm),
+        compiler_params=pltpu.CompilerParams(vmem_limit_bytes=VMEM_BYTES),
+        name="widen_attention",
+    )(qkv, out)
 
 
 def in_plane(
@@ -939,42 +1240,12 @@
     w_down,
     out_grad,
 ):
-    c = lax.axis_index("ctx")
     plane = 8
     rows, width = hidden_in.shape[1:]
     tokens = plane * rows
     shard = width // depth
     half = HEAD_SIZE // 2
-    columns = w_gate.shape[1]
-    mine = columns // plane
-    strip = mine // depth
-    deep = w_down.shape[0]
-
-    def share(a, axis):
-        return lax.dynamic_index_in_dim(a, c, axis, keepdims=False)
-
-    def halves(a, heads):
-        a = share(a.reshape(shard, plane, heads, 2, half), 1)
-        a = jnp.pad(a, ((0, 0), (0, 0), (0, 0), (0, LANES // 2 - half)))
-        return a.reshape(shard, heads * LANES)
-
-    value_part = jnp.pad(share(value_projection.reshape(shard, plane, HEAD_SIZE), 1), ((0, 0), (0, LANES - HEAD_SIZE)))
-    qkv_part = jnp.concatenate([halves(w_query, 2), halves(key_projection, 1), value_part], 1)
-
-    def cut(a):
-        return share(a.reshape(shard, depth, plane, strip), 2).reshape(shard, mine)
-
-    out_part = share(w_out.reshape(plane, shard // plane, width), 0)
-    down_part = share(w_down.reshape(plane, deep // plane, width), 0)
-
-    def over_depth(a):
-        return lax.all_gather(a, "fsdp", axis=0, tiled=True)
-
-    qkv_w = over_depth(qkv_part)
-    out_slices = over_depth(out_part)
-    gate_w = over_depth(cut(w_gate))
-    up_w = over_depth(cut(w_up))
-    down_w = over_depth(down_part)
+    mine = w_gate.shape[1] // plane
 
     position = positions[0]
     lane = lax.broadcasted_iota(jnp.int32, (8, LANES), 1)
@@ -986,8 +1257,24 @@
         ],
         0,
     )
+    freq = THETA ** (-(jnp.arange(half, dtype=F32) * 2.0 / HEAD_SIZE))
+    start = freq[:, None] * info[:1].astype(F32)
+    quarter = lane[:1] // (LANES // 4)
+    base = jnp.where(quarter % 2 == 0, jnp.cos(start), jnp.sin(start))
+    inner = freq[:, None] * jnp.arange(BLOCK, dtype=F32)[None]
+    step = jnp.concatenate([jnp.cos(inner), jnp.sin(inner)], 0)
+
     hidden_low = hidden_in[0]
-    normed_all, gains_all, infos = first_gather(hidden_low, gains, info, depth, 0)
+    weights = (w_query, key_projection, value_projection, w_out, w_gate, w_up, w_down)
+    normed_all, qkv, qkv_w, table, gains_all, infos, out_slices, gate_up_part, down_part = first_part(
+        hidden_low, gains, info, base, step, weights, depth, 0
+    )
+
+    def over_depth(a):
+        return lax.all_gather(a, "fsdp", axis=0, tiled=True)
+
+    gate_up_w = over_depth(gate_up_part)
+    down_w = over_depth(down_part)
     gain_one = gains_all[:, 0].reshape(width)
     gain_two = gains_all[:, 4].reshape(width)
     starts = infos[:, 0].reshape(plane, 2, LANES // 2)[:, :, 0].reshape(2 * plane)
@@ -997,102 +1284,67 @@
         jnp.where(ranks[None, :] == jnp.arange(blocks)[:, None], jnp.arange(blocks)[None, :], 0), 1
     ).astype(jnp.int32)
 
-    freq = THETA ** (-(jnp.arange(half, dtype=F32) * 2.0 / HEAD_SIZE))
-    pad = jnp.zeros((LANES // 2 - half,), F32)
-    freq = jnp.concatenate([freq, pad, freq, pad])
-    base = starts.astype(F32)[:, None] * freq[None]
-    inner = jnp.arange(BLOCK, dtype=F32)[:, None] * freq[None]
-    tables_in = (jnp.cos(base), jnp.sin(base), jnp.cos(inner), jnp.sin(inner))
-
     normed_all = normed_all.reshape(tokens, width)
-    q, k, v = project(normed_all, qkv_w, tables_in)
-    attended, attended_low, lse = attend(order, q, k, v)
-
-    out_all = plane_gather(out_slices.reshape(depth * (shard // plane), width), 1)
-    out_w = (
-        out_all.reshape(plane, depth, shard // plane, width).transpose(1, 0, 2, 3).reshape(width, width)
-    )
-    mixed_heads = plane_exchange(attended_low.reshape(plane, rows, 2 * LANES), 2)
-    attended_tok = (
-        mixed_heads.reshape(plane, rows, 2, LANES)[..., :HEAD_SIZE].transpose(1, 0, 2, 3).reshape(rows, width)
-    )
+    attended, attended_low, lse = attend(order, qkv)
+    (out_all,) = plane_gather([out_slices.reshape(depth * (shard // plane), width)], 1)
+    out_w = out_all.reshape(plane, depth, shard // plane, width).transpose(1, 0, 2, 3).reshape(width, width)
+    attended_t = plane_exchange(attended_low, 2).reshape(width, rows)
     hidden = hidden_low.astype(F32)
-    mixed = hidden + jnp.dot(attended_tok, out_w, preferred_element_type=F32)
+    mixed = hidden + dot_first(attended_t, out_w)
     normed_two = norm_forward(mixed, gain_two).astype(BF16)
-    two_all = plane_gather(normed_two, 3).reshape(tokens, width)
     grad_low = out_grad[0]
-    grad_all = plane_gather(grad_low, 4).reshape(tokens, width)
-
-    gate = jnp.dot(two_all, gate_w, preferred_element_type=F32)
-    up = jnp.dot(two_all, up_w, preferred_element_type=F32)
+    two_all, grad_all = plane_gather([normed_two, grad_low], 3)
+    two_all = two_all.reshape(tokens, width)
+    grad_all = grad_all.reshape(tokens, width)
+
+    gate_up = jnp.dot(two_all, gate_up_w, preferred_element_type=F32)
+    gate, up = gate_up[:, :mine], gate_up[:, mine:]
     sigma = jax.nn.sigmoid(gate)
     active = (gate * sigma * up).astype(BF16)
     down_sum = jnp.dot(active, down_w, preferred_element_type=F32).astype(BF16)
     result = mixed + plane_scatter(down_sum.reshape(plane, rows, width), 5)
     layer_out = result.astype(BF16)[None]
 
-    down_grad = dot_first(active, grad_all)
     active_grad = dot_last(grad_all, down_w)
-    gate_grad = (active_grad * up * sigma * (1.0 + gate * (1.0 - sigma))).astype(BF16)
-    up_grad = (active_grad * gate * sigma).astype(BF16)
-    gate_wgrad = dot_first(two_all, gate_grad)
-    up_wgrad = dot_first(two_all, up_grad)
-    two_grad_sum = (dot_last(gate_grad, gate_w) + dot_last(up_grad, up_w)).astype(BF16)
+    gate_grad = active_grad * up * sigma * (1.0 + gate * (1.0 - sigma))
+    up_grad = active_grad * gate * sigma
+    both_grad = jnp.concatenate([gate_grad, up_grad], 1).astype(BF16)
+    two_grad_sum = dot_last(both_grad, gate_up_w).astype(BF16)
+
+    def scatter_depth(a, axis=0):
+        return lax.psum_scatter(a.astype(BF16), "fsdp", scatter_dimension=axis, tiled=True)
+
+    gate_up_shard = scatter_depth(dot_first(two_all, both_grad))
+    down_shard = scatter_depth(dot_first(active, grad_all))
+
     two_grad = plane_scatter(two_grad_sum.reshape(plane, rows, width), 6)
     mixed_part, gain_two_grad = norm_back(mixed, gain_two, two_grad)
     mixed_grad = grad_low.astype(F32) + mixed_part
     branch_grad = mixed_grad.astype(BF16)
 
-    def scatter_depth(a):
-        return lax.psum_scatter(a.astype(BF16), "fsdp", scatter_dimension=0, tiled=True)
-
-    gate_shard = scatter_depth(gate_wgrad)
-    up_shard = scatter_depth(up_wgrad)
-    down_shard = scatter_depth(down_grad)
-
-    attended_grad = dot_last(branch_grad, out_w).astype(BF16)
-    out_wgrad = dot_first(attended_tok, branch_grad).astype(BF16)
-    spread = jnp.pad(
-        attended_grad.reshape(rows, plane, 2, HEAD_SIZE), ((0, 0), (0, 0), (0, 0), (0, LANES - HEAD_SIZE))
-    )
-    spread = spread.transpose(1, 0, 2, 3).reshape(plane, rows, 2 * LANES)
-    do = plane_exchange(spread, 7).reshape(tokens, 2 * LANES)
-    qkv_grad = attend_back(order, q, k, v, attended, do, lse, tables_in)
-    one_grad_sum = dot_last(qkv_grad, qkv_w).astype(BF16)
-    qkv_wgrad = dot_first(normed_all, qkv_grad).astype(BF16)
+    attended_grad = dot_last(out_w, branch_grad).astype(BF16)
+    do = plane_exchange(attended_grad.reshape(plane, 2 * HEAD_SIZE, rows), 7)
+    out_wgrad = jnp.dot(attended_t, branch_grad, preferred_element_type=F32).astype(BF16)
+    out_rows = out_wgrad.reshape(depth, plane, shard // plane, width).transpose(1, 0, 2, 3)
+    out_sum = plane_scatter(out_rows.reshape(plane, shard // plane * depth, width), 9)
+    out_shard = scatter_depth(out_sum)
+
+    qkv_grad = attend_back(order, qkv, attended, do, lse, table)
+    one_grad_sum = dot_first(qkv_grad, qkv_w).astype(BF16)
+    qkv_wgrad = jnp.dot(qkv_grad, normed_all, preferred_element_type=F32).astype(BF16)
+    qkv_wgrad = qkv_wgrad.reshape(4 * HEAD_SIZE, depth, shard).transpose(1, 0, 2).reshape(-1, shard)
     qkv_shard = scatter_depth(qkv_wgrad)
+    gate_up_all, down_all = plane_gather([gate_up_shard, down_shard], 10)
+    gate_total, up_total, down_total = widen_mlp(gate_up_all, down_all)
     one_grad = plane_scatter(one_grad_sum.reshape(plane, rows, width), 8)
     input_part, gain_one_grad = norm_back(hidden, gain_one, one_grad)
     input_grad = (mixed_grad + input_part).astype(BF16)[None]
 
-    out_rows = out_wgrad.reshape(depth, plane, shard // plane, width).transpose(1, 0, 2, 3)
-    out_sum = plane_scatter(out_rows.reshape(plane, shard // plane * depth, width), 9)
-    out_shard = scatter_depth(out_sum)
-
-    joined = jnp.concatenate([gate_shard, up_shard, down_shard.reshape(-1, mine)], 0)
-    joined = plane_gather(joined, 10).astype(F32)
-    def columns_of(a):
-        return a.reshape(plane, shard, depth, strip).transpose(1, 2, 0, 3).reshape(shard, columns)
-
-    gate_total = columns_of(joined[:, :shard])
-    up_total = columns_of(joined[:, shard : 2 * shard])
-    down_total = joined[:, 2 * shard :].reshape(deep, width)
-
-    tail = jnp.concatenate([qkv_shard, out_shard.reshape(-1, 4 * LANES)], 0)
-    tail = plane_gather(tail, 11).astype(F32)
-    out_total = tail[:, shard:].reshape(shard, width)
-    heads = tail[:, :shard].reshape(plane, shard, 4, LANES)
-
-    def unhalve(a, n):
-        a = a.reshape(plane, shard, n, 2, LANES // 2)[..., :half]
-        return a.transpose(1, 0, 2, 3, 4).reshape(shard, plane * n * HEAD_SIZE)
-
-    query_total = unhalve(heads[:, :, :2], 2)
-    key_total = unhalve(heads[:, :, 2:3], 1)
-    value_total = heads[:, :, 3, :HEAD_SIZE].transpose(1, 0, 2).reshape(shard, plane * HEAD_SIZE)
-
-    gain_sums = lax.psum(jnp.stack([gain_one_grad, gain_two_grad]), ("ctx", "fsdp"))
-    gain_sums = lax.dynamic_slice_in_dim(gain_sums, lax.axis_index("fsdp") * shard, shard, 1)
+    gain_rows = jnp.concatenate(
+        [jnp.broadcast_to(gain_one_grad[None], (4, width)), jnp.broadcast_to(gain_two_grad[None], (4, width))], 0
+    )
+    qkv_all, out_grads, gain_sums = last_gather(qkv_shard, out_shard, gain_rows, depth, 11)
+    query_total, key_total, value_total, out_total = widen_attention(qkv_all, out_grads)
     return (
         layer_out,
         input_grad,
@@ -1101,7 +1353,7 @@
         key_total,
         value_total,
         out_total,
-        gain_sums[1],
+        gain_sums[4],
         gate_total,
         up_total,
         down_total,

time: 795 us -> 599 us (0.75)
  local copies, waits for them, and re-layouts: 161 us -> 15.2 us
  blocking collectives: 68 us -> 0 us
  waiting for transfers between devices: 0.24 us -> 26.6 us
  matrix products: 97.4 us -> 82.9 us
  Pallas kernels: 422 us -> 435 us
    reshape x12 -> x1, local copies, waits for them, and re-layouts: 61.7 us -> 1.13 us  [in_plane(): qkv_wgrad.reshape(4 * HEAD_SIZE, depth, shard).transpose(1, 0, 2)]
    psum x1 -> x0, blocking collectives: 41.8 us -> none  [in_plane(): lax.psum(jnp.stack([gain_one_grad, gain_two_grad]), ('ctx', 'fsdp'))]
    unnamed x44 -> x19, local copies, waits for them, and re-layouts: 32.7 us -> 0.17 us
    pallas_call x7, Pallas kernels: 202 us -> 229 us  [the longest x3 134 us: plane_gather(): pl.pallas_call(kernel, out_shape=[jax.ShapeDtypeStruct((8,) + a.shape, a....]
    slice x11 -> x1, local copies, waits for them, and re-layouts: 28.5 us -> 1.38 us  [in_plane(): gain_sums[4]]
    all_gather x1 -> x0, blocking collectives: 26.2 us -> none  [over_depth(): return lax.all_gather(a, 'fsdp', axis=0, tiled=True)]
    reduce_scatter x5 -> x4, waiting for transfers between devices: 0.06 us -> 25.8 us  [scatter_depth(): lax.psum_scatter(a.astype(BF16), 'fsdp', scatter_dimension=axis, tiled=True)]
    transpose x2 -> x0, local copies, waits for them, and re-layouts: 18.1 us -> none  [columns_of(): a.reshape(plane, shard, depth, strip).transpose(1, 2, 0, 3)]
  transfers between devices with their start and end apart: 9 -> 6, of which waited for: 0 -> 1; matrix products, arithmetic and copies ran while one was open for 17% -> 12% of each run, Pallas kernels for 36% -> 38%
where the time goes in v2:
time: 599 us; the launch traced here: 594 us
  Pallas kernels  435 us (73%)
  matrix products  82.9 us (14%)
  waiting for transfers between devices  26.6 us (4%)
  other arithmetic  18.5 us (3%)
  local copies, waits for them, and re-layouts  15.2 us (3%)
  between operations  14.6 us (2%)
    pallas_call x3, Pallas kernels, plane_gather(): pl.pallas_call(kernel, out_shape=[jax.ShapeDtypeStruct((8,) + a.shape, a....  134 us
    pallas_call x4, Pallas kernels, plane_scatter(): pl.pallas_call(scatter_kernel, out_shape=jax.ShapeDtypeStruct((rows, widt...  133 us
    pallas_call x1, Pallas kernels, first_part(): pl.pallas_call(first_kernel, out_shape=(shape((8, rows, width), BF16), sh...  52.3 us
    dot_general x4, matrix products, dot_first(): lax.dot_general(left, right, (((0,), (0,)), ((), ())), preferred_element_...  31 us
    pallas_call x1, Pallas kernels, last_gather(): pl.pallas_call(last_kernel, out_shape=(jax.ShapeDtypeStruct((8,) + a.shap...  26.4 us
    dot_general x3, matrix products, dot_last(): lax.dot_general(left, right, (((1,), (1,)), ((), ())), preferred_element_...  25.8 us
    reduce_scatter x4, waiting for transfers between devices, scatter_depth(): lax.psum_scatter(a.astype(BF16), 'fsdp', scatter_dimension=axis, tiled=True)  25.8 us
    pallas_call x1, Pallas kernels, attend(): pl.pallas_call(attend_kernel, grid_spec=pltpu.PrefetchScalarGridSpec(num_...  24.8 us
  transfers between devices with their start and end apart: 6, of which 1 were waited for; matrix products, arithmetic and copies ran while one was open for 12% of the time, Pallas kernels for 38%

profile of v2, /device:TPU:0, one launch (start us, length us, event | category | flops | bytes accessed | tf_op | source)
XLA Modules:
  0.0 593.7 jit_solution(9906425757498079951)
XLA Ops:
  7.2 0.0 all-gather.3.cloned.1.call-start
  7.2 1.2 fusion.22
  8.4 0.7 broadcast_in_dim.41
  9.1 0.7 broadcast_in_dim.40
  9.8 0.6 pad_maximum_fusion.5.gain_ref
  10.4 1.3 fusion.21
  11.7 0.9 fusion.16
  12.6 0.6 pad_maximum_fusion.3.step_ref
  13.2 0.6 iota.32.info_ref
  13.8 52.3 %first_part.1 = (bf16[8,256,1536]{2,1,0:T(8,128)(2,1)}, bf16[384,2048]{1,0:T(8,128)(2,1)}, bf16[384,1536]{1,0:T(8,128)(2,1)}, f32[96,2048]{1,0:T(8,128)}, f32[4,...) custom-call(bf16[256,1536]{1,0:T(8,128)(2,1)} %bitcast.61, ...), custom_call_target="tpu_custom_call" | custom-call | tf_op jit(solution)/shard_map/first_part/pallas_call | solution.py:881
  66.1 0.0 all-gather.3.cloned.1.call-update
  66.2 0.0 all-gather.5.cloned.1.call-start
  66.2 0.7 all-gather.5.cloned.1.call-update
  66.9 0.2 reduce-scatter.7.cloned.1.call-start
  67.1 0.8 slice_reduce_fusion.2
  67.9 0.1 reshape_squeeze.4
  68.0 0.6 slice_reduce_fusion.5
  68.6 0.1 copy.34
  68.8 0.6 broadcast_subtract_fusion
  69.4 0.1 sub.35
  69.5 0.6 select_reduce_fusion.order_ref
  70.1 24.8 %attend.1 = (f32[192,2048]{1,0:T(8,128)}, bf16[8,192,256]{2,1,0:T(8,128)(2,1)}, f32[16,1,256]{2,1,0:T(1,128)}) custom-call(s32[16]{0:T(128)} %select_reduce_fusion.order_ref, bf16[384,2048]{1,0:T(8,128)(2,1)} %get-tuple-element.38.qkv_ref), custom_call_target="tpu_custom_call" | custom-call | tf_op jit(solution)/shard_map/attend/pallas_call | solution.py:992
  94.9 12.8 %plane_exchange.2 = bf16[8,192,256]{2,1,0:T(8,128)(2,1)} custom-call(bf16[8,192,256]{2,1,0:T(8,128)(2,1)} %get-tuple-element.39.x_ref), custom_call_target="tpu_custom_call" | custom-call | tf_op jit(solution)/shard_map/plane_exchange/pallas_call | solution.py:605
  107.8 24.4 %plane_gather.3 = bf16[8,192,1536]{2,1,0:T(8,128)(2,1)} custom-call(bf16[192,1536]{1,0:T(8,128)(2,1)} %bitcast.73), custom_call_target="tpu_custom_call" | custom-call | tf_op jit(solution)/shard_map/plane_gather/pallas_call | solution.py:574
  132.3 5.0 copy.31
  137.3 0.9 slice_reduce_fusion
  138.2 3.8 multiply_reduce_fusion.2
  142.1 1.1 multiply_convert_fusion.3.refs_0_
  143.2 61.7 %plane_gather.4 = (bf16[8,256,1536]{2,1,0:T(8,128)(2,1)}, bf16[8,256,1536]{2,1,0:T(8,128)(2,1)}) custom-call(bf16[256,1536]{1,0:T(8,128)(2,1)} %multiply_convert_fusion.3.refs_0_, bf16[256,1536]{1,0:T(8,128)(2,1)} %bitcast.70), custom_call_target="tpu_custom_call" | custom-call | tf_op jit(solution)/shard_map/plane_gather/pallas_call | solution.py:574
  204.8 0.0 all-gather.3.cloned.1.call-done
  204.9 11.8 %fusion.23 = f32[2048,1024]{0,1:T(8,128)} fusion(bf16[2048,1536]{1,0:T(8,128)(2,1)} %bitcast.75, bf16[1536,1024]{1,0:T(8,128)(2,1)} %all-gather.3.cloned.1.call-done), kind=kOutput, calls=%fused_computation.80 | convolution fusion | flops 6442450944 | bytes 17825792 | tf_op jit(solution)/shard_map/dot_general | solution.py:1300
  216.6 11.9 %multiply_convert_fusion.1 = (bf16[2048,512]{0,1:T(8,128)(2,1)S(1)}, bf16[2048,512]{0,1:T(8,128)(2,1)S(1)}, bf16[2048,512]{0,1:T(8,128)(2,1)}) fusion(f32[2048,1024]{0,1:T(8,128)} %fusion.23, bf16[2048,1536]{1,0:T(8,128)(2,1)} %bitcast.77, bf16[512,1536]{1,0:T(8,128)(2,1)} %all-gather.5.cloned.1.call-done), kind=kOutput, calls=%fused_computation.6 | convolution fusion | flops 3238002688 | bytes 22544384 | tf_op jit(solution)/shard_map/dot_general | solution.py:70
  228.5 9.3 %convolution_convert_fusion.2 = bf16[2048,1536]{1,0:T(8,128)(2,1)} fusion(bf16[1536,1024]{1,0:T(8,128)(2,1)S(1)} %copy-done.5, bf16[2048,512]{0,1:T(8,128)(2,1)S(1)} %get-tuple-element.74, bf16[2048,512]{0,1:T(8,128)(2,1)S(1)} %get-tuple-element.73), kind=kOutput, calls=%fused_computation.2 | convolution fusion | flops 6453985280 | bytes 13631488 | tf_op jit(solution)/shard_map/dot_general | solution.py:70
  237.8 35.1 %plane_scatter.5 = f32[256,1536]{1,0:T(8,128)} custom-call(bf16[8,256,1536]{2,1,0:T(8,128)(2,1)} %bitcast.67), custom_call_target="tpu_custom_call" | custom-call | tf_op jit(solution)/shard_map/plane_scatter/pallas_call | solution.py:698
  272.9 1.9 multiply_reduce_fusion
  274.9 7.0 %convolution_convert_fusion.3 = bf16[2048,1536]{1,0:T(8,128)(2,1)} fusion(bf16[2048,512]{0,1:T(8,128)(2,1)} %get-tuple-element.75, bf16[512,1536]{1,0:T(8,128)(2,1)S(1)} %copy-done.6), kind=kOutput, calls=%fused_computation.3 | convolution fusion | flops 3224371200 | bytes 9961472 | tf_op jit(solution)/shard_map/dot_general | solution.py:1304
  281.9 34.7 %plane_scatter.4 = f32[256,1536]{1,0:T(8,128)} custom-call(bf16[8,256,1536]{2,1,0:T(8,128)(2,1)} %bitcast.68), custom_call_target="tpu_custom_call" | custom-call | tf_op jit(solution)/shard_map/plane_scatter/pallas_call | solution.py:698
  316.6 3.6 subtract_add_fusion
  320.2 1.4 convolution_convert_fusion
  321.6 2.5 copy.33
  324.1 27.9 %plane_scatter.7 = f32[192,1536]{1,0:T(8,128)} custom-call(bf16[8,192,1536]{2,1,0:T(8,128)(2,1)} %bitcast.63), custom_call_target="tpu_custom_call" | custom-call | tf_op jit(solution)/shard_map/plane_scatter/pallas_call | solution.py:698
  351.9 2.3 convert_element_type.77
  354.2 0.2 reduce-scatter.5.cloned.1.call-start
  354.5 4.6 convolution_convert_fusion.7
  359.1 11.8 %plane_exchange.3.do_ref = bf16[8,192,256]{2,1,0:T(8,128)(2,1)} custom-call(bf16[8,192,256]{2,1,0:T(8,128)(2,1)} %bitcast.72), custom_call_target="tpu_custom_call" | custom-call | tf_op jit(solution)/shard_map/plane_exchange/pallas_call | solution.py:605
  370.9 24.2 %attend_back.1 = bf16[384,2048]{1,0:T(8,128)(2,1)} custom-call(s32[16]{0:T(128)} %select_reduce_fusion.order_ref, bf16[384,2048]{1,0:T(8,128)(2,1)} %get-tuple-element.38.qkv_ref, f32[192,2048]{1,0:T(8,128)} %get-tuple-element.46.o_ref, bf16[8,192,256]{2,1,0:T(8,128)(2,1)} %plane_exchange.3.do_ref, f32[16,1,256]{2,1,0:T(1,128)} %get-tuple-element.47.lse_ref, ...), custom_call_target="tpu_custom_call" | custom-call | tf_op jit(solution)/shard_map/attend_back/pallas_call | solution.py:1072
  395.1 5.9 convolution_convert_fusion.6
  400.9 1.1 copy.38
  402.1 0.0 reduce-scatter.11.cloned.1.call-start
  402.1 8.0 %convolution_convert_fusion.5 = bf16[512,1536]{1,0:T(8,128)(2,1)} fusion(bf16[2048,512]{0,1:T(8,128)(2,1)} %get-tuple-element.75, bf16[2048,1536]{1,0:T(8,128)(2,1)} %bitcast.78), kind=kOutput, calls=%fused_computation.15 | convolution fusion | flops 3222011904 | bytes 9961472 | tf_op jit(solution)/shard_map/dot_general | solution.py:64
  410.2 0.0 reduce-scatter.9.cloned.1.call-start
  410.2 11.3 %convolution_convert_fusion.4 = bf16[1536,1024]{1,0:T(8,128)(2,1)} fusion(bf16[2048,1536]{1,0:T(8,128)(2,1)} %bitcast.76, bf16[2048,512]{0,1:T(8,128)(2,1)} %copy-done.8, bf16[2048,512]{0,1:T(8,128)(2,1)} %copy-done.7), kind=kOutput, calls=%fused_computation.9 | convolution fusion | flops 6452412416 | bytes 13631488 | tf_op jit(solution)/shard_map/dot_general | solution.py:64
  421.5 0.2 fusion
  421.8 7.9 %convolution_convert_fusion.1 = bf16[2048,1536]{1,0:T(8,128)(2,1)} fusion(bf16[384,2048]{1,0:T(8,128)(2,1)} %attend_back.1, bf16[384,1536]{1,0:T(8,128)(2,1)} %get-tuple-element.49), kind=kOutput, calls=%fused_computation.1 | convolution fusion | flops 2419064832 | bytes 9043968 | tf_op jit(solution)/shard_map/dot_general | solution.py:64
  429.7 35.1 %plane_scatter.6 = f32[256,1536]{1,0:T(8,128)} custom-call(bf16[8,256,1536]{2,1,0:T(8,128)(2,1)} %bitcast.66), custom_call_target="tpu_custom_call" | custom-call | tf_op jit(solution)/shard_map/plane_scatter/pallas_call | solution.py:698
  464.8 2.0 fusion.9
  466.8 0.6 pad_maximum_fusion.4.gain_ref
  467.5 1.5 fusion.11
  468.9 26.4 %last_gather.1 = (bf16[8,384,384]{2,1,0:T(8,128)(2,1)}, bf16[8,48,1536]{2,1,0:T(8,128)(2,1)}, f32[8,384]{1,0:T(8,128)}) custom-call(bf16[384,384]{1,0:T(8,128)(2,1)} %reduce-scatter.5.cloned.1.call-done.a_ref, bf16[48,1536]{1,0:T(8,128)(2,1)} %reduce-scatter.7.cloned.1.call-done.b_ref, f32[8,1536]{1,0:T(8,128)} %pad_maximum_fusion.4.gain_ref), custom_call_target="tpu_custom_call" | custom-call | tf_op jit(solution)/shard_map/last_gather/pallas_call | solution.py:1143
  495.3 5.5 widen_attention.1
  500.9 1.4 slice_reduce_fusion.3
  502.2 25.8 %reduce-scatter.9.cloned.1.call-done.refs_0_ = bf16[384,1024]{1,0:T(8,128)(2,1)} async-done(((bf16[1536,1024]{1,0:T(8,128)(2,1)}), bf16[384,1024]{1,0:T(8,128)(2,1)}) %reduce-scatter.9.cloned.1.call-update) | async-done | bytes 786448 | tf_op jit(solution)/shard_map/reduce_scatter | solution.py:1315
  528.0 47.6 %plane_gather.5 = (bf16[8,384,1024]{2,1,0:T(8,128)(2,1)}, bf16[8,128,1536]{2,1,0:T(8,128)(2,1)}) custom-call(bf16[384,1024]{1,0:T(8,128)(2,1)} %reduce-scatter.9.cloned.1.call-done.refs_0_, bf16[128,1536]{1,0:T(8,128)(2,1)} %reduce-scatter.11.cloned.1.call-done.refs_1_), custom_call_target="tpu_custom_call" | custom-call | tf_op jit(solution)/shard_map/plane_gather/pallas_call | solution.py:574
  575.7 11.0 %widen_mlp.1 = (f32[384,4096]{1,0:T(8,128)}, f32[384,4096]{1,0:T(8,128)}, f32[1024,1536]{1,0:T(8,128)}) custom-call(bf16[8,384,1024]{2,1,0:T(8,128)(2,1)} %get-tuple-element.58.a_ref, bf16[8,128,1536]{2,1,0:T(8,128)(2,1)} %get-tuple-element.59.d_ref), custom_call_target="tpu_custom_call" | custom-call | tf_op jit(solution)/shard_map/widen_mlp/pallas_call | solution.py:1187
  (37 shorter events, 0.2 us)
Async XLA Ops:
  7.2 197.7 %all-gather.3.cloned.1.call-start = ((), (), s32[]{:S(2)}) async-start(), calls=%async_computation.4 | async-start | bytes 3932160 | tf_op jit(solution)/shard_map/all_gather | solution.py:1274
  66.2 150.5 %all-gather.5.cloned.1.call-start = ((), (), s32[]{:S(2)}) async-start(), calls=%async_computation.5 | async-start | bytes 1966080 | tf_op jit(solution)/shard_map/all_gather | solution.py:1274
  66.9 402.0 %reduce-scatter.7.cloned.1.call-start = ((), (), s32[]{:S(2)}) async-start(), calls=%async_computation.7 | async-start | bytes 737280 | tf_op jit(solution)/shard_map/reduce_scatter | solution.py:1315
  132.2 6.0 %copy-start = (bf16[1,256,1536]{2,1,0:T(8,128)(2,1)S(1)}, bf16[1,256,1536]{2,1,0:T(8,128)(2,1)}, u32[]{:S(2)}) copy-start(bf16[1,256,1536]{2,1,0:T(8,128)(2,1)} %param.12) | copy-start | bytes 2359300
  132.2 6.0 %copy-start.1 = (bf16[8,192,256]{2,1,0:T(8,128)(2,1)S(1)}, bf16[8,192,256]{2,1,0:T(8,128)(2,1)}, u32[]{:S(2)}) copy-start(bf16[8,192,256]{2,1,0:T(8,128)(2,1)} %plane_exchange.2) | copy-start | bytes 2359300
  216.6 11.9 %copy-start.5 = (bf16[1536,1024]{1,0:T(8,128)(2,1)S(1)}, bf16[1536,1024]{1,0:T(8,128)(2,1)}, u32[]{:S(2)}) copy-start(bf16[1536,1024]{1,0:T(8,128)(2,1)} %all-gather.3.cloned.1.call-done) | copy-start | bytes 9437188
  228.5 9.3 %copy-start.7 = (bf16[2048,512]{0,1:T(8,128)(2,1)}, bf16[2048,512]{0,1:T(8,128)(2,1)S(1)}, u32[]{:S(2)}) copy-start(bf16[2048,512]{0,1:T(8,128)(2,1)S(1)} %get-tuple-element.73) | copy-start | bytes 6291460
  228.5 9.3 %copy-start.8 = (bf16[2048,512]{0,1:T(8,128)(2,1)}, bf16[2048,512]{0,1:T(8,128)(2,1)S(1)}, u32[]{:S(2)}) copy-start(bf16[2048,512]{0,1:T(8,128)(2,1)S(1)} %get-tuple-element.74) | copy-start | bytes 6291460
  272.9 1.9 copy-start.6
  320.2 1.4 copy-start.2
  351.9 2.5 copy-start.3
  354.2 114.7 %reduce-scatter.5.cloned.1.call-start = ((), (), s32[]{:S(2)}) async-start(), calls=%async_computation.6 | async-start | bytes 1474560 | tf_op jit(solution)/shard_map/reduce_scatter | solution.py:1315
  402.1 100.1 %reduce-scatter.11.cloned.1.call-start = ((), (), s32[]{:S(2)}) async-start(), calls=%async_computation.9 | async-start | bytes 1966080 | tf_op jit(solution)/shard_map/reduce_scatter | solution.py:1315
  410.2 117.8 %reduce-scatter.9.cloned.1.call-start = ((), (), s32[]{:S(2)}) async-start(), calls=%async_computation.8 | async-start | bytes 3932160 | tf_op jit(solution)/shard_map/reduce_scatter | solution.py:1315
  464.8 2.6 copy-start.4
Sparse Core Ops, SparseCore 0:
  66.3 61.8 all-gather.2
  129.8 35.7 all-gather.4
  354.4 19.8 reduce-scatter.6
  402.2 27.5 reduce-scatter.4
  432.0 33.9 reduce-scatter.10
  468.8 59.2 reduce-scatter.8

commit v3 on v2

--- a/solution.py
+++ b/solution.py
@@ -528,9 +528,9 @@
         def _():
             self.copy(1, k, z + 1 + k, z + 1).wait_recv()
 
-    def sent(self):
+    def sent(self, steps):
         z, top = self.z, self.depth - 1
-        for k in range(top):
+        for k in steps:
 
             @pl.when((z >= k) & (z < top))
             def _():
@@ -545,174 +545,6 @@
     return pltpu.CompilerParams(
         collective_id=cid, has_side_effects=True, vmem_limit_bytes=VMEM_BYTES
     )
-
-
-def plane_gather(arrays, cid):
-    n = len(arrays)
-    by_rows = [a.shape[0] % 32 == 0 for a in arrays]
-
-    def kernel(*refs):
-        ins, outs, (send, recv, local) = refs[:n], refs[n : 2 * n], refs[2 * n :]
-        c = lax.axis_index("ctx")
-        greet([{"ctx": flip(c, k)} for k in (1, 2, 4)])
-        here = [pltpu.make_async_copy(ins[i], outs[i].at[c], local.at[i]) for i in range(n)]
-        gathers = []
-        for i in range(n):
-            at, own = (row_half, own_half(ins[i])) if by_rows[i] else (column_half, own_half(ins[i], 1))
-            gathers.append(Gather(c, own, outs[i], at, send.at[i], recv.at[i]))
-        for g in gathers:
-            g.begin()
-        for h in here:
-            h.start()
-        for g in gathers:
-            g.finish()
-        for h in here:
-            h.wait()
-        for g in gathers:
-            g.sent()
-
-    return pl.pallas_call(
-        kernel,
-        out_shape=[jax.ShapeDtypeStruct((8,) + a.shape, a.dtype) for a in arrays],
-        in_specs=[pl.BlockSpec(memory_space=ANY)] * n,
-        out_specs=[pl.BlockSpec(memory_space=ANY)] * n,
-        scratch_shapes=[DMA((n, 8, 2)), DMA((n, 8, 2)), DMA((n,))],
-        compiler_params=params(cid),
-        name="plane_gather",
-    )(*arrays)
-
-
-def plane_exchange(x, cid):
-    def kernel(x_ref, o_ref, send, recv, local):
-        c = lax.axis_index("ctx")
-        greet([{"ctx": flip(c, k)} for k in range(1, 8)])
-        here = pltpu.make_async_copy(x_ref.at[c], o_ref.at[c], local)
-        here.start()
-        sent = []
-        for k in (6, 7, 2, 4, 3, 5, 1):
-            d = remote(
-                x_ref.at[flip(c, k)], o_ref.at[c], send.at[k], recv.at[k], ctx=flip(c, k)
-            )
-            d.start()
-            sent.append(d)
-        here.wait()
-        for k in (6, 7, 2, 4, 3, 5, 1):
-            ref = o_ref.at[flip(c, k)]
-            remote(ref, ref, send.at[k], recv.at[k], ctx=flip(c, k)).wait_recv()
-        for d in sent:
-            d.wait_send()
-
-    return pl.pallas_call(
-        kernel,
-        out_shape=jax.ShapeDtypeStruct(x.shape, x.dtype),
-        in_specs=[pl.BlockSpec(memory_space=ANY)],
-        out_specs=pl.BlockSpec(memory_space=ANY),
-        scratch_shapes=[DMA((8,)), DMA((8,)), DMA],
-        compiler_params=params(cid),
-        name="plane_exchange",
-    )(x)
-
-
-def scatter_kernel(p_ref, o_ref, first, total, last, diagonal, s1, v1, s2, v2):
-    c = lax.axis_index("ctx")
-    greet([{"ctx": flip(c, k)} for k in (1, 2, 4)])
-    rows = p_ref.shape[1]
-    piece = rows // 2
-    pending = []
-
-    def go(d):
-        d.start()
-        pending.append(d)
-
-    def sl(q):
-        return pl.ds(q * piece, piece)
-
-    for j, k in enumerate((6, 2, 4, 0)):
-        for q in (0, 1):
-            go(
-                remote(
-                    p_ref.at[flip(c, 1 ^ k), sl(q)],
-                    first.at[j, sl(q)],
-                    s1.at[j, q],
-                    v1.at[j, q],
-                    ctx=flip(c, 1),
-                )
-            )
-
-    def paired(j, q):
-        ref = first.at[j, sl(q)]
-        remote(ref, ref, s1.at[j, q], v1.at[j, q], ctx=flip(c, 1)).wait_recv()
-
-    def chip(j, k, q):
-        return p_ref[flip(c, k), sl(q)].astype(F32) + first[j, sl(q)].astype(F32)
-
-    def came(channel, ref, q, frm):
-        remote(ref, ref, s2.at[channel, q], v2.at[channel, q], ctx=flip(c, frm)).wait_recv()
-
-    for q, to in ((0, 2), (1, 4)):
-        paired(0, q)
-        total[0, sl(q)] = chip(0, 6, q).astype(BF16)
-        go(
-            remote(
-                total.at[0, sl(q)], diagonal.at[sl(q)], s2.at[2, q], v2.at[2, q], ctx=flip(c, to)
-            )
-        )
-
-    def final(j, k, q, merged):
-        v = chip(j, k, q)
-        if merged:
-            v = v + diagonal[sl(q)].astype(F32)
-        total[j, sl(q)] = v.astype(BF16)
-        go(
-            remote(
-                total.at[j, sl(q)],
-                last.at[j - 1, sl(q)],
-                s2.at[j - 1, q],
-                v2.at[j - 1, q],
-                ctx=flip(c, k),
-            )
-        )
-
-    paired(1, 0)
-    final(1, 2, 0, False)
-    paired(2, 1)
-    final(2, 4, 1, False)
-    paired(2, 0)
-    came(2, diagonal.at[sl(0)], 0, 2)
-    final(2, 4, 0, True)
-    paired(1, 1)
-    came(2, diagonal.at[sl(1)], 1, 4)
-    final(1, 2, 1, True)
-    for q in (0, 1):
-        paired(3, q)
-    for q in (0, 1):
-        came(0, last.at[0, sl(q)], q, 2)
-        came(1, last.at[1, sl(q)], q, 4)
-        o_ref[sl(q)] = chip(3, 0, q) + (last[0, sl(q)].astype(F32) + last[1, sl(q)].astype(F32))
-    for d in pending:
-        d.wait_send()
-
-
-def plane_scatter(p, cid):
-    rows, width = p.shape[1:]
-    return pl.pallas_call(
-        scatter_kernel,
-        out_shape=jax.ShapeDtypeStruct((rows, width), F32),
-        in_specs=[pl.BlockSpec(memory_space=VMEM)],
-        out_specs=pl.BlockSpec(memory_space=VMEM),
-        scratch_shapes=[
-            VMEM((4, rows, width), BF16),
-            VMEM((3, rows, width), BF16),
-            VMEM((2, rows, width), BF16),
-            VMEM((rows, width), BF16),
-            DMA((4, 2)),
-            DMA((4, 2)),
-            DMA((3, 2)),
-            DMA((3, 2)),
-        ],
-        compiler_params=params(cid),
-        name="plane_scatter",
-    )(p)
 
 
 def contract(a, b, dims):
@@ -736,16 +568,18 @@
 
 
 def first_kernel(
-    x_ref, gain_ref, info_ref, base_ref, step_ref, wq_ref, wk_ref, wv_ref, wo_ref, wg_ref, wu_ref, wd_ref,
-    all_ref, qkv_ref, w_ref, table_ref, gains_ref, infos_ref, wo_all, gu_ref, down_ref,
-    xs, bases, gsend, grecv, isend, irecv, bsend, brecv, send, recv, zsend, zrecv, osend, orecv, local, parts,
+    x_ref, gain_ref, info_ref, base_ref, step_ref, wq_ref, wk_ref, wv_ref, wo_ref, wg_ref, wu_ref, wd_ref, grad_ref,
+    all_ref, qkv_ref, w_ref, table_ref, gains_ref, infos_ref, wo_all, gu_all, down_all, grad_all,
+    xs, bases, gsend, grecv, isend, irecv, bsend, brecv, send, recv, zsend, zrecv, osend, orecv,
+    usend, urecv, dsend, drecv, send2, recv2, local, parts,
 ):
     c = lax.axis_index("ctx")
     z = lax.axis_index("fsdp")
     depth = gains_ref.shape[0]
     shard, width = wq_ref.shape
     rows = x_ref.shape[0]
-    strip = gu_ref.shape[1] // 2 // depth
+    strip = gu_all.shape[2] // 2 // depth
+    down_rows = down_all.shape[1]
     others = [lax.rem(z + k, depth) for k in range(1, depth)]
     greet([{"ctx": flip(c, k)} for k in range(1, 8)] + [{"fsdp": o} for o in others])
 
@@ -785,18 +619,20 @@
     out_line = Line(z, depth, lambda d: wo_all.at[d], osend, orecv)
     out_line.step(0)
 
-    copies = [pltpu.make_async_copy(wd_ref.at[pl.ds(c * down_ref.shape[0], down_ref.shape[0])], down_ref, parts.at[1])]
+    first = [pltpu.make_async_copy(wd_ref.at[pl.ds(c * down_rows, down_rows)], down_all.at[z], parts.at[1])]
     for i, weight in enumerate((wg_ref, wu_ref)):
         for s in range(depth):
-            copies.append(
+            first.append(
                 pltpu.make_async_copy(
                     weight.at[:, lanes((s * 8 + c) * strip, strip)],
-                    gu_ref.at[:, pl.ds((i * depth + s) * strip, strip)],
+                    gu_all.at[z, :, pl.ds((i * depth + s) * strip, strip)],
                     parts.at[2 + i * depth + s],
                 )
             )
-    for d in copies:
+    for d in first:
         d.start()
+    copies = [pltpu.make_async_copy(grad_ref, grad_all.at[c], parts.at[2 + 2 * depth])]
+    copies[0].start()
 
     def keep(k):
         d = pltpu.make_async_copy(xs.at[flip(c, k)], all_ref.at[flip(c, k)], local.at[k])
@@ -816,23 +652,23 @@
             start = b * (LANES // 2)
             base_cos = bases[d, :, start : start + 1]
             base_sin = bases[d, :, start + LANES // 4 : start + LANES // 4 + 1]
-            at = lanes(d * rows + b * BLOCK, BLOCK)
-            table_ref[:half, at] = base_cos * step_cos - base_sin * step_sin
-            table_ref[half:, at] = base_sin * step_cos + base_cos * step_sin
+            table_ref[2 * d + b, :half] = base_cos * step_cos - base_sin * step_sin
+            table_ref[2 * d + b, half:] = base_sin * step_cos + base_cos * step_sin
 
     for k in range(8):
         rotary(k)
 
     def project(k):
         d = flip(c, k)
-        at = lanes(d * rows, rows)
         half = HEAD_SIZE // 2
-        cosine, sine = table_ref[:half, at], table_ref[half:, at]
         raw = contract(w_ref[...], xs[d], ((1,), (1,)))
-        for h in range(3):
-            head = slice(h * HEAD_SIZE, (h + 1) * HEAD_SIZE)
-            qkv_ref[head, at] = turned(raw[head], cosine, sine).astype(BF16)
-        qkv_ref[3 * HEAD_SIZE :, at] = raw[3 * HEAD_SIZE :].astype(BF16)
+        for b in (0, 1):
+            cosine, sine = table_ref[2 * d + b, :half], table_ref[2 * d + b, half:]
+            part = raw[:, b * BLOCK : (b + 1) * BLOCK]
+            for h in range(3):
+                head = slice(h * HEAD_SIZE, (h + 1) * HEAD_SIZE)
+                qkv_ref[2 * d + b, head] = turned(part[head], cosine, sine).astype(BF16)
+            qkv_ref[2 * d + b, 3 * HEAD_SIZE :] = part[3 * HEAD_SIZE :].astype(BF16)
 
     line.landed(0)
     line.step(1)
@@ -847,30 +683,51 @@
     out_line.landed(1)
     out_line.step(2)
     line.landed(2)
+    for d in first:
+        d.wait()
+    gu_line = Line(z, depth, lambda d: gu_all.at[d], usend, urecv)
+    down_line = Line(z, depth, lambda d: down_all.at[d], dsend, drecv)
+    gu_line.step(0)
+    down_line.step(0)
+    g2 = Gather(c, own_half(grad_ref), grad_all, row_half, send2, recv2)
+    g2.begin()
     project(0)
     g.far()
     project(2)
     project(4)
-    for channel, k in ((0, 1), (3, 3), (4, 5)):
+    for channel, k in ((0, 1), (3, 3)):
         g.paired(channel, k)
         keep(k)
         project(k)
+    g2.near_half()
+    g.paired(4, 5)
+    keep(5)
+    project(5)
     keep(6)
     project(6)
     g.paired(5, 7)
     keep(7)
     project(7)
+    g2.near_rest()
     out_line.landed(2)
+    gu_line.landed(0)
+    down_line.landed(0)
+    g2.far()
+    for channel, k in ((0, 1), (3, 3), (4, 5), (5, 7)):
+        g2.paired(channel, k)
     for d in copies:
         d.wait()
     for d in sent:
         d.wait_send()
-    line.sent()
-    out_line.sent()
+    line.sent((0, 1, 2))
+    out_line.sent((0, 1, 2))
+    gu_line.sent((0,))
+    down_line.sent((0,))
     g.sent()
-
-
-def first_part(x, gains, info, base, step, weights, depth, cid):
+    g2.sent()
+
+
+def first_part(x, gains, info, base, step, weights, grad, depth, cid):
     rows, width = x.shape
     shard = gains.shape[1]
     columns = weights[4].shape[1]
@@ -882,17 +739,18 @@
         first_kernel,
         out_shape=(
             shape((8, rows, width), BF16),
-            shape((4 * HEAD_SIZE, 8 * rows), BF16),
+            shape((8 * rows // BLOCK, 4 * HEAD_SIZE, BLOCK), BF16),
             shape((4 * HEAD_SIZE, width), BF16),
-            shape((HEAD_SIZE, 8 * rows), F32),
+            shape((8 * rows // BLOCK, HEAD_SIZE, BLOCK), F32),
             shape((depth,) + gains.shape, F32),
             shape((8,) + info.shape, jnp.int32),
             shape((depth, shard // 8, width), BF16),
-            shape((shard, 2 * columns // 8), BF16),
-            shape((down_rows, width), BF16),
+            shape((depth, shard, 2 * columns // 8), BF16),
+            shape((depth, down_rows, width), BF16),
+            shape((8, rows, width), BF16),
         ),
-        in_specs=[vm] * 8 + [hbm] * 4,
-        out_specs=(hbm, vm, vm, vm, vm, vm, hbm, hbm, hbm),
+        in_specs=[vm] * 8 + [hbm] * 5,
+        out_specs=(hbm, vm, vm, vm, vm, vm, hbm, hbm, hbm, hbm),
         scratch_shapes=[
             VMEM((8, rows, width), BF16),
             VMEM((8,) + base.shape, F32),
@@ -904,16 +762,12 @@
             DMA((8,)),
             DMA((8, 2)),
             DMA((8, 2)),
-            DMA((2, depth)),
-            DMA((2, depth)),
-            DMA((2, depth)),
-            DMA((2, depth)),
-            DMA((8,)),
-            DMA((2 + 2 * depth,)),
-        ],
+        ]
+        + [DMA((2, depth))] * 8
+        + [DMA((8, 2)), DMA((8, 2)), DMA((8,)), DMA((3 + 2 * depth,))],
         compiler_params=params(cid),
         name="first_part",
-    )(x, gains, info, base, step, *weights)
+    )(x, gains, info, base, step, *weights, grad)
 
 
 CHUNK = 512
@@ -923,8 +777,8 @@
     return pl.BlockSpec(a.shape, lambda j, *_: (0,) * len(a.shape))
 
 
-def two_heads(ref, at):
-    return jnp.concatenate([ref[:HEAD_SIZE, at], ref[HEAD_SIZE : 2 * HEAD_SIZE, at]], 1)
+def two_heads(ref, block):
+    return jnp.concatenate([ref[block, :HEAD_SIZE], ref[block, HEAD_SIZE : 2 * HEAD_SIZE]], 1)
 
 
 def causal(s, t, j):
@@ -933,181 +787,771 @@
     return jnp.where(key <= query, s, -jnp.inf)
 
 
-def attend_kernel(order_ref, qkv_ref, o_ref, low_ref, lse_ref, keys, values):
-    j = pl.program_id(0)
-    tokens = qkv_ref.shape[1]
+def attend_kernel(
+    order_ref, qkv_ref, ow_ref, gu_in, down_in, o_ref, low_ref, lse_ref, ow_all, gu_all, down_all,
+    keys, values, send, recv, local, usend, urecv, dsend, drecv,
+):
+    c = lax.axis_index("ctx")
+    z = lax.axis_index("fsdp")
+    depth = gu_all.shape[0]
+    others = [lax.rem(z + k, depth) for k in range(1, depth)]
+    greet([{"ctx": flip(c, k)} for k in (1, 2, 4)] + [{"fsdp": o} for o in others])
+    few = depth // 2
+    g = Gather(
+        c,
+        lambda h: ow_ref.at[pl.ds(h * few, few)],
+        ow_all,
+        lambda ref, d, h: ref.at[pl.ds(h * few, few), d],
+        send,
+        recv,
+    )
+    here = pltpu.make_async_copy(ow_ref, ow_all.at[:, c], local)
+    here.start()
+    g.begin()
+    gu_line = Line(z, depth, lambda d: gu_all.at[d], usend, urecv)
+    down_line = Line(z, depth, lambda d: down_all.at[d], dsend, drecv)
+    gu_line.step(1)
+    down_line.step(1)
+
+    blocks = qkv_ref.shape[0]
+    per = CHUNK // BLOCK
     factor = HEAD_SIZE ** (-0.5) * math.log2(math.e)
-
-    @pl.when(j == 0)
-    def _():
-        for b in range(tokens // BLOCK):
-            at = lanes(order_ref[b] * BLOCK, BLOCK)
-            there = slice(b * BLOCK, (b + 1) * BLOCK)
-            keys[there, :] = qkv_ref[2 * HEAD_SIZE : 3 * HEAD_SIZE, at].T
-            values[:, there] = qkv_ref[3 * HEAD_SIZE :, at]
-
-    block = order_ref[j]
-    at = lanes(block * BLOCK, BLOCK)
-    q = two_heads(qkv_ref, at)
-    last = j // (CHUNK // BLOCK)
-
-    def step(t, carry, masked):
-        top, denom, acc = carry
-        s = jnp.dot(keys[pl.ds(pl.multiple_of(t * CHUNK, CHUNK), CHUNK), :], q, preferred_element_type=F32)
-        if masked:
-            s = causal(s, t, j)
-        new_top = jnp.maximum(top, jnp.max(s, 0, keepdims=True))
-        p = jnp.exp2((s - new_top) * factor)
-        shrink = jnp.exp2((top - new_top) * factor)
-        denom = denom * shrink + jnp.sum(p, 0, keepdims=True)
-        acc = acc * shrink + jnp.dot(values[:, lanes(t * CHUNK, CHUNK)], p.astype(BF16), preferred_element_type=F32)
-        return new_top, denom, acc
-
-    carry = (
-        jnp.full((1, 2 * BLOCK), -1e30, F32),
-        jnp.zeros((1, 2 * BLOCK), F32),
-        jnp.zeros((HEAD_SIZE, 2 * BLOCK), F32),
-    )
-    carry = lax.fori_loop(0, last, lambda t, state: step(t, state, False), carry)
-    top, denom, acc = step(last, carry, True)
-    out = acc / denom
-    lse_ref[pl.ds(j, 1), :, :] = (top * factor + jnp.log2(denom)).reshape(1, 1, 2 * BLOCK)
-    device = block // 2
-    within = lanes((block - 2 * device) * BLOCK, BLOCK)
-    for h in (0, 1):
-        head = slice(h * HEAD_SIZE, (h + 1) * HEAD_SIZE)
-        part = out[:, h * BLOCK : (h + 1) * BLOCK]
-        o_ref[head, at] = part
-        low_ref[device, head, within] = part.astype(BF16)
-
-
-def attend(order, qkv):
-    tokens = qkv.shape[1]
-    blocks = tokens // BLOCK
+    for b in range(blocks):
+        there = slice(b * BLOCK, (b + 1) * BLOCK)
+        keys[there, :] = qkv_ref[order_ref[b], 2 * HEAD_SIZE : 3 * HEAD_SIZE].T
+        values[:, there] = qkv_ref[order_ref[b], 3 * HEAD_SIZE :]
+
+    def attend_block(j, last):
+        q = two_heads(qkv_ref, order_ref[j])
+
+        def step(t, carry, masked):
+            top, denom, acc = carry
+            s = jnp.dot(keys[pl.ds(t * CHUNK, CHUNK), :], q, preferred_element_type=F32)
+            if masked:
+                s = causal(s, t, j)
+            new_top = jnp.maximum(top, jnp.max(s, 0, keepdims=True))
+            p = jnp.exp2((s - new_top) * factor)
+            shrink = jnp.exp2((top - new_top) * factor)
+            denom = denom * shrink + jnp.sum(p, 0, keepdims=True)
+            acc = acc * shrink + jnp.dot(
+                values[:, pl.ds(t * CHUNK, CHUNK)], p.astype(BF16), preferred_element_type=F32
+            )
+            return new_top, denom, acc
+
+        carry = (
+            jnp.full((1, 2 * BLOCK), -1e30, F32),
+            jnp.zeros((1, 2 * BLOCK), F32),
+            jnp.zeros((HEAD_SIZE, 2 * BLOCK), F32),
+        )
+        for t in range(last):
+            carry = step(t, carry, False)
+        top, denom, acc = step(last, carry, True)
+        out = acc / denom
+        lse_ref[pl.ds(j, 1), :, :] = (top * factor + jnp.log2(denom)).reshape(1, 1, 2 * BLOCK)
+        for h in (0, 1):
+            head = slice(h * HEAD_SIZE, (h + 1) * HEAD_SIZE)
+            part = out[:, h * BLOCK : (h + 1) * BLOCK]
+            o_ref[j, head] = part
+            low_ref[j, head] = part.astype(BF16)
+
+    turns = blocks // per
+    for turn in range(turns):
+
+        @pl.loop(turn * per, (turn + 1) * per)
+        def _(j):
+            attend_block(j, turn)
+
+        if turn == 1:
+            g.near_half()
+        if turn == 2:
+            g.near_rest()
+    g.far()
+    for channel, k in ((0, 1), (3, 3), (4, 5), (5, 7)):
+        g.paired(channel, k)
+    here.wait()
+    gu_line.landed(1)
+    down_line.landed(1)
+    g.sent()
+    gu_line.sent((1,))
+    down_line.sent((1,))
+
+
+def attend(order, qkv, out_part, gate_up, down, cid):
+    blocks = qkv.shape[0]
+    tokens = blocks * BLOCK
+    depth, some, width = out_part.shape
     outs = (
-        jax.ShapeDtypeStruct((2 * HEAD_SIZE, tokens), F32),
-        jax.ShapeDtypeStruct((8, 2 * HEAD_SIZE, tokens // 8), BF16),
+        jax.ShapeDtypeStruct((blocks, 2 * HEAD_SIZE, BLOCK), F32),
+        jax.ShapeDtypeStruct((blocks, 2 * HEAD_SIZE, BLOCK), BF16),
         jax.ShapeDtypeStruct((blocks, 1, 2 * BLOCK), F32),
-    )
+        jax.ShapeDtypeStruct((depth, 8, some, width), BF16),
+        jax.ShapeDtypeStruct(gate_up.shape, BF16),
+        jax.ShapeDtypeStruct(down.shape, BF16),
+    )
+    vm = pl.BlockSpec(memory_space=VMEM)
+    hbm = pl.BlockSpec(memory_space=ANY)
     return pl.pallas_call(
         attend_kernel,
-        grid_spec=pltpu.PrefetchScalarGridSpec(
-            num_scalar_prefetch=1,
-            grid=(blocks,),
-            in_specs=[whole_block(qkv)],
-            out_specs=[whole_block(a) for a in outs],
-            scratch_shapes=[VMEM((tokens, HEAD_SIZE), BF16), VMEM((HEAD_SIZE, tokens), BF16)],
+        out_shape=outs,
+        in_specs=[pl.BlockSpec(memory_space=pltpu.SMEM), vm, hbm, hbm, hbm],
+        out_specs=(vm, vm, vm, hbm, hbm, hbm),
+        scratch_shapes=[VMEM((tokens, HEAD_SIZE), BF16), VMEM((HEAD_SIZE, tokens), BF16), DMA((8, 2)), DMA((8, 2)), DMA]
+        + [DMA((2, depth))] * 4,
+        input_output_aliases={3: 4, 4: 5},
+        compiler_params=params(cid),
+        name="attend",
+    )(order, qkv, out_part, gate_up, down)
+
+
+class Scatter:
+    ORDER = (6, 2, 4, 0)
+
+    def __init__(self, c, p, first, last, diagonal, s1, v1, s2, v2):
+        self.c, self.p, self.first = c, p, first
+        self.last, self.diagonal = last, diagonal
+        self.s1, self.v1, self.s2, self.v2 = s1, v1, s2, v2
+        self.half = p.shape[1] // 2
+        self.pending = []
+
+    @staticmethod
+    def scratch(rows, width):
+        return [
+            VMEM((4, rows, width), BF16),
+            VMEM((2, rows, width), BF16),
+            VMEM((rows, width), BF16),
+            DMA((4, 2)),
+            DMA((4, 2)),
+            DMA((3, 2)),
+            DMA((3, 2)),
+        ]
+
+    def sl(self, q):
+        return pl.ds(q * self.half, self.half)
+
+    def go(self, d):
+        d.start()
+        self.pending.append(d)
+
+    def give(self, k):
+        j = self.ORDER.index(k)
+        for q in (0, 1):
+            source = self.p.at[flip(self.c, 1 ^ k), self.sl(q)]
+            there = self.first.at[j, self.sl(q)]
+            self.go(remote(source, there, self.s1.at[j, q], self.v1.at[j, q], ctx=flip(self.c, 1)))
+
+    def paired(self, j, q):
+        ref = self.first.at[j, self.sl(q)]
+        remote(ref, ref, self.s1.at[j, q], self.v1.at[j, q], ctx=flip(self.c, 1)).wait_recv()
+
+    def chip(self, j, q):
+        k = self.ORDER[j]
+        return self.p[flip(self.c, k), self.sl(q)].astype(F32) + self.first[j, self.sl(q)].astype(F32)
+
+    def came(self, channel, ref, q, frm):
+        remote(
+            ref, ref, self.s2.at[channel, q], self.v2.at[channel, q], ctx=flip(self.c, frm)
+        ).wait_recv()
+
+    def far(self):
+        for q, to in ((0, 2), (1, 4)):
+            self.paired(0, q)
+            self.first[0, self.sl(q)] = self.chip(0, q).astype(BF16)
+            self.go(
+                remote(
+                    self.first.at[0, self.sl(q)],
+                    self.diagonal.at[self.sl(q)],
+                    self.s2.at[2, q],
+                    self.v2.at[2, q],
+                    ctx=flip(self.c, to),
+                )
+            )
+
+    def onward(self, j, q, merged):
+        v = self.chip(j, q)
+        if merged:
+            v = v + self.diagonal[self.sl(q)].astype(F32)
+        self.first[j, self.sl(q)] = v.astype(BF16)
+        self.go(
+            remote(
+                self.first.at[j, self.sl(q)],
+                self.last.at[j - 1, self.sl(q)],
+                self.s2.at[j - 1, q],
+                self.v2.at[j - 1, q],
+                ctx=flip(self.c, self.ORDER[j]),
+            )
+        )
+
+    def direct(self):
+        self.paired(1, 0)
+        self.onward(1, 0, False)
+        self.paired(2, 1)
+        self.onward(2, 1, False)
+
+    def merged(self):
+        self.paired(2, 0)
+        self.came(2, self.diagonal.at[self.sl(0)], 0, 2)
+        self.onward(2, 0, True)
+        self.paired(1, 1)
+        self.came(2, self.diagonal.at[self.sl(1)], 1, 4)
+        self.onward(1, 1, True)
+
+    def result(self, q):
+        self.paired(3, q)
+        self.came(0, self.last.at[0, self.sl(q)], q, 2)
+        self.came(1, self.last.at[1, self.sl(q)], q, 4)
+        return self.chip(3, q) + (
+            self.last[0, self.sl(q)].astype(F32) + self.last[1, self.sl(q)].astype(F32)
+        )
+
+    def sent(self):
+        for d in self.pending:
+            d.wait_send()
+
+
+def exchange_start(c, source, target, send, recv):
+    sent = []
+    for k in (6, 7, 2, 4, 3, 5, 1):
+        there = target.at[pl.ds(2 * c, 2)]
+        d = remote(source.at[pl.ds(2 * flip(c, k), 2)], there, send.at[k], recv.at[k], ctx=flip(c, k))
+        d.start()
+        sent.append(d)
+    return sent
+
+
+def exchange_landed(c, target, send, recv):
+    for k in (6, 7, 2, 4, 3, 5, 1):
+        ref = target.at[pl.ds(2 * flip(c, k), 2)]
+        remote(ref, ref, send.at[k], recv.at[k], ctx=flip(c, k)).wait_recv()
+
+
+def both_blocks(ref, i):
+    return jnp.concatenate([ref[2 * i], ref[2 * i + 1]], 1)
+
+
+def middle_kernel(
+    rank_ref, low_ref, x_ref, gains_ref, g_ref, ow_ref, gu_in, down_in,
+    mixed_ref, mgrad_ref, gsum_ref, do_ref, owg_ref, gug_ref, dg_ref, p1_ref, gu_all, down_all,
+    out_w, wgu, wd, grads, two, p2, act, dgu, stage, give, got,
+    first, last, diagonal, s1, v1, s2, v2,
+    esend, erecv, fsend, frecv, send, recv, usend, urecv, dsend, drecv, load, put, wput,
+):
+    c = lax.axis_index("ctx")
+    z = lax.axis_index("fsdp")
+    depth, shard, both = gu_all.shape
+    mine = both // 2
+    rows, width = x_ref.shape
+    rows_of_out = out_w.shape[1]
+    others = [lax.rem(z + k, depth) for k in range(1, depth)]
+    greet([{"ctx": flip(c, k)} for k in range(1, 8)] + [{"fsdp": o} for o in others])
+    gu_line = Line(z, depth, lambda d: gu_all.at[d], usend, urecv)
+    down_line = Line(z, depth, lambda d: down_all.at[d], dsend, drecv)
+    gu_line.step(2)
+    down_line.step(2)
+    loads = [pltpu.make_async_copy(ow_ref, out_w, load.at[0]), pltpu.make_async_copy(g_ref, grads, load.at[1])]
+    for d in loads:
+        d.start()
+
+    for i in range(rank_ref.shape[0]):
+        give[i] = low_ref[rank_ref[i]]
+    sent = exchange_start(c, give, got, esend, erecv)
+    got[pl.ds(2 * c, 2)] = give[pl.ds(2 * c, 2)]
+    loads[0].wait()
+    exchange_landed(c, got, esend, erecv)
+    x = lax.fori_loop(
+        0, 8, lambda i, total: total + contract(both_blocks(got, i), out_w[i], ((0,), (0,))), x_ref[...].astype(F32)
+    )
+    mixed_ref[...] = x
+    gain = jnp.concatenate([gains_ref[k, 4:5, :] for k in range(depth)], 1)
+    factor = lax.rsqrt(jnp.mean(x * x, -1, keepdims=True) + EPS)
+    two[c] = (x * factor * gain).astype(BF16)
+    g = Gather(c, own_half(two.at[c]), two, row_half, send, recv)
+    g.begin()
+    loads[1].wait()
+    gu_line.landed(2)
+    weights = [pltpu.make_async_copy(gu_all, wgu, load.at[2])]
+    weights[0].start()
+    down_line.landed(2)
+    weights.append(pltpu.make_async_copy(down_all, wd, load.at[3]))
+    weights[1].start()
+    for d in weights:
+        d.wait()
+
+    def block(d, slot):
+        up_w = wgu[...].reshape(width, both)
+        down_w = wd[...].reshape(mine, width)
+        gate_up = jnp.dot(two[d], up_w, preferred_element_type=F32)
+        gate, up = gate_up[:, :mine], gate_up[:, mine:]
+        sigma = jax.nn.sigmoid(gate)
+        silu = gate * sigma
+        active = (silu * up).astype(BF16)
+        act[d] = active
+        active_grad = contract(grads[d], down_w, ((1,), (1,)))
+        gate_grad = active_grad * up * sigma * (1.0 + gate * (1.0 - sigma))
+        up_grad = active_grad * silu
+        grad = jnp.concatenate([gate_grad, up_grad], 1).astype(BF16)
+        dgu[d] = grad
+        p2[d] = contract(grad, up_w, ((1,), (1,))).astype(BF16)
+        stage[slot] = jnp.dot(active, down_w, preferred_element_type=F32).astype(BF16)
+        pltpu.make_async_copy(stage.at[slot], p1_ref.at[d], put.at[slot]).start()
+
+    def drain(slot):
+        pltpu.make_async_copy(stage.at[slot], p1_ref.at[c], put.at[slot]).wait()
+
+    def pair(k, again):
+        d = flip(c, k)
+        other = flip(c, 1 ^ k)
+
+        @pl.loop(0, 2)
+        def _(i):
+            if again:
+                drain(i)
+            block(other + i * (d - other), i)
+
+    scatter = Scatter(c, p2, first, last, diagonal, s1, v1, s2, v2)
+    g.paired(0, 1)
+    pair(0, False)
+    scatter.give(0)
+    g.near_half()
+    g.near_rest()
+    g.paired(3, 3)
+    pair(2, True)
+    scatter.give(2)
+    g.far()
+    g.paired(5, 7)
+    pair(6, True)
+    scatter.give(6)
+    g.paired(4, 5)
+    scatter.far()
+    pair(4, True)
+    scatter.give(4)
+    scatter.direct()
+
+    puts = []
+
+    def wide(f):
+        part = lambda i, total: total + contract(
+            two[pl.ds(2 * i, 2), :, f * shard : (f + 1) * shard].reshape(2 * rows, shard),
+            dgu[pl.ds(2 * i, 2)].reshape(2 * rows, both),
+            ((0,), (0,)),
+        )
+        wgu[f] = lax.fori_loop(0, 4, part, jnp.zeros((shard, both), F32)).astype(BF16)
+        puts.append(pltpu.make_async_copy(wgu.at[f], gug_ref.at[f], wput.at[f]))
+        puts[-1].start()
+
+    wide(0)
+    scatter.merged()
+    for f in range(1, depth):
+        wide(f)
+    strip = mine // depth
+    for f in range(0, depth, 2):
+        part = lambda i, total: total + contract(
+            act[pl.ds(2 * i, 2), :, f * strip : (f + 2) * strip].reshape(2 * rows, 2 * strip),
+            grads[pl.ds(2 * i, 2)].reshape(2 * rows, width),
+            ((0,), (0,)),
+        )
+        part = lax.fori_loop(0, 4, part, jnp.zeros((2 * strip, width), F32))
+        wd[f : f + 2] = part.astype(BF16).reshape(2, strip, width)
+    puts.append(pltpu.make_async_copy(wd, dg_ref, wput.at[depth]))
+    puts[-1].start()
+
+    two_grad = jnp.concatenate([scatter.result(0), scatter.result(1)], 0)
+    x = mixed_ref[...]
+    factor = lax.rsqrt(jnp.mean(x * x, -1, keepdims=True) + EPS)
+    scaled = two_grad * gain
+    mixed_grad = (
+        grads[c].astype(F32)
+        + factor * scaled
+        - x * (factor * factor * factor) * jnp.mean(scaled * x, -1, keepdims=True)
+    )
+    gsum_ref[...] = jnp.broadcast_to(jnp.sum(two_grad * x * factor, 0, keepdims=True), gsum_ref.shape)
+    mgrad_ref[...] = mixed_grad
+    branch = mixed_grad.astype(BF16)
+    for d in sent:
+        d.wait_send()
+    for i in range(8):
+        part = contract(out_w[i], branch, ((1,), (1,))).astype(BF16)
+        give[2 * i] = part[:, :BLOCK]
+        give[2 * i + 1] = part[:, BLOCK:]
+    sent = exchange_start(c, give, do_ref, fsend, frecv)
+    do_ref[pl.ds(2 * c, 2)] = give[pl.ds(2 * c, 2)]
+    for d in puts:
+        d.wait()
+    for i in (0, 1):
+        drain(i)
+    few = rows_of_out // depth
+    for i in range(8):
+        part = jnp.dot(both_blocks(got, i), branch, preferred_element_type=F32).astype(BF16)
+        f = i * depth // 8
+        for t in range(depth):
+            out_w[i * depth % 8 + t, f * few : (f + 1) * few] = part[t * few : (t + 1) * few]
+    out_put = pltpu.make_async_copy(out_w, owg_ref, load.at[0])
+    out_put.start()
+    exchange_landed(c, do_ref, fsend, frecv)
+    out_put.wait()
+    for d in sent:
+        d.wait_send()
+    scatter.sent()
+    g.sent()
+    gu_line.sent((2,))
+    down_line.sent((2,))
+
+
+def middle(rank, low, x, gains, grad_all, out_w, gate_up, down, cid):
+    rows, width = x.shape
+    depth, shard, both = gate_up.shape
+    shape = jax.ShapeDtypeStruct
+    vm = pl.BlockSpec(memory_space=VMEM)
+    hbm = pl.BlockSpec(memory_space=ANY)
+    heads = (8 * rows // BLOCK, 2 * HEAD_SIZE, BLOCK)
+    block = (8, rows, width)
+    return pl.pallas_call(
+        middle_kernel,
+        out_shape=(
+            shape((rows, width), F32),
+            shape((rows, width), F32),
+            shape((8, width), F32),
+            shape(heads, BF16),
+            shape(out_w.shape, BF16),
+            shape(gate_up.shape, BF16),
+            shape(down.shape, BF16),
+            shape(block, BF16),
+            shape(gate_up.shape, BF16),
+            shape(down.shape, BF16),
         ),
-        out_shape=outs,
-        compiler_params=pltpu.CompilerParams(vmem_limit_bytes=VMEM_BYTES),
-        name="attend",
-    )(order, qkv)
-
-
-def attend_back_kernel(
-    order_ref, qkv_ref, o_ref, do_ref, lse_ref, table_ref, d_ref, keys, keys_t, values, dk, dv
+        in_specs=[pl.BlockSpec(memory_space=pltpu.SMEM), vm, vm, vm, hbm, hbm, hbm, hbm],
+        out_specs=(vm, vm, vm, vm, hbm, hbm, hbm, hbm, hbm, hbm),
+        scratch_shapes=[
+            VMEM(out_w.shape, BF16),
+            VMEM(gate_up.shape, BF16),
+            VMEM(down.shape, BF16),
+            VMEM(block, BF16),
+            VMEM(block, BF16),
+            VMEM(block, BF16),
+            VMEM((8, rows, both // 2), BF16),
+            VMEM((8, rows, both), BF16),
+            VMEM((2, rows, width), BF16),
+            VMEM(heads, BF16),
+            VMEM(heads, BF16),
+        ]
+        + Scatter.scratch(rows, width)
+        + [DMA((8,))] * 4
+        + [DMA((8, 2))] * 2
+        + [DMA((2, depth))] * 4
+        + [DMA((4,)), DMA((2,)), DMA((depth + 1,))],
+        input_output_aliases={6: 8, 7: 9},
+        compiler_params=params(cid),
+        name="middle",
+    )(rank, low, x, gains, grad_all, out_w, gate_up, down)
+
+
+class LineScatter:
+    def __init__(self, z, own, left, right, total, send, recv):
+        self.z, self.own, self.left, self.right, self.total = z, own, left, right, total
+        self.send, self.recv = send, recv
+        self.top = own.shape[0] - 1
+
+    @staticmethod
+    def scratch(shape):
+        depth = shape[0]
+        hops = (depth - 1,) + tuple(shape[1:])
+        return [VMEM(hops, BF16), VMEM(hops, BF16), VMEM(shape[1:], F32), DMA((2, depth)), DMA((2, depth))]
+
+    def copy(self, way, s, part, to):
+        there = (self.left, self.right)[way].at[s]
+        return remote(self.own.at[part], there, self.send.at[way, s], self.recv.at[way, s], fsdp=to)
+
+    def landed(self, way, s):
+        ref = (self.left, self.right)[way].at[s]
+        remote(ref, ref, self.send.at[way, s], self.recv.at[way, s], fsdp=self.z - 1 + 2 * way).wait_recv()
+
+    def step(self, s):
+        z, top = self.z, self.top
+        for way in (0, 1):
+            place = z if way == 0 else top - z
+            part = top - s + z if way == 0 else s - top + z
+
+            @pl.when((place <= s) & (place < top))
+            def _():
+                if s:
+
+                    @pl.when(place > 0)
+                    def _():
+                        self.landed(way, s - 1)
+                        came = (self.left, self.right)[way][s - 1]
+                        self.own[part] = (self.own[part].astype(F32) + came.astype(F32)).astype(BF16)
+
+                self.copy(way, s, part, z + 1 - 2 * way).start()
+
+    def result(self):
+        self.total[...] = self.own[self.z].astype(F32)
+        for way in (0, 1):
+            place = self.z if way == 0 else self.top - self.z
+
+            @pl.when(place > 0)
+            def _():
+                self.landed(way, self.top - 1)
+                self.total[...] += (self.left, self.right)[way][self.top - 1].astype(F32)
+
+        return self.total[...].astype(BF16)
+
+    def sent(self):
+        z, top = self.z, self.top
+        for s in range(top):
+            for way in (0, 1):
+                place = z if way == 0 else top - z
+                part = top - s + z if way == 0 else s - top + z
+
+                @pl.when((place <= s) & (place < top))
+                def _():
+                    self.copy(way, s, part, z + 1 - 2 * way).wait_send()
+
+
+def back_kernel(
+    order_ref, rank_ref, qkv_ref, o_ref, do_ref, lse_ref, table_ref, w_ref, mixed_ref, all_ref, p1_ref, owg_ref, gug_ref,
+    layer_ref, osum_ref, gsum_ref, p3_ref, qg_ref,
+    keys, keys_t, values, dk, dv, dqn, dqkv, acc, xs, stage, p1, owg, gug, *rest,
 ):
-    j = pl.program_id(0)
-    tokens = qkv_ref.shape[1]
+    first, second, third, (load, xload, put) = rest[:7], rest[7:14], rest[14:19], rest[19:]
+    c = lax.axis_index("ctx")
+    z = lax.axis_index("fsdp")
+    depth, shard = qg_ref.shape[0], qg_ref.shape[2]
+    rows, width = layer_ref.shape
+    others = [lax.rem(z + k, depth) for k in range(1, depth)]
+    greet([{"ctx": flip(c, k)} for k in (1, 2, 4)] + [{"fsdp": o} for o in others])
+    loads = [
+        pltpu.make_async_copy(a, t, load.at[i])
+        for i, (a, t) in enumerate(((gug_ref, gug), (p1_ref, p1), (owg_ref, owg)))
+    ]
+    for d in loads:
+        d.start()
+    line = LineScatter(z, gug, *third)
+    layer = Scatter(c, p1, *first)
+    out = Scatter(c, owg, *second)
+
+    blocks = qkv_ref.shape[0]
+    per = CHUNK // BLOCK
     scale = HEAD_SIZE ** (-0.5)
     factor = scale * math.log2(math.e)
     half = HEAD_SIZE // 2
-
-    @pl.when(j == 0)
-    def _():
-        for b in range(tokens // BLOCK):
-            at = lanes(order_ref[b] * BLOCK, BLOCK)
-            there = slice(b * BLOCK, (b + 1) * BLOCK)
-            key = qkv_ref[2 * HEAD_SIZE : 3 * HEAD_SIZE, at]
-            keys[there, :] = key.T
-            keys_t[:, there] = key
-            values[there, :] = qkv_ref[3 * HEAD_SIZE :, at].T
-        dk[...] = jnp.zeros_like(dk)
-        dv[...] = jnp.zeros_like(dv)
-
-    block = order_ref[j]
-    at = lanes(block * BLOCK, BLOCK)
-    q = two_heads(qkv_ref, at)
-    device = block // 2
-    within = lanes((block - 2 * device) * BLOCK, BLOCK)
-    do = jnp.concatenate([do_ref[device, :HEAD_SIZE, within], do_ref[device, HEAD_SIZE:, within]], 1)
-    delta = jnp.sum(two_heads(o_ref, at) * do.astype(F32), 0, keepdims=True)
-    lse = lse_ref[j]
-    last = j // (CHUNK // BLOCK)
-
-    def step(t, dq, masked):
-        rows = pl.ds(pl.multiple_of(t * CHUNK, CHUNK), CHUNK)
-        s = jnp.dot(keys[rows, :], q, preferred_element_type=F32)
-        if masked:
-            s = causal(s, t, j)
-        p = jnp.exp2(s * factor - lse)
-        dp = jnp.dot(values[rows, :], do, preferred_element_type=F32)
-        ds = (p * (dp - delta)).astype(BF16)
-        dv[rows, :] += contract(p.astype(BF16), do, ((1,), (1,)))
-        dk[rows, :] += contract(ds, q, ((1,), (1,)))
-        return dq + jnp.dot(keys_t[:, lanes(t * CHUNK, CHUNK)], ds, preferred_element_type=F32)
-
-    dq = jnp.zeros((HEAD_SIZE, 2 * BLOCK), F32)
-    dq = lax.fori_loop(0, last, lambda t, state: step(t, state, False), dq)
-    dq = step(last, dq, True) * scale
-    for h in (0, 1):
-        head = slice(h * HEAD_SIZE, (h + 1) * HEAD_SIZE)
-        d_ref[head, at] = turned(dq[:, h * BLOCK : (h + 1) * BLOCK], table_ref[:half, at], -table_ref[half:, at]).astype(BF16)
-
-    @pl.when(j == tokens // BLOCK - 1)
-    def _():
-        for b in range(tokens // BLOCK):
-            to = lanes(order_ref[b] * BLOCK, BLOCK)
-            there = slice(b * BLOCK, (b + 1) * BLOCK)
-            d_ref[2 * HEAD_SIZE : 3 * HEAD_SIZE, to] = turned(
-                dk[there, :].T * scale, table_ref[:half, to], -table_ref[half:, to]
-            ).astype(BF16)
-            d_ref[3 * HEAD_SIZE :, to] = dv[there, :].T.astype(BF16)
-
-
-def attend_back(order, *arrays):
-    tokens = arrays[0].shape[1]
-    out = jax.ShapeDtypeStruct((4 * HEAD_SIZE, tokens), BF16)
+    for b in range(blocks):
+        there = slice(b * BLOCK, (b + 1) * BLOCK)
+        key = qkv_ref[order_ref[b], 2 * HEAD_SIZE : 3 * HEAD_SIZE]
+        keys[there, :] = key.T
+        keys_t[:, there] = key
+        values[there, :] = qkv_ref[order_ref[b], 3 * HEAD_SIZE :].T
+    dk[...] = jnp.zeros_like(dk)
+    dv[...] = jnp.zeros_like(dv)
+    loads[0].wait()
+    line.step(0)
+    loads[1].wait()
+    for k in Scatter.ORDER:
+        layer.give(k)
+    loads[2].wait()
+    for k in Scatter.ORDER:
+        out.give(k)
+
+    def attend_block(j, last):
+        block = order_ref[j]
+        q = two_heads(qkv_ref, block)
+        do = two_heads(do_ref, block)
+        delta = jnp.sum(two_heads(o_ref, j) * do.astype(F32), 0, keepdims=True)
+        lse = lse_ref[j]
+
+        def step(t, dq, masked):
+            there = pl.ds(t * CHUNK, CHUNK)
+            s = jnp.dot(keys[there, :], q, preferred_element_type=F32)
+            if masked:
+                s = causal(s, t, j)
+            p = jnp.exp2(s * factor - lse)
+            dp = jnp.dot(values[there, :], do, preferred_element_type=F32)
+            ds = (p * (dp - delta)).astype(BF16)
+            wide = pl.ds(t * per, per)
+            dv[wide] += contract(p.astype(BF16), do, ((1,), (1,))).reshape(per, BLOCK, HEAD_SIZE)
+            dk[wide] += contract(ds, q, ((1,), (1,))).reshape(per, BLOCK, HEAD_SIZE)
+            return dq + jnp.dot(keys_t[:, there], ds, preferred_element_type=F32)
+
+        dq = jnp.zeros((HEAD_SIZE, 2 * BLOCK), F32)
+        for t in range(last):
+            dq = step(t, dq, False)
+        dq = step(last, dq, True) * scale
+        cosine, sine = table_ref[block, :half], table_ref[block, half:]
+        for h in (0, 1):
+            part = dq[:, h * BLOCK : (h + 1) * BLOCK]
+            dqn[j, h * HEAD_SIZE : (h + 1) * HEAD_SIZE] = turned(part, cosine, -sine).astype(BF16)
+
+    for turn in range(blocks // per):
+
+        @pl.loop(turn * per, (turn + 1) * per)
+        def _(j):
+            attend_block(j, turn)
+
+        if turn == 0:
+            layer.far()
+        if turn == 1:
+            layer.direct()
+        if turn == 2:
+            layer.merged()
+            line.step(1)
+            out.far()
+    for q in (0, 1):
+        at = pl.ds(q * (rows // 2), rows // 2)
+        layer_ref[at] = (mixed_ref[at] + layer.result(q)).astype(BF16)
+    out.direct()
+
+    for i in range(blocks):
+        to = slice(i * BLOCK, (i + 1) * BLOCK)
+        natural = rank_ref[i]
+        dqkv[: 2 * HEAD_SIZE, to] = dqn[natural]
+        dqkv[2 * HEAD_SIZE : 3 * HEAD_SIZE, to] = turned(
+            dk[natural].T * scale, table_ref[i, :half], -table_ref[i, half:]
+        ).astype(BF16)
+        dqkv[3 * HEAD_SIZE :, to] = dv[natural].T.astype(BF16)
+
+    def x_load(d, slot):
+        return pltpu.make_async_copy(all_ref.at[d], xs.at[slot], xload.at[slot])
+
+    def p_put(d, slot):
+        return pltpu.make_async_copy(stage.at[slot], p3_ref.at[d], put.at[slot])
+
+    x_load(0, 0).start()
+    acc[...] = jnp.zeros_like(acc)
+    for d in range(8):
+        slot = d % 2
+        if d + 1 < 8:
+            x_load(d + 1, 1 - slot).start()
+        if d > 1:
+            p_put(d - 2, slot).wait()
+        part = dqkv[:, d * rows : (d + 1) * rows]
+        stage[slot] = contract(part, w_ref[...], ((0,), (0,))).astype(BF16)
+        p_put(d, slot).start()
+        x_load(d, slot).wait()
+        acc[...] += jnp.dot(part, xs[slot], preferred_element_type=F32)
+        if d == 1:
+            out.merged()
+        if d == 3:
+            line.step(2)
+    for f in range(depth):
+        qg_ref[f] = acc[:, f * shard : (f + 1) * shard].astype(BF16)
+    osum = jnp.concatenate([out.result(0), out.result(1)], 0)
+    osum_ref[...] = osum.astype(BF16).reshape(osum_ref.shape)
+    gsum_ref[...] = line.result()
+    for d in (6, 7):
+        p_put(d, d % 2).wait()
+    layer.sent()
+    out.sent()
+    line.sent()
+
+
+def back(order, rank, arrays, big, depth, cid):
+    blocks = arrays[0].shape[0]
+    tokens = blocks * BLOCK
+    rows, width = arrays[-1].shape
+    out_rows = big[2].shape[1]
+    shard, both = big[3].shape[1:]
+    shape = jax.ShapeDtypeStruct
+    vm = pl.BlockSpec(memory_space=VMEM)
+    hbm = pl.BlockSpec(memory_space=ANY)
+    sm = pl.BlockSpec(memory_space=pltpu.SMEM)
     tall = (tokens, HEAD_SIZE)
+    block = (8, rows, width)
     return pl.pallas_call(
-        attend_back_kernel,
-        grid_spec=pltpu.PrefetchScalarGridSpec(
-            num_scalar_prefetch=1,
-            grid=(tokens // BLOCK,),
-            in_specs=[whole_block(a) for a in arrays],
-            out_specs=whole_block(out),
-            scratch_shapes=[VMEM(tall, BF16), VMEM(tall[::-1], BF16), VMEM(tall, BF16), VMEM(tall, F32), VMEM(tall, F32)],
+        back_kernel,
+        out_shape=(
+            shape((rows, width), BF16),
+            shape((depth, out_rows // depth, width), BF16),
+            shape((shard, both), BF16),
+            shape(block, BF16),
+            shape((depth, 4 * HEAD_SIZE, shard), BF16),
         ),
-        out_shape=out,
-        compiler_params=pltpu.CompilerParams(vmem_limit_bytes=VMEM_BYTES),
-        name="attend_back",
-    )(order, *arrays)
-
-
-def last_kernel(a_ref, b_ref, gain_ref, a_all, b_all, sum_ref, by_z, part, by_c, send, recv, local, zs, zr, cs, cr):
+        in_specs=[sm, sm] + [vm] * len(arrays) + [hbm] * len(big),
+        out_specs=(vm, vm, vm, hbm, vm),
+        scratch_shapes=[
+            VMEM(tall, BF16),
+            VMEM(tall[::-1], BF16),
+            VMEM(tall, BF16),
+            VMEM((blocks, BLOCK, HEAD_SIZE), F32),
+            VMEM((blocks, BLOCK, HEAD_SIZE), F32),
+            VMEM((blocks, 2 * HEAD_SIZE, BLOCK), BF16),
+            VMEM((4 * HEAD_SIZE, tokens), BF16),
+            VMEM((4 * HEAD_SIZE, width), F32),
+            VMEM((2, rows, width), BF16),
+            VMEM((2, rows, width), BF16),
+            VMEM(block, BF16),
+            VMEM((8, out_rows, width), BF16),
+            VMEM(big[3].shape, BF16),
+        ]
+        + Scatter.scratch(rows, width)
+        + Scatter.scratch(out_rows, width)
+        + LineScatter.scratch(big[3].shape)
+        + [DMA((3,)), DMA((2,)), DMA((2,))],
+        compiler_params=params(cid),
+        name="back",
+    )(order, rank, *arrays, *big)
+
+
+def last_kernel(
+    x_ref, mgrad_ref, gains_ref, gain_two_ref, p3_ref, gu_ref, dg_ref, qg_ref, og_ref,
+    input_ref, sum_ref, gu_all, down_all, q_all, o_all,
+    p3, down, heads, outs, down_sum, q_sum, o_sum, gain_rows, by_z, part, by_c, *rest,
+):
+    scatter_refs, lines = rest[:7], (rest[7:12], rest[12:17], rest[17:22])
+    send, recv, local, load, zs, zr, cs, cr = rest[22:]
     c = lax.axis_index("ctx")
     z = lax.axis_index("fsdp")
     depth, _, shard = by_z.shape
+    rows, width = x_ref.shape
     others = [lax.rem(z + k, depth) for k in range(1, depth)]
     greet([{"ctx": flip(c, k)} for k in range(1, 8)] + [{"fsdp": o} for o in others])
+    loads = [
+        pltpu.make_async_copy(a, t, load.at[i])
+        for i, (a, t) in enumerate(((dg_ref, down), (qg_ref, heads), (og_ref, outs), (p3_ref, p3)))
+    ]
+    for d in loads:
+        d.start()
+    here = [pltpu.make_async_copy(gu_ref, gu_all.at[c], local.at[0])]
+    here[0].start()
+    gate_up = Gather(c, own_half(gu_ref), gu_all, row_half, send.at[0], recv.at[0])
+    down_line, q_line, o_line = (LineScatter(z, a, *refs) for a, refs in zip((down, heads, outs), lines))
+    loads[0].wait()
+    down_line.step(0)
+    loads[1].wait()
+    q_line.step(0)
+    loads[2].wait()
+    o_line.step(0)
+    loads[3].wait()
+    scatter = Scatter(c, p3, *scatter_refs)
+    for k in Scatter.ORDER:
+        scatter.give(k)
+    scatter.far()
+    gate_up.begin()
+    scatter.direct()
+    down_line.step(1)
+    scatter.merged()
+    q_line.step(1)
+    o_line.step(1)
+
+    gain = jnp.concatenate([gains_ref[k, 0:1, :] for k in range(depth)], 1)
+    one_grad = jnp.concatenate([scatter.result(0), scatter.result(1)], 0)
+    gate_up.near_half()
+    x = x_ref[...].astype(F32)
+    factor = lax.rsqrt(jnp.mean(x * x, -1, keepdims=True) + EPS)
+    scaled = one_grad * gain
+    back = factor * scaled - x * (factor * factor * factor) * jnp.mean(scaled * x, -1, keepdims=True)
+    input_ref[...] = (mgrad_ref[...] + back).astype(BF16)
+    gain_rows[:4] = jnp.broadcast_to(jnp.sum(one_grad * x * factor, 0, keepdims=True), (4, width))
+    gain_rows[4:] = gain_two_ref[4:]
     sent = []
     for k, o in enumerate(others):
-        d = remote(gain_ref.at[:, lanes(o * shard, shard)], by_z.at[z], zs.at[k], zr.at[k], fsdp=o)
+        d = remote(gain_rows.at[:, lanes(o * shard, shard)], by_z.at[z], zs.at[k], zr.at[k], fsdp=o)
         d.start()
         sent.append(d)
-    gathers = [
-        Gather(c, own_half(a_ref), a_all, row_half, send.at[0], recv.at[0]),
-        Gather(c, own_half(b_ref, 1), b_all, column_half, send.at[1], recv.at[1]),
-    ]
-    here = [
-        pltpu.make_async_copy(a_ref, a_all.at[c], local.at[0]),
-        pltpu.make_async_copy(b_ref, b_all.at[c], local.at[1]),
-    ]
-    for g in gathers:
-        g.begin()
-    for d in here:
-        d.start()
-    total = gain_ref[:, lanes(z * shard, shard)]
+    gate_up.near_rest()
+    down_line.step(2)
+    q_line.step(2)
+    o_line.step(2)
+    gate_up.far()
+
+    total = gain_rows[:, lanes(z * shard, shard)]
     for k in range(depth - 1):
         ref = by_z.at[lax.rem(z + depth - 1 - k, depth)]
         remote(ref, ref, zs.at[k], zr.at[k], fsdp=others[k]).wait_recv()
@@ -1118,8 +1562,25 @@
         d.start()
         sent.append(d)
     by_c[c] = total
+
+    gathers = [gate_up]
+    tails = ((down_line, down_sum, down_all), (q_line, q_sum, q_all), (o_line, o_sum, o_all))
+    for i, (line, mine, everyone) in enumerate(tails):
+        mine[...] = line.result()
+        here.append(pltpu.make_async_copy(mine, everyone.at[c], local.at[i + 1]))
+        here[-1].start()
+        at, own = (row_half, own_half(mine)) if mine.shape[0] % 32 == 0 else (column_half, own_half(mine, 1))
+        gathers.append(Gather(c, own, everyone, at, send.at[i + 1], recv.at[i + 1]))
+        gathers[-1].begin()
+    for g in gathers[1:]:
+        g.near_half()
+    for g in gathers[1:]:
+        g.near_rest()
+    for g in gathers[1:]:
+        g.far()
     for g in gathers:
-        g.finish()
+        for channel, k in ((0, 1), (3, 3), (4, 5), (5, 7)):
+            g.paired(channel, k)
     for k in range(1, 8):
         ref = by_c.at[flip(c, k)]
         remote(ref, ref, cs.at[k], cr.at[k], ctx=flip(c, k)).wait_recv()
@@ -1131,39 +1592,37 @@
         d.wait()
     for d in sent:
         d.wait_send()
+    scatter.sent()
+    for line in (down_line, q_line, o_line):
+        line.sent()
     for g in gathers:
         g.sent()
 
 
-def last_gather(a, b, gains, depth, cid):
-    shard = gains.shape[1] // depth
+def last_part(x, mixed_grad, gains, gain_two, p3, gate_up, down, heads, outs, cid):
+    rows, width = x.shape
+    depth, _, shard = gains.shape
+    shape = jax.ShapeDtypeStruct
+    vm = pl.BlockSpec(memory_space=VMEM)
     hbm = pl.BlockSpec(memory_space=ANY)
-    vm = pl.BlockSpec(memory_space=VMEM)
     small = (8, shard)
+    threes = (down, heads, outs)
     return pl.pallas_call(
         last_kernel,
-        out_shape=(
-            jax.ShapeDtypeStruct((8,) + a.shape, BF16),
-            jax.ShapeDtypeStruct((8,) + b.shape, BF16),
-            jax.ShapeDtypeStruct(small, F32),
-        ),
-        in_specs=[hbm, hbm, vm],
-        out_specs=(hbm, hbm, vm),
-        scratch_shapes=[
-            VMEM((depth,) + small, F32),
-            VMEM(small, F32),
-            VMEM((8,) + small, F32),
-            DMA((2, 8, 2)),
-            DMA((2, 8, 2)),
-            DMA((2,)),
-            DMA((depth,)),
-            DMA((depth,)),
-            DMA((8,)),
-            DMA((8,)),
-        ],
+        out_shape=[shape((rows, width), BF16), shape(small, F32), shape((8,) + gate_up.shape, BF16)]
+        + [shape((8,) + a.shape[1:], BF16) for a in threes],
+        in_specs=[vm] * 4 + [hbm] * 5,
+        out_specs=[vm, vm] + [hbm] * 4,
+        scratch_shapes=[VMEM(p3.shape, BF16)]
+        + [VMEM(a.shape, BF16) for a in threes]
+        + [VMEM(a.shape[1:], BF16) for a in threes]
+        + [VMEM((8, width), F32), VMEM((depth,) + small, F32), VMEM(small, F32), VMEM((8,) + small, F32)]
+        + Scatter.scratch(rows, width)
+        + [r for a in threes for r in LineScatter.scratch(a.shape)]
+        + [DMA((4, 8, 2)), DMA((4, 8, 2)), DMA((4,)), DMA((4,)), DMA((depth,)), DMA((depth,)), DMA((8,)), DMA((8,))],
         compiler_params=params(cid),
-        name="last_gather",
-    )(a, b, gains)
+        name="last_part",
+    )(x, mixed_grad, gains, gain_two, p3, gate_up, down, heads, outs)
 
 
 def widen_mlp(gate_up, down):
@@ -1242,10 +1701,8 @@
 ):
     plane = 8
     rows, width = hidden_in.shape[1:]
-    tokens = plane * rows
     shard = width // depth
     half = HEAD_SIZE // 2
-    mine = w_gate.shape[1] // plane
 
     position = positions[0]
     lane = lax.broadcasted_iota(jnp.int32, (8, LANES), 1)
@@ -1266,88 +1723,33 @@
 
     hidden_low = hidden_in[0]
     weights = (w_query, key_projection, value_projection, w_out, w_gate, w_up, w_down)
-    normed_all, qkv, qkv_w, table, gains_all, infos, out_slices, gate_up_part, down_part = first_part(
-        hidden_low, gains, info, base, step, weights, depth, 0
-    )
-
-    def over_depth(a):
-        return lax.all_gather(a, "fsdp", axis=0, tiled=True)
-
-    gate_up_w = over_depth(gate_up_part)
-    down_w = over_depth(down_part)
-    gain_one = gains_all[:, 0].reshape(width)
-    gain_two = gains_all[:, 4].reshape(width)
+    grad_low = out_grad[0]
+    (normed_all, qkv, qkv_w, table, gains_all, infos, out_part, gate_up_w, down_w, grad_all) = first_part(
+        hidden_low, gains, info, base, step, weights, grad_low, depth, 0
+    )
     starts = infos[:, 0].reshape(plane, 2, LANES // 2)[:, :, 0].reshape(2 * plane)
-    ranks = (starts - jnp.min(starts)) // BLOCK
+    rank = ((starts - jnp.min(starts)) // BLOCK).astype(jnp.int32)
     blocks = 2 * plane
     order = jnp.sum(
-        jnp.where(ranks[None, :] == jnp.arange(blocks)[:, None], jnp.arange(blocks)[None, :], 0), 1
+        jnp.where(rank[None, :] == jnp.arange(blocks)[:, None], jnp.arange(blocks)[None, :], 0), 1
     ).astype(jnp.int32)
 
-    normed_all = normed_all.reshape(tokens, width)
-    attended, attended_low, lse = attend(order, qkv)
-    (out_all,) = plane_gather([out_slices.reshape(depth * (shard // plane), width)], 1)
-    out_w = out_all.reshape(plane, depth, shard // plane, width).transpose(1, 0, 2, 3).reshape(width, width)
-    attended_t = plane_exchange(attended_low, 2).reshape(width, rows)
-    hidden = hidden_low.astype(F32)
-    mixed = hidden + dot_first(attended_t, out_w)
-    normed_two = norm_forward(mixed, gain_two).astype(BF16)
-    grad_low = out_grad[0]
-    two_all, grad_all = plane_gather([normed_two, grad_low], 3)
-    two_all = two_all.reshape(tokens, width)
-    grad_all = grad_all.reshape(tokens, width)
-
-    gate_up = jnp.dot(two_all, gate_up_w, preferred_element_type=F32)
-    gate, up = gate_up[:, :mine], gate_up[:, mine:]
-    sigma = jax.nn.sigmoid(gate)
-    active = (gate * sigma * up).astype(BF16)
-    down_sum = jnp.dot(active, down_w, preferred_element_type=F32).astype(BF16)
-    result = mixed + plane_scatter(down_sum.reshape(plane, rows, width), 5)
-    layer_out = result.astype(BF16)[None]
-
-    active_grad = dot_last(grad_all, down_w)
-    gate_grad = active_grad * up * sigma * (1.0 + gate * (1.0 - sigma))
-    up_grad = active_grad * gate * sigma
-    both_grad = jnp.concatenate([gate_grad, up_grad], 1).astype(BF16)
-    two_grad_sum = dot_last(both_grad, gate_up_w).astype(BF16)
-
-    def scatter_depth(a, axis=0):
-        return lax.psum_scatter(a.astype(BF16), "fsdp", scatter_dimension=axis, tiled=True)
-
-    gate_up_shard = scatter_depth(dot_first(two_all, both_grad))
-    down_shard = scatter_depth(dot_first(active, grad_all))
-
-    two_grad = plane_scatter(two_grad_sum.reshape(plane, rows, width), 6)
-    mixed_part, gain_two_grad = norm_back(mixed, gain_two, two_grad)
-    mixed_grad = grad_low.astype(F32) + mixed_part
-    branch_grad = mixed_grad.astype(BF16)
-
-    attended_grad = dot_last(out_w, branch_grad).astype(BF16)
-    do = plane_exchange(attended_grad.reshape(plane, 2 * HEAD_SIZE, rows), 7)
-    out_wgrad = jnp.dot(attended_t, branch_grad, preferred_element_type=F32).astype(BF16)
-    out_rows = out_wgrad.reshape(depth, plane, shard // plane, width).transpose(1, 0, 2, 3)
-    out_sum = plane_scatter(out_rows.reshape(plane, shard // plane * depth, width), 9)
-    out_shard = scatter_depth(out_sum)
-
-    qkv_grad = attend_back(order, qkv, attended, do, lse, table)
-    one_grad_sum = dot_first(qkv_grad, qkv_w).astype(BF16)
-    qkv_wgrad = jnp.dot(qkv_grad, normed_all, preferred_element_type=F32).astype(BF16)
-    qkv_wgrad = qkv_wgrad.reshape(4 * HEAD_SIZE, depth, shard).transpose(1, 0, 2).reshape(-1, shard)
-    qkv_shard = scatter_depth(qkv_wgrad)
-    gate_up_all, down_all = plane_gather([gate_up_shard, down_shard], 10)
+    attended, attended_low, lse, out_w, gate_up_w, down_w = attend(order, qkv, out_part, gate_up_w, down_w, 1)
+    mixed, mixed_grad, gain_two_grad, do, out_wgrad, gate_up_wgrad, down_wgrad, down_sum, _, _ = middle(
+        rank, attended_low, hidden_low, gains_all, grad_all, out_w.reshape(plane, -1, width), gate_up_w, down_w, 2
+    )
+    arrays = (qkv, attended, do, lse, table, qkv_w, mixed)
+    layer_out, out_sum, gate_up_sum, one_sum, qkv_wgrad = back(
+        order, rank, arrays, (normed_all, down_sum, out_wgrad, gate_up_wgrad), depth, 3
+    )
+    input_grad, gain_sums, gate_up_all, down_all, qkv_all, out_grads = last_part(
+        hidden_low, mixed_grad, gains_all, gain_two_grad, one_sum, gate_up_sum, down_wgrad, qkv_wgrad, out_sum, 4
+    )
     gate_total, up_total, down_total = widen_mlp(gate_up_all, down_all)
-    one_grad = plane_scatter(one_grad_sum.reshape(plane, rows, width), 8)
-    input_part, gain_one_grad = norm_back(hidden, gain_one, one_grad)
-    input_grad = (mixed_grad + input_part).astype(BF16)[None]
-
-    gain_rows = jnp.concatenate(
-        [jnp.broadcast_to(gain_one_grad[None], (4, width)), jnp.broadcast_to(gain_two_grad[None], (4, width))], 0
-    )
-    qkv_all, out_grads, gain_sums = last_gather(qkv_shard, out_shard, gain_rows, depth, 11)
     query_total, key_total, value_total, out_total = widen_attention(qkv_all, out_grads)
     return (
-        layer_out,
-        input_grad,
+        layer_out[None],
+        input_grad[None],
         gain_sums[0],
         query_total,
         key_total,

time: 599 us -> 423 us (0.71)
  matrix products: 82.9 us -> 0 us
  Pallas kernels: 435 us -> 404 us
  waiting for transfers between devices: 26.6 us -> 0 us
  between operations: 14.6 us -> 0.96 us
  other arithmetic: 18.5 us -> 5.34 us
  local copies, waits for them, and re-layouts: 15.2 us -> 7.36 us
    dot_general x11 -> x0, matrix products: 82.9 us -> none  [the longest x4 31 us: dot_first(): lax.dot_general(left, right, (((0,), (0,)), ((), ())), preferred_element_...]
    pallas_call x12 -> x4, Pallas kernels: 366 us -> 305 us  [the longest x1 104 us: middle(): pl.pallas_call(middle_kernel, out_shape=(shape((rows, width), F32), shape...]
    pallas_call x1, Pallas kernels: 52.3 us -> 82.6 us  [first_part(): pl.pallas_call(first_kernel, out_shape=(shape((8, rows, width), BF16), sh...]
    reduce_scatter x4 -> x0, waiting for transfers between devices: 25.8 us -> none  [scatter_depth(): lax.psum_scatter(a.astype(BF16), 'fsdp', scatter_dimension=axis, tiled=True)]
    reshape x3 -> x0, local copies, waits for them, and re-layouts: 8.67 us -> none  [the longest x1 5.04 us: in_plane(): out_all.reshape(plane, depth, shard // plane, width).transpose(1, 0, 2, 3)]
  transfers between devices with their start and end apart: 6 -> 0, of which waited for: 1 -> 0; matrix products, arithmetic and copies ran while one was open for 12% -> 0% of each run, Pallas kernels for 38% -> 0%
where the time goes in v3:
time: 423 us; the launch traced here: 418 us
  Pallas kernels  404 us (96%)
  local copies, waits for them, and re-layouts  7.36 us (2%)
  other arithmetic  5.34 us (1%)
    pallas_call x1, Pallas kernels, middle(): pl.pallas_call(middle_kernel, out_shape=(shape((rows, width), F32), shape...  104 us
    pallas_call x1, Pallas kernels, last_part(): pl.pallas_call(last_kernel, out_shape=[shape((rows, width), BF16), shape(...  99.3 us
    pallas_call x1, Pallas kernels, first_part(): pl.pallas_call(first_kernel, out_shape=(shape((8, rows, width), BF16), sh...  82.6 us
    pallas_call x1, Pallas kernels, back(): pl.pallas_call(back_kernel, out_shape=(shape((rows, width), BF16), shape(...  68.8 us
    pallas_call x1, Pallas kernels, attend(): pl.pallas_call(attend_kernel, out_shape=outs, in_specs=[pl.BlockSpec(memo...  32.8 us
    pallas_call x1, Pallas kernels, widen_mlp(): pl.pallas_call(kernel, grid=(8,), out_shape=(wide, wide, jax.ShapeDtypeSt...  11.1 us

profile of v3, /device:TPU:0, one launch (start us, length us, event | category | flops | bytes accessed | tf_op | source)
XLA Modules:
  0.0 417.6 jit_solution(6131789119762236038)
XLA Ops:
  0.7 1.2 fusion.6
  1.9 1.3 fusion.5
  3.2 0.6 iota.32.info_ref
  3.8 0.7 broadcast_in_dim.52
  4.4 0.7 broadcast_in_dim.53
  5.1 0.6 pad_maximum_fusion.1.gain_ref
  5.7 0.9 fusion.2
  6.6 0.6 pad_maximum_fusion.step_ref
  7.2 82.6 %first_part.1 = (bf16[8,256,1536]{2,1,0:T(8,128)(2,1)}, bf16[16,384,128]{2,1,0:T(8,128)(2,1)}, bf16[384,1536]{1,0:T(8,128)(2,1)}, f32[16,96,128]{2,1,0:T(8,128)}...) custom-call(bf16[256,1536]{1,0:T(8,128)(2,1)} %bitcast.9, ...), custom_call_target="tpu_custom_call" | custom-call | tf_op jit(solution)/shard_map/first_part/pallas_call | solution.py:738
  89.9 0.8 slice_reduce_fusion
  90.6 0.1 reshape_squeeze.4
  90.7 0.6 slice_reduce_fusion.3
  91.3 0.1 copy.30
  91.5 0.6 broadcast_subtract_fusion
  92.1 0.1 sub.26
  92.2 0.0 copy-start.2
  92.2 0.6 select_reduce_fusion.order_ref
  92.9 32.8 %attend.1 = (f32[16,192,128]{2,1,0:T(8,128)}, bf16[16,192,128]{2,1,0:T(8,128)(2,1)}, f32[16,1,256]{2,1,0:T(1,128)}, bf16[4,8,48,1536]{3,2,1,0:T(8,128)(2,1)}, bf...) custom-call(s32[16]{0:T(128)} %select_reduce_fusion.order_ref, ...), custom_call_target="tpu_custom_call", output_to_operand_aliasing={{4}: (3, {}), {5}: (4, {})} | custom-call | tf_op jit(solution)/shard_map/attend/pallas_call | solution.py:893
  125.7 0.0 copy-done.2
  125.7 103.8 %middle.1 = (f32[256,1536]{1,0:T(8,128)}, f32[256,1536]{1,0:T(8,128)}, f32[8,1536]{1,0:T(8,128)}, bf16[16,192,128]{2,1,0:T(8,128)(2,1)}, bf16[8,192,1536]{2,1,0:...) custom-call(s32[16]{0:T(128)} %copy-done.2, ...), custom_call_target="tpu_custom_call", output_to_operand_aliasing={{8}: (6, {}), {9}: (7, {})} | custom-call | tf_op jit(solution)/shard_map/middle/pallas_call | solution.py:1207
  229.5 68.8 %back.1 = (bf16[256,1536]{1,0:T(8,128)(2,1)}, bf16[4,48,1536]{2,1,0:T(8,128)(2,1)}, bf16[384,1024]{1,0:T(8,128)(2,1)}, bf16[8,256,1536]{2,1,0:T(8,128)(2,1)}, bf16[4,384,384]{2,1,0:T(8,128)(2,1)}) custom-call(s32[16]{0:T(128)} %select_reduce_fusion.order_ref, s32[16]{0:T(128)} %copy-done.2, bf16[16,384,128]{2,1,0:T(8,128)(2,1)} %get-tuple-element.54.qkv_ref, ...), custom_call_target="tpu_custom_call" | custom-call | tf_op jit(solution)/shard_map/back/pallas_call | solution.py:1457
  298.3 99.3 %last_part.1 = (bf16[256,1536]{1,0:T(8,128)(2,1)}, f32[8,384]{1,0:T(8,128)}, bf16[8,384,1024]{2,1,0:T(8,128)(2,1)}, bf16[8,128,1536]{2,1,0:T(8,128)(2,1)}, bf16[...) custom-call(bf16[256,1536]{1,0:T(8,128)(2,1)} %bitcast.11, f32[256,1536]{1,0:T(8,128)} %get-tuple-element.75.mgrad_ref, ...), custom_call_target="tpu_custom_call" | custom-call | tf_op jit(solution)/shard_map/last_part/pallas_call | solution.py:1610
  397.6 1.4 slice_reduce_fusion.1
  399.0 5.5 %widen_attention.1 = (f32[384,1536]{1,0:T(8,128)}, f32[384,768]{1,0:T(8,128)}, f32[384,768]{1,0:T(8,128)}, f32[384,1536]{1,0:T(8,128)}) custom-call(bf16[8,384,384]{2,1,0:T(8,128)(2,1)} %get-tuple-element.84.a_ref, bf16[8,48,1536]{2,1,0:T(8,128)(2,1)} %get-tuple-element.85.o_ref), custom_call_target="tpu_custom_call" | custom-call | tf_op jit(solution)/shard_map/widen_attention/pallas_call | solution.py:1677
  404.5 0.0 copy-start
  404.5 0.0 copy-start.1
  404.5 11.1 %widen_mlp.1 = (f32[384,4096]{1,0:T(8,128)}, f32[384,4096]{1,0:T(8,128)}, f32[1024,1536]{1,0:T(8,128)}) custom-call(bf16[8,384,1024]{2,1,0:T(8,128)(2,1)} %get-tuple-element.90.a_ref, bf16[8,128,1536]{2,1,0:T(8,128)(2,1)} %get-tuple-element.91.d_ref), custom_call_target="tpu_custom_call" | custom-call | tf_op jit(solution)/shard_map/widen_mlp/pallas_call | solution.py:1646
  415.6 0.0 copy-done
  415.6 0.9 copy.38
  416.5 0.0 copy-done.1
  416.5 0.9 copy.39
  (3 shorter events, 0.0 us)
Async XLA Ops:
  92.2 33.4 %copy-start.2 = (s32[16]{0:T(128)}, s32[16]{0:T(128)S(1)}, u32[]{:S(2)}) copy-start(s32[16]{0:T(128)S(1)} %and_select_fusion.rank_ref) | copy-start | bytes 196
  404.5 11.1 %copy-start = (bf16[256,1536]{1,0:T(8,128)(2,1)S(1)}, bf16[256,1536]{1,0:T(8,128)(2,1)}, u32[]{:S(2)}) copy-start(bf16[256,1536]{1,0:T(8,128)(2,1)} %get-tuple-element.74) | copy-start | bytes 2359300
  404.5 12.0 %copy-start.1 = (bf16[256,1536]{1,0:T(8,128)(2,1)S(1)}, bf16[256,1536]{1,0:T(8,128)(2,1)}, u32[]{:S(2)}) copy-start(bf16[256,1536]{1,0:T(8,128)(2,1)} %get-tuple-element.82) | copy-start | bytes 2359300

commit v4 on v3

--- a/solution.py
+++ b/solution.py
@@ -499,12 +499,13 @@
 
 
 class Line:
-    def __init__(self, z, depth, at, send, recv):
-        self.z, self.depth, self.at, self.send, self.recv = z, depth, at, send, recv
+    def __init__(self, z, depth, at, send, recv, own=None):
+        self.z, self.depth, self.at, self.send, self.recv, self.own = z, depth, at, send, recv, own
 
     def copy(self, way, k, part, to):
         ref = self.at(part)
-        return remote(ref, ref, self.send.at[way, k], self.recv.at[way, k], fsdp=to)
+        source = ref if k or self.own is None else self.own
+        return remote(source, ref, self.send.at[way, k], self.recv.at[way, k], fsdp=to)
 
     def step(self, k):
         z, top = self.z, self.depth - 1
@@ -570,7 +571,7 @@
 def first_kernel(
     x_ref, gain_ref, info_ref, base_ref, step_ref, wq_ref, wk_ref, wv_ref, wo_ref, wg_ref, wu_ref, wd_ref, grad_ref,
     all_ref, qkv_ref, w_ref, table_ref, gains_ref, infos_ref, wo_all, gu_all, down_all, grad_all,
-    xs, bases, gsend, grecv, isend, irecv, bsend, brecv, send, recv, zsend, zrecv, osend, orecv,
+    xs, gu_own, bases, gsend, grecv, isend, irecv, bsend, brecv, send, recv, zsend, zrecv, osend, orecv,
     usend, urecv, dsend, drecv, send2, recv2, local, parts,
 ):
     c = lax.axis_index("ctx")
@@ -592,8 +593,25 @@
     for d in sent:
         d.start()
     out_rows = shard // 8
-    mine = pltpu.make_async_copy(wo_ref.at[pl.ds(c * out_rows, out_rows)], wo_all.at[z], parts.at[0])
-    mine.start()
+    out_own = wo_ref.at[pl.ds(c * out_rows, out_rows)]
+    down_own = wd_ref.at[pl.ds(c * down_rows, down_rows)]
+    strips = []
+    for i, weight in enumerate((wg_ref, wu_ref)):
+        for s in range(depth):
+            strips.append(
+                pltpu.make_async_copy(
+                    weight.at[:, lanes((s * 8 + c) * strip, strip)],
+                    gu_own.at[:, pl.ds((i * depth + s) * strip, strip)],
+                    parts.at[4 + i * depth + s],
+                )
+            )
+    for d in strips:
+        d.start()
+    copies = [
+        pltpu.make_async_copy(out_own, wo_all.at[z], parts.at[0]),
+        pltpu.make_async_copy(down_own, down_all.at[z], parts.at[1]),
+        pltpu.make_async_copy(grad_ref, grad_all.at[c], parts.at[2]),
+    ]
     gains_ref[z] = gain_ref[...]
     infos_ref[c] = info_ref[...]
     bases[c] = base_ref[...]
@@ -615,24 +633,10 @@
     xs[c] = (x * factor * gain).astype(BF16)
     g = Gather(c, own_half(xs.at[c]), xs, row_half, send, recv)
     g.begin()
-    mine.wait()
-    out_line = Line(z, depth, lambda d: wo_all.at[d], osend, orecv)
+    out_line = Line(z, depth, lambda d: wo_all.at[d], osend, orecv, out_own)
     out_line.step(0)
-
-    first = [pltpu.make_async_copy(wd_ref.at[pl.ds(c * down_rows, down_rows)], down_all.at[z], parts.at[1])]
-    for i, weight in enumerate((wg_ref, wu_ref)):
-        for s in range(depth):
-            first.append(
-                pltpu.make_async_copy(
-                    weight.at[:, lanes((s * 8 + c) * strip, strip)],
-                    gu_all.at[z, :, pl.ds((i * depth + s) * strip, strip)],
-                    parts.at[2 + i * depth + s],
-                )
-            )
-    for d in first:
+    for d in copies:
         d.start()
-    copies = [pltpu.make_async_copy(grad_ref, grad_all.at[c], parts.at[2 + 2 * depth])]
-    copies[0].start()
 
     def keep(k):
         d = pltpu.make_async_copy(xs.at[flip(c, k)], all_ref.at[flip(c, k)], local.at[k])
@@ -683,12 +687,14 @@
     out_line.landed(1)
     out_line.step(2)
     line.landed(2)
-    for d in first:
+    for d in strips:
         d.wait()
-    gu_line = Line(z, depth, lambda d: gu_all.at[d], usend, urecv)
-    down_line = Line(z, depth, lambda d: down_all.at[d], dsend, drecv)
+    gu_line = Line(z, depth, lambda d: gu_all.at[d], usend, urecv, gu_own)
+    down_line = Line(z, depth, lambda d: down_all.at[d], dsend, drecv, down_own)
     gu_line.step(0)
     down_line.step(0)
+    copies.append(pltpu.make_async_copy(gu_own, gu_all.at[z], parts.at[3]))
+    copies[-1].start()
     g2 = Gather(c, own_half(grad_ref), grad_all, row_half, send2, recv2)
     g2.begin()
     project(0)
@@ -753,6 +759,7 @@
         out_specs=(hbm, vm, vm, vm, vm, vm, hbm, hbm, hbm, hbm),
         scratch_shapes=[
             VMEM((8, rows, width), BF16),
+            VMEM((shard, 2 * columns // 8), BF16),
             VMEM((8,) + base.shape, F32),
             DMA((depth,)),
             DMA((depth,)),
@@ -764,7 +771,7 @@
             DMA((8, 2)),
         ]
         + [DMA((2, depth))] * 8
-        + [DMA((8, 2)), DMA((8, 2)), DMA((8,)), DMA((3 + 2 * depth,))],
+        + [DMA((8, 2)), DMA((8, 2)), DMA((8,)), DMA((4 + 2 * depth,))],
         compiler_params=params(cid),
         name="first_part",
     )(x, gains, info, base, step, *weights, grad)
@@ -788,7 +795,7 @@
 
 
 def attend_kernel(
-    order_ref, qkv_ref, ow_ref, gu_in, down_in, o_ref, low_ref, lse_ref, ow_all, gu_all, down_all,
+    order_ref, qkv_ref, ow_ref, gu_in, down_in, low_ref, lse_ref, ow_all, gu_all, down_all,
     keys, values, send, recv, local, usend, urecv, dsend, drecv,
 ):
     c = lax.axis_index("ctx")
@@ -850,9 +857,7 @@
         lse_ref[pl.ds(j, 1), :, :] = (top * factor + jnp.log2(denom)).reshape(1, 1, 2 * BLOCK)
         for h in (0, 1):
             head = slice(h * HEAD_SIZE, (h + 1) * HEAD_SIZE)
-            part = out[:, h * BLOCK : (h + 1) * BLOCK]
-            o_ref[j, head] = part
-            low_ref[j, head] = part.astype(BF16)
+            low_ref[j, head] = out[:, h * BLOCK : (h + 1) * BLOCK].astype(BF16)
 
     turns = blocks // per
     for turn in range(turns):
@@ -881,7 +886,6 @@
     tokens = blocks * BLOCK
     depth, some, width = out_part.shape
     outs = (
-        jax.ShapeDtypeStruct((blocks, 2 * HEAD_SIZE, BLOCK), F32),
         jax.ShapeDtypeStruct((blocks, 2 * HEAD_SIZE, BLOCK), BF16),
         jax.ShapeDtypeStruct((blocks, 1, 2 * BLOCK), F32),
         jax.ShapeDtypeStruct((depth, 8, some, width), BF16),
@@ -894,10 +898,10 @@
         attend_kernel,
         out_shape=outs,
         in_specs=[pl.BlockSpec(memory_space=pltpu.SMEM), vm, hbm, hbm, hbm],
-        out_specs=(vm, vm, vm, hbm, hbm, hbm),
+        out_specs=(vm, vm, hbm, hbm, hbm),
         scratch_shapes=[VMEM((tokens, HEAD_SIZE), BF16), VMEM((HEAD_SIZE, tokens), BF16), DMA((8, 2)), DMA((8, 2)), DMA]
         + [DMA((2, depth))] * 4,
-        input_output_aliases={3: 4, 4: 5},
+        input_output_aliases={3: 3, 4: 4},
         compiler_params=params(cid),
         name="attend",
     )(order, qkv, out_part, gate_up, down)
@@ -912,6 +916,7 @@
         self.s1, self.v1, self.s2, self.v2 = s1, v1, s2, v2
         self.half = p.shape[1] // 2
         self.pending = []
+        self.settled = False
 
     @staticmethod
     def scratch(rows, width):
@@ -995,11 +1000,19 @@
         self.came(2, self.diagonal.at[self.sl(1)], 1, 4)
         self.onward(1, 1, True)
 
+    def settle(self):
+        for q in (0, 1):
+            self.paired(3, q)
+            self.first[3, self.sl(q)] = self.chip(3, q).astype(BF16)
+        self.settled = True
+
     def result(self, q):
-        self.paired(3, q)
+        if not self.settled:
+            self.paired(3, q)
         self.came(0, self.last.at[0, self.sl(q)], q, 2)
         self.came(1, self.last.at[1, self.sl(q)], q, 4)
-        return self.chip(3, q) + (
+        chip = self.first[3, self.sl(q)].astype(F32) if self.settled else self.chip(3, q)
+        return chip + (
             self.last[0, self.sl(q)].astype(F32) + self.last[1, self.sl(q)].astype(F32)
         )
 
@@ -1245,8 +1258,8 @@
 
 
 class LineScatter:
-    def __init__(self, z, own, left, right, total, send, recv):
-        self.z, self.own, self.left, self.right, self.total = z, own, left, right, total
+    def __init__(self, z, own, left, right, send, recv):
+        self.z, self.own, self.left, self.right = z, own, left, right
         self.send, self.recv = send, recv
         self.top = own.shape[0] - 1
 
@@ -1254,7 +1267,7 @@
     def scratch(shape):
         depth = shape[0]
         hops = (depth - 1,) + tuple(shape[1:])
-        return [VMEM(hops, BF16), VMEM(hops, BF16), VMEM(shape[1:], F32), DMA((2, depth)), DMA((2, depth))]
+        return [VMEM(hops, BF16), VMEM(hops, BF16), DMA((2, depth)), DMA((2, depth))]
 
     def copy(self, way, s, part, to):
         there = (self.left, self.right)[way].at[s]
@@ -1283,16 +1296,26 @@
                 self.copy(way, s, part, z + 1 - 2 * way).start()
 
     def result(self):
-        self.total[...] = self.own[self.z].astype(F32)
-        for way in (0, 1):
-            place = self.z if way == 0 else self.top - self.z
-
-            @pl.when(place > 0)
-            def _():
-                self.landed(way, self.top - 1)
-                self.total[...] += (self.left, self.right)[way][self.top - 1].astype(F32)
-
-        return self.total[...].astype(BF16)
+        z, last = self.z, self.top - 1
+
+        def close(ways):
+            total = self.own[z].astype(F32)
+            for way in ways:
+                self.landed(way, last)
+                total = total + (self.left, self.right)[way][last].astype(F32)
+            self.own[z] = total.astype(BF16)
+
+        @pl.when(z == 0)
+        def _():
+            close((1,))
+
+        @pl.when((z > 0) & (z < self.top))
+        def _():
+            close((0, 1))
+
+        @pl.when(z == self.top)
+        def _():
+            close((0,))
 
     def sent(self):
         z, top = self.z, self.top
@@ -1307,26 +1330,37 @@
 
 
 def back_kernel(
-    order_ref, rank_ref, qkv_ref, o_ref, do_ref, lse_ref, table_ref, w_ref, mixed_ref, all_ref, p1_ref, owg_ref, gug_ref,
-    layer_ref, osum_ref, gsum_ref, p3_ref, qg_ref,
-    keys, keys_t, values, dk, dv, dqn, dqkv, acc, xs, stage, p1, owg, gug, *rest,
+    order_ref, rank_ref, qkv_ref, o_ref, do_ref, lse_ref, table_ref, w_ref, gains_ref, gain_two_ref,
+    mixed_ref, mgrad_ref, x_ref, all_ref, p1_ref, owg_ref, gug_ref, dg_ref,
+    layer_ref, input_ref, sum_ref, gu_all, down_all, q_all, o_all,
+    keys, keys_t, values, dk, dv, dqn, dqkv, acc, xs, big, owg, gug, down, heads, outs,
+    gain_rows, by_z, part_sum, by_c, first, last, diagonal, first2, last2, diagonal2, *rest,
 ):
-    first, second, third, (load, xload, put) = rest[:7], rest[7:14], rest[14:19], rest[19:]
+    scatter_sems = (rest[:4], rest[4:8], rest[8:12])
+    lines = (rest[12:16], rest[16:20], rest[20:24], rest[24:28])
+    send, recv, local, load, xload, zs, zr, cs, cr, free = rest[28:]
     c = lax.axis_index("ctx")
     z = lax.axis_index("fsdp")
-    depth, shard = qg_ref.shape[0], qg_ref.shape[2]
-    rows, width = layer_ref.shape
+    depth, shard = heads.shape[0], heads.shape[2]
+    rows, width = xs.shape[1:]
     others = [lax.rem(z + k, depth) for k in range(1, depth)]
-    greet([{"ctx": flip(c, k)} for k in (1, 2, 4)] + [{"fsdp": o} for o in others])
+    greet([{"ctx": flip(c, k)} for k in range(1, 8)] + [{"fsdp": o} for o in others])
+    some = acc.at[pl.ds(0, rows)]
     loads = [
         pltpu.make_async_copy(a, t, load.at[i])
-        for i, (a, t) in enumerate(((gug_ref, gug), (p1_ref, p1), (owg_ref, owg)))
+        for i, (a, t) in enumerate(
+            ((gug_ref, gug), (p1_ref, big), (owg_ref, owg), (dg_ref, down), (mixed_ref, some), (mgrad_ref, some), (x_ref, xs.at[0]))
+        )
     ]
-    for d in loads:
+    for d in loads[:4]:
         d.start()
-    line = LineScatter(z, gug, *third)
-    layer = Scatter(c, p1, *first)
-    out = Scatter(c, owg, *second)
+    gu_line, down_line, q_line, o_line = (
+        LineScatter(z, a, *refs) for a, refs in zip((gug, down, heads, outs), lines)
+    )
+    layer = Scatter(c, big, first, last, diagonal, *scatter_sems[0])
+    out = Scatter(c, owg, first2, last2, diagonal2, *scatter_sems[1])
+    one = Scatter(c, big, first, last, diagonal, *scatter_sems[2])
+    near = [flip(c, k) for k in (1, 2, 4)]
 
     blocks = qkv_ref.shape[0]
     per = CHUNK // BLOCK
@@ -1342,19 +1376,23 @@
     dk[...] = jnp.zeros_like(dk)
     dv[...] = jnp.zeros_like(dv)
     loads[0].wait()
-    line.step(0)
+    gu_line.step(0)
     loads[1].wait()
-    for k in Scatter.ORDER:
-        layer.give(k)
+    layer.give(6)
+    layer.give(2)
+    layer.give(4)
     loads[2].wait()
-    for k in Scatter.ORDER:
+    out.give(6)
+    layer.give(0)
+    for k in (2, 4, 0):
         out.give(k)
+    loads[3].wait()
 
     def attend_block(j, last):
         block = order_ref[j]
         q = two_heads(qkv_ref, block)
         do = two_heads(do_ref, block)
-        delta = jnp.sum(two_heads(o_ref, j) * do.astype(F32), 0, keepdims=True)
+        delta = jnp.sum(two_heads(o_ref, j).astype(F32) * do.astype(F32), 0, keepdims=True)
         lse = lse_ref[j]
 
         def step(t, dq, masked):
@@ -1387,16 +1425,14 @@
 
         if turn == 0:
             layer.far()
+            out.far()
         if turn == 1:
             layer.direct()
+            out.direct()
         if turn == 2:
             layer.merged()
-            line.step(1)
-            out.far()
-    for q in (0, 1):
-        at = pl.ds(q * (rows // 2), rows // 2)
-        layer_ref[at] = (mixed_ref[at] + layer.result(q)).astype(BF16)
-    out.direct()
+            gu_line.step(1)
+            down_line.step(0)
 
     for i in range(blocks):
         to = slice(i * BLOCK, (i + 1) * BLOCK)
@@ -1410,173 +1446,111 @@
     def x_load(d, slot):
         return pltpu.make_async_copy(all_ref.at[d], xs.at[slot], xload.at[slot])
 
-    def p_put(d, slot):
-        return pltpu.make_async_copy(stage.at[slot], p3_ref.at[d], put.at[slot])
-
     x_load(0, 0).start()
+    out.merged()
+    layer.settle()
+    layer.sent()
     acc[...] = jnp.zeros_like(acc)
     for d in range(8):
         slot = d % 2
         if d + 1 < 8:
             x_load(d + 1, 1 - slot).start()
-        if d > 1:
-            p_put(d - 2, slot).wait()
         part = dqkv[:, d * rows : (d + 1) * rows]
-        stage[slot] = contract(part, w_ref[...], ((0,), (0,))).astype(BF16)
-        p_put(d, slot).start()
+        big[d] = contract(part, w_ref[...], ((0,), (0,))).astype(BF16)
         x_load(d, slot).wait()
         acc[...] += jnp.dot(part, xs[slot], preferred_element_type=F32)
-        if d == 1:
-            out.merged()
         if d == 3:
-            line.step(2)
+            gu_line.step(2)
     for f in range(depth):
-        qg_ref[f] = acc[:, f * shard : (f + 1) * shard].astype(BF16)
-    osum = jnp.concatenate([out.result(0), out.result(1)], 0)
-    osum_ref[...] = osum.astype(BF16).reshape(osum_ref.shape)
-    gsum_ref[...] = line.result()
-    for d in (6, 7):
-        p_put(d, d % 2).wait()
-    layer.sent()
-    out.sent()
-    line.sent()
-
-
-def back(order, rank, arrays, big, depth, cid):
-    blocks = arrays[0].shape[0]
-    tokens = blocks * BLOCK
-    rows, width = arrays[-1].shape
-    out_rows = big[2].shape[1]
-    shard, both = big[3].shape[1:]
-    shape = jax.ShapeDtypeStruct
-    vm = pl.BlockSpec(memory_space=VMEM)
-    hbm = pl.BlockSpec(memory_space=ANY)
-    sm = pl.BlockSpec(memory_space=pltpu.SMEM)
-    tall = (tokens, HEAD_SIZE)
-    block = (8, rows, width)
-    return pl.pallas_call(
-        back_kernel,
-        out_shape=(
-            shape((rows, width), BF16),
-            shape((depth, out_rows // depth, width), BF16),
-            shape((shard, both), BF16),
-            shape(block, BF16),
-            shape((depth, 4 * HEAD_SIZE, shard), BF16),
-        ),
-        in_specs=[sm, sm] + [vm] * len(arrays) + [hbm] * len(big),
-        out_specs=(vm, vm, vm, hbm, vm),
-        scratch_shapes=[
-            VMEM(tall, BF16),
-            VMEM(tall[::-1], BF16),
-            VMEM(tall, BF16),
-            VMEM((blocks, BLOCK, HEAD_SIZE), F32),
-            VMEM((blocks, BLOCK, HEAD_SIZE), F32),
-            VMEM((blocks, 2 * HEAD_SIZE, BLOCK), BF16),
-            VMEM((4 * HEAD_SIZE, tokens), BF16),
-            VMEM((4 * HEAD_SIZE, width), F32),
-            VMEM((2, rows, width), BF16),
-            VMEM((2, rows, width), BF16),
-            VMEM(block, BF16),
-            VMEM((8, out_rows, width), BF16),
-            VMEM(big[3].shape, BF16),
-        ]
-        + Scatter.scratch(rows, width)
-        + Scatter.scratch(out_rows, width)
-        + LineScatter.scratch(big[3].shape)
-        + [DMA((3,)), DMA((2,)), DMA((2,))],
-        compiler_params=params(cid),
-        name="back",
-    )(order, rank, *arrays, *big)
-
-
-def last_kernel(
-    x_ref, mgrad_ref, gains_ref, gain_two_ref, p3_ref, gu_ref, dg_ref, qg_ref, og_ref,
-    input_ref, sum_ref, gu_all, down_all, q_all, o_all,
-    p3, down, heads, outs, down_sum, q_sum, o_sum, gain_rows, by_z, part, by_c, *rest,
-):
-    scatter_refs, lines = rest[:7], (rest[7:12], rest[12:17], rest[17:22])
-    send, recv, local, load, zs, zr, cs, cr = rest[22:]
-    c = lax.axis_index("ctx")
-    z = lax.axis_index("fsdp")
-    depth, _, shard = by_z.shape
-    rows, width = x_ref.shape
-    others = [lax.rem(z + k, depth) for k in range(1, depth)]
-    greet([{"ctx": flip(c, k)} for k in range(1, 8)] + [{"fsdp": o} for o in others])
-    loads = [
-        pltpu.make_async_copy(a, t, load.at[i])
-        for i, (a, t) in enumerate(((dg_ref, down), (qg_ref, heads), (og_ref, outs), (p3_ref, p3)))
-    ]
-    for d in loads:
-        d.start()
-    here = [pltpu.make_async_copy(gu_ref, gu_all.at[c], local.at[0])]
-    here[0].start()
-    gate_up = Gather(c, own_half(gu_ref), gu_all, row_half, send.at[0], recv.at[0])
-    down_line, q_line, o_line = (LineScatter(z, a, *refs) for a, refs in zip((down, heads, outs), lines))
-    loads[0].wait()
-    down_line.step(0)
-    loads[1].wait()
+        heads[f] = acc[:, f * shard : (f + 1) * shard].astype(BF16)
+    loads[4].start()
+    loads[6].start()
+    down_line.step(1)
     q_line.step(0)
-    loads[2].wait()
+    loads[4].wait()
+    for q in (0, 1):
+        at = pl.ds(q * (rows // 2), rows // 2)
+        xs[1, at] = (acc[at] + layer.result(q)).astype(BF16)
+    loads[5].start()
+    layer_put = pltpu.make_async_copy(xs.at[1], layer_ref, xload.at[1])
+    layer_put.start()
+    for d in near:
+        pl.semaphore_signal(free, inc=1, device_id={"ctx": d}, device_id_type=MESH)
+    pl.semaphore_wait(free, len(near))
+    for k in Scatter.ORDER:
+        one.give(k)
+    one.far()
+    outs[...] = jnp.concatenate([out.result(0), out.result(1)], 0).astype(BF16).reshape(outs.shape)
     o_line.step(0)
-    loads[3].wait()
-    scatter = Scatter(c, p3, *scatter_refs)
-    for k in Scatter.ORDER:
-        scatter.give(k)
-    scatter.far()
-    gate_up.begin()
-    scatter.direct()
-    down_line.step(1)
-    scatter.merged()
+    one.direct()
+    gu_line.result()
+    here = []
+    gathers = []
+
+    def spread(i, source, everyone):
+        here.append(pltpu.make_async_copy(source, everyone.at[c], local.at[i]))
+        here[-1].start()
+        at, own = (row_half, own_half(source)) if source.shape[0] % 32 == 0 else (column_half, own_half(source, 1))
+        gathers.append(Gather(c, own, everyone, at, send.at[i], recv.at[i]))
+        gathers[-1].begin()
+
+    spread(0, gug.at[z], gu_all)
+    down_line.step(2)
     q_line.step(1)
     o_line.step(1)
+    one.merged()
 
     gain = jnp.concatenate([gains_ref[k, 0:1, :] for k in range(depth)], 1)
-    one_grad = jnp.concatenate([scatter.result(0), scatter.result(1)], 0)
-    gate_up.near_half()
-    x = x_ref[...].astype(F32)
-    factor = lax.rsqrt(jnp.mean(x * x, -1, keepdims=True) + EPS)
+    one_grad = jnp.concatenate([one.result(0), one.result(1)], 0)
+    gathers[0].near_half()
+    loads[5].wait()
+    loads[6].wait()
+    layer_put.wait()
+    x = xs[0].astype(F32)
+    norm = lax.rsqrt(jnp.mean(x * x, -1, keepdims=True) + EPS)
     scaled = one_grad * gain
-    back = factor * scaled - x * (factor * factor * factor) * jnp.mean(scaled * x, -1, keepdims=True)
-    input_ref[...] = (mgrad_ref[...] + back).astype(BF16)
-    gain_rows[:4] = jnp.broadcast_to(jnp.sum(one_grad * x * factor, 0, keepdims=True), (4, width))
+    grad = norm * scaled - x * (norm * norm * norm) * jnp.mean(scaled * x, -1, keepdims=True)
+    xs[1] = (acc[:rows] + grad).astype(BF16)
+    here.append(pltpu.make_async_copy(xs.at[1], input_ref, xload.at[0]))
+    here[-1].start()
+    gain_rows[:4] = jnp.broadcast_to(jnp.sum(one_grad * x * norm, 0, keepdims=True), (4, width))
     gain_rows[4:] = gain_two_ref[4:]
     sent = []
     for k, o in enumerate(others):
         d = remote(gain_rows.at[:, lanes(o * shard, shard)], by_z.at[z], zs.at[k], zr.at[k], fsdp=o)
         d.start()
         sent.append(d)
-    gate_up.near_rest()
-    down_line.step(2)
+    gathers[0].near_rest()
     q_line.step(2)
     o_line.step(2)
-    gate_up.far()
+    down_line.result()
+    spread(1, down.at[z], down_all)
+    gathers[0].far()
 
     total = gain_rows[:, lanes(z * shard, shard)]
     for k in range(depth - 1):
         ref = by_z.at[lax.rem(z + depth - 1 - k, depth)]
         remote(ref, ref, zs.at[k], zr.at[k], fsdp=others[k]).wait_recv()
         total = total + by_z[lax.rem(z + depth - 1 - k, depth)]
-    part[...] = total
+    part_sum[...] = total
     for k in range(1, 8):
-        d = remote(part, by_c.at[c], cs.at[k], cr.at[k], ctx=flip(c, k))
+        d = remote(part_sum, by_c.at[c], cs.at[k], cr.at[k], ctx=flip(c, k))
         d.start()
         sent.append(d)
     by_c[c] = total
 
-    gathers = [gate_up]
-    tails = ((down_line, down_sum, down_all), (q_line, q_sum, q_all), (o_line, o_sum, o_all))
-    for i, (line, mine, everyone) in enumerate(tails):
-        mine[...] = line.result()
-        here.append(pltpu.make_async_copy(mine, everyone.at[c], local.at[i + 1]))
-        here[-1].start()
-        at, own = (row_half, own_half(mine)) if mine.shape[0] % 32 == 0 else (column_half, own_half(mine, 1))
-        gathers.append(Gather(c, own, everyone, at, send.at[i + 1], recv.at[i + 1]))
-        gathers[-1].begin()
-    for g in gathers[1:]:
+    gathers[1].near_half()
+    q_line.result()
+    spread(2, heads.at[z], q_all)
+    gathers[1].near_rest()
+    o_line.result()
+    spread(3, outs.at[z], o_all)
+    gathers[1].far()
+    for g in gathers[2:]:
         g.near_half()
-    for g in gathers[1:]:
+    for g in gathers[2:]:
         g.near_rest()
-    for g in gathers[1:]:
+    for g in gathers[2:]:
         g.far()
     for g in gathers:
         for channel, k in ((0, 1), (3, 3), (4, 5), (5, 7)):
@@ -1592,37 +1566,59 @@
         d.wait()
     for d in sent:
         d.wait_send()
-    scatter.sent()
-    for line in (down_line, q_line, o_line):
+    out.sent()
+    one.sent()
+    for line in (gu_line, down_line, q_line, o_line):
         line.sent()
     for g in gathers:
         g.sent()
 
 
-def last_part(x, mixed_grad, gains, gain_two, p3, gate_up, down, heads, outs, cid):
-    rows, width = x.shape
-    depth, _, shard = gains.shape
+def back(order, rank, arrays, large, depth, cid):
+    blocks = arrays[0].shape[0]
+    tokens = blocks * BLOCK
+    rows, width = large[0].shape
+    out_rows = large[5].shape[1]
+    gate_up, down = large[6], large[7]
+    shard = gate_up.shape[1]
     shape = jax.ShapeDtypeStruct
     vm = pl.BlockSpec(memory_space=VMEM)
     hbm = pl.BlockSpec(memory_space=ANY)
+    sm = pl.BlockSpec(memory_space=pltpu.SMEM)
+    tall = (tokens, HEAD_SIZE)
     small = (8, shard)
-    threes = (down, heads, outs)
+    lines = (gate_up.shape, down.shape, (depth, 4 * HEAD_SIZE, shard), (depth, out_rows // depth, width))
+    scatter = Scatter.scratch(rows, width)
     return pl.pallas_call(
-        last_kernel,
-        out_shape=[shape((rows, width), BF16), shape(small, F32), shape((8,) + gate_up.shape, BF16)]
-        + [shape((8,) + a.shape[1:], BF16) for a in threes],
-        in_specs=[vm] * 4 + [hbm] * 5,
-        out_specs=[vm, vm] + [hbm] * 4,
-        scratch_shapes=[VMEM(p3.shape, BF16)]
-        + [VMEM(a.shape, BF16) for a in threes]
-        + [VMEM(a.shape[1:], BF16) for a in threes]
+        back_kernel,
+        out_shape=[shape((rows, width), BF16), shape((rows, width), BF16), shape(small, F32)]
+        + [shape((8,) + a[1:], BF16) for a in lines],
+        in_specs=[sm, sm] + [vm] * len(arrays) + [hbm] * len(large),
+        out_specs=[hbm, hbm, vm] + [hbm] * 4,
+        scratch_shapes=[
+            VMEM(tall, BF16),
+            VMEM(tall[::-1], BF16),
+            VMEM(tall, BF16),
+            VMEM((blocks, BLOCK, HEAD_SIZE), F32),
+            VMEM((blocks, BLOCK, HEAD_SIZE), F32),
+            VMEM((blocks, 2 * HEAD_SIZE, BLOCK), BF16),
+            VMEM((4 * HEAD_SIZE, tokens), BF16),
+            VMEM((4 * HEAD_SIZE, width), F32),
+            VMEM((2, rows, width), BF16),
+            VMEM((8, rows, width), BF16),
+            VMEM((8, out_rows, width), BF16),
+        ]
+        + [VMEM(a, BF16) for a in lines]
         + [VMEM((8, width), F32), VMEM((depth,) + small, F32), VMEM(small, F32), VMEM((8,) + small, F32)]
-        + Scatter.scratch(rows, width)
-        + [r for a in threes for r in LineScatter.scratch(a.shape)]
-        + [DMA((4, 8, 2)), DMA((4, 8, 2)), DMA((4,)), DMA((4,)), DMA((depth,)), DMA((depth,)), DMA((8,)), DMA((8,))],
+        + scatter[:3]
+        + Scatter.scratch(out_rows, width)[:3]
+        + scatter[3:] * 3
+        + [r for a in lines for r in LineScatter.scratch(a)]
+        + [DMA((4, 8, 2)), DMA((4, 8, 2)), DMA((4,)), DMA((7,)), DMA((2,))]
+        + [DMA((depth,)), DMA((depth,)), DMA((8,)), DMA((8,)), pltpu.SemaphoreType.REGULAR],
         compiler_params=params(cid),
-        name="last_part",
-    )(x, mixed_grad, gains, gain_two, p3, gate_up, down, heads, outs)
+        name="back",
+    )(order, rank, *arrays, *large)
 
 
 def widen_mlp(gate_up, down):
@@ -1734,16 +1730,14 @@
         jnp.where(rank[None, :] == jnp.arange(blocks)[:, None], jnp.arange(blocks)[None, :], 0), 1
     ).astype(jnp.int32)
 
-    attended, attended_low, lse, out_w, gate_up_w, down_w = attend(order, qkv, out_part, gate_up_w, down_w, 1)
+    attended_low, lse, out_w, gate_up_w, down_w = attend(order, qkv, out_part, gate_up_w, down_w, 1)
     mixed, mixed_grad, gain_two_grad, do, out_wgrad, gate_up_wgrad, down_wgrad, down_sum, _, _ = middle(
         rank, attended_low, hidden_low, gains_all, grad_all, out_w.reshape(plane, -1, width), gate_up_w, down_w, 2
     )
-    arrays = (qkv, attended, do, lse, table, qkv_w, mixed)
-    layer_out, out_sum, gate_up_sum, one_sum, qkv_wgrad = back(
-        order, rank, arrays, (normed_all, down_sum, out_wgrad, gate_up_wgrad), depth, 3
-    )
-    input_grad, gain_sums, gate_up_all, down_all, qkv_all, out_grads = last_part(
-        hidden_low, mixed_grad, gains_all, gain_two_grad, one_sum, gate_up_sum, down_wgrad, qkv_wgrad, out_sum, 4
+    arrays = (qkv, attended_low, do, lse, table, qkv_w, gains_all, gain_two_grad)
+    large = (mixed, mixed_grad, hidden_low, normed_all, down_sum, out_wgrad, gate_up_wgrad, down_wgrad)
+    layer_out, input_grad, gain_sums, gate_up_all, down_all, qkv_all, out_grads = back(
+        order, rank, arrays, large, depth, 3
     )
     gate_total, up_total, down_total = widen_mlp(gate_up_all, down_all)
     query_total, key_total, value_total, out_total = widen_attention(qkv_all, out_grads)

time: 423 us -> 392 us (0.927)
  Pallas kernels: 404 us -> 374 us
    pallas_call x2 -> x1, Pallas kernels: 168 us -> 151 us  [back(): pl.pallas_call(back_kernel, out_shape=[shape((rows, width), BF16), shape(...]
    pallas_call x1, Pallas kernels: 82.6 us -> 69.4 us  [first_part(): pl.pallas_call(first_kernel, out_shape=(shape((8, rows, width), BF16), sh...]
where the time goes in v4:
time: 392 us; the launch traced here: 387 us
  Pallas kernels  374 us (95%)
  local copies, waits for them, and re-layouts  7.36 us (2%)
  other arithmetic  5.34 us (1%)
    pallas_call x1, Pallas kernels, back(): pl.pallas_call(back_kernel, out_shape=[shape((rows, width), BF16), shape(...  151 us
    pallas_call x1, Pallas kernels, middle(): pl.pallas_call(middle_kernel, out_shape=(shape((rows, width), F32), shape...  104 us
    pallas_call x1, Pallas kernels, first_part(): pl.pallas_call(first_kernel, out_shape=(shape((8, rows, width), BF16), sh...  69.4 us
    pallas_call x1, Pallas kernels, attend(): pl.pallas_call(attend_kernel, out_shape=outs, in_specs=[pl.BlockSpec(memo...  32.4 us
    pallas_call x1, Pallas kernels, widen_mlp(): pl.pallas_call(kernel, grid=(8,), out_shape=(wide, wide, jax.ShapeDtypeSt...  11.1 us

profile of v4, /device:TPU:0, one launch (start us, length us, event | category | flops | bytes accessed | tf_op | source)
XLA Modules:
  0.0 387.2 jit_solution(8101451052285337754)
XLA Ops:
  0.7 1.2 fusion.6
  1.9 1.3 fusion.5
  3.2 0.6 iota.32.info_ref
  3.8 0.7 broadcast_in_dim.52
  4.4 0.7 broadcast_in_dim.53
  5.1 0.6 pad_maximum_fusion.1.gain_ref
  5.7 0.9 fusion.2
  6.6 0.6 pad_maximum_fusion.step_ref
  7.2 69.4 %first_part.1 = (bf16[8,256,1536]{2,1,0:T(8,128)(2,1)}, bf16[16,384,128]{2,1,0:T(8,128)(2,1)}, bf16[384,1536]{1,0:T(8,128)(2,1)}, f32[16,96,128]{2,1,0:T(8,128)}...) custom-call(bf16[256,1536]{1,0:T(8,128)(2,1)} %bitcast.9, ...), custom_call_target="tpu_custom_call" | custom-call | tf_op jit(solution)/shard_map/first_part/pallas_call | solution.py:744
  76.7 0.8 slice_reduce_fusion
  77.4 0.1 reshape_squeeze.4
  77.5 0.6 slice_reduce_fusion.3
  78.1 0.1 copy.30
  78.3 0.6 broadcast_subtract_fusion
  78.9 0.1 sub.26
  79.0 0.0 copy-start.2
  79.0 0.6 select_reduce_fusion.order_ref
  79.7 32.4 %attend.1 = (bf16[16,192,128]{2,1,0:T(8,128)(2,1)}, f32[16,1,256]{2,1,0:T(1,128)}, bf16[4,8,48,1536]{3,2,1,0:T(8,128)(2,1)}, bf16[4,384,1024]{2,1,0:T(8,128)(2,1)}, bf16[4,128,1536]{2,1,0:T(8,128)(2,1)}) custom-call(s32[16]{0:T(128)} %select_reduce_fusion.order_ref, ...), custom_call_target="tpu_custom_call", output_to_operand_aliasing={{3}: (3, {}), {4}: (4, {})} | custom-call | tf_op jit(solution)/shard_map/attend/pallas_call | solution.py:897
  112.0 0.0 copy-done.2
  112.0 103.7 %middle.1 = (f32[256,1536]{1,0:T(8,128)}, f32[256,1536]{1,0:T(8,128)}, f32[8,1536]{1,0:T(8,128)}, bf16[16,192,128]{2,1,0:T(8,128)(2,1)}, bf16[8,192,1536]{2,1,0:...) custom-call(s32[16]{0:T(128)} %copy-done.2, ...), custom_call_target="tpu_custom_call", output_to_operand_aliasing={{8}: (6, {}), {9}: (7, {})} | custom-call | tf_op jit(solution)/shard_map/middle/pallas_call | solution.py:1220
  215.7 151.5 %back.1 = (bf16[256,1536]{1,0:T(8,128)(2,1)}, bf16[256,1536]{1,0:T(8,128)(2,1)}, f32[8,384]{1,0:T(8,128)}, bf16[8,384,1024]{2,1,0:T(8,128)(2,1)}, bf16[8,128,153...) custom-call(s32[16]{0:T(128)} %select_reduce_fusion.order_ref, s32[16]{0:T(128)} %copy-done.2, ...), custom_call_target="tpu_custom_call" | custom-call | tf_op jit(solution)/shard_map/back/pallas_call | solution.py:1592
  367.2 1.4 slice_reduce_fusion.1
  368.6 5.5 %widen_attention.1 = (f32[384,1536]{1,0:T(8,128)}, f32[384,768]{1,0:T(8,128)}, f32[384,768]{1,0:T(8,128)}, f32[384,1536]{1,0:T(8,128)}) custom-call(bf16[8,384,384]{2,1,0:T(8,128)(2,1)} %get-tuple-element.74.a_ref, bf16[8,48,1536]{2,1,0:T(8,128)(2,1)} %get-tuple-element.75.o_ref), custom_call_target="tpu_custom_call" | custom-call | tf_op jit(solution)/shard_map/widen_attention/pallas_call | solution.py:1673
  374.1 0.0 copy-start.1
  374.1 0.0 copy-start
  374.1 11.1 %widen_mlp.1 = (f32[384,4096]{1,0:T(8,128)}, f32[384,4096]{1,0:T(8,128)}, f32[1024,1536]{1,0:T(8,128)}) custom-call(bf16[8,384,1024]{2,1,0:T(8,128)(2,1)} %get-tuple-element.80.a_ref, bf16[8,128,1536]{2,1,0:T(8,128)(2,1)} %get-tuple-element.81.d_ref), custom_call_target="tpu_custom_call" | custom-call | tf_op jit(solution)/shard_map/widen_mlp/pallas_call | solution.py:1642
  385.2 0.0 copy-done.1
  385.2 0.9 copy.38
  386.1 0.0 copy-done
  386.1 0.9 copy.39
  (3 shorter events, 0.0 us)
Async XLA Ops:
  79.0 33.0 %copy-start.2 = (s32[16]{0:T(128)}, s32[16]{0:T(128)S(1)}, u32[]{:S(2)}) copy-start(s32[16]{0:T(128)S(1)} %and_select_fusion.rank_ref) | copy-start | bytes 196
  374.1 11.1 %copy-start.1 = (bf16[256,1536]{1,0:T(8,128)(2,1)S(1)}, bf16[256,1536]{1,0:T(8,128)(2,1)}, u32[]{:S(2)}) copy-start(bf16[256,1536]{1,0:T(8,128)(2,1)} %get-tuple-element.71) | copy-start | bytes 2359300
  374.1 12.0 %copy-start = (bf16[256,1536]{1,0:T(8,128)(2,1)S(1)}, bf16[256,1536]{1,0:T(8,128)(2,1)}, u32[]{:S(2)}) copy-start(bf16[256,1536]{1,0:T(8,128)(2,1)} %get-tuple-element.72) | copy-start | bytes 2359300

commit v5 on v4

--- a/solution.py
+++ b/solution.py
@@ -3,6 +3,7 @@
 
 import jax
 import jax.numpy as jnp
+import numpy as np
 from jax import lax
 from jax.experimental import pallas as pl
 from jax.experimental.pallas import tpu as pltpu
@@ -440,8 +441,14 @@
         ).wait_recv()
 
     def begin(self):
+        self.begin_half()
+        self.begin_rest()
+
+    def begin_half(self):
         self.start(1, 0, 2, 0, own=True)
         self.start(2, 0, 4, 1, own=True)
+
+    def begin_rest(self):
         self.start(1, 0, 2, 1, own=True)
         self.start(2, 0, 4, 0, own=True)
         self.start(0, 0, 1, 0, own=True)
@@ -568,11 +575,24 @@
     return contract(hit.astype(BF16), weight, ((1,), (1,))).astype(BF16)
 
 
+CHUNK = 512
+
+
+def two_heads(ref, block):
+    return jnp.concatenate([ref[block, :HEAD_SIZE], ref[block, HEAD_SIZE : 2 * HEAD_SIZE]], 1)
+
+
+def causal(s, t, j):
+    key = t * CHUNK + lax.broadcasted_iota(jnp.int32, s.shape, 0)
+    query = j * BLOCK + lax.broadcasted_iota(jnp.int32, s.shape, 1) % BLOCK
+    return jnp.where(key <= query, s, -jnp.inf)
+
+
 def first_kernel(
-    x_ref, gain_ref, info_ref, base_ref, step_ref, wq_ref, wk_ref, wv_ref, wo_ref, wg_ref, wu_ref, wd_ref, grad_ref,
-    all_ref, qkv_ref, w_ref, table_ref, gains_ref, infos_ref, wo_all, gu_all, down_all, grad_all,
-    xs, gu_own, bases, gsend, grecv, isend, irecv, bsend, brecv, send, recv, zsend, zrecv, osend, orecv,
-    usend, urecv, dsend, drecv, send2, recv2, local, parts,
+    pos_ref, x_ref, gain_one_ref, gain_two_ref, freq_ref, step_ref, wq_ref, wk_ref, wv_ref, wo_ref, wg_ref, wu_ref, wd_ref, grad_ref,
+    all_ref, qkv_ref, w_ref, table_ref, gains_ref, order_ref, rank_ref, low_ref, lse_ref, ow_all, gu_all, down_all, grad_all,
+    infos_ref, infos, wo_all, keys, values, xs, wz, whole, gu_own, out_mine, down_mine, grad_mine, bases, gain_ref, info_ref, base_ref, gsend, grecv, isend, irecv, bsend, brecv, send, recv, zsend, zrecv, osend, orecv,
+    usend, urecv, dsend, drecv, send2, recv2, send3, recv3, local, parts,
 ):
     c = lax.axis_index("ctx")
     z = lax.axis_index("fsdp")
@@ -582,8 +602,16 @@
     strip = gu_all.shape[2] // 2 // depth
     down_rows = down_all.shape[1]
     others = [lax.rem(z + k, depth) for k in range(1, depth)]
+    lane = lax.broadcasted_iota(jnp.int32, info_ref.shape, 1)
+    info_ref[...] = jnp.where(lane < LANES // 2, pos_ref[0, 0], pos_ref[0, BLOCK])
+    start = freq_ref[...] * info_ref[:1].astype(F32)
+    base_ref[...] = jnp.where(lane[:1] // (LANES // 4) % 2 == 0, jnp.cos(start), jnp.sin(start))
+    gain_ref[:4] = jnp.broadcast_to(gain_one_ref[...].astype(F32), (4, shard))
+    gain_ref[4:] = jnp.broadcast_to(gain_two_ref[...].astype(F32), (4, shard))
     greet([{"ctx": flip(c, k)} for k in range(1, 8)] + [{"fsdp": o} for o in others])
 
+    g2 = Gather(c, own_half(grad_ref), grad_all, row_half, send2, recv2)
+    g2.begin_half()
     sent = []
     for k, o in enumerate(others):
         sent.append(remote(gain_ref, gains_ref.at[z], gsend.at[k], grecv.at[k], fsdp=o))
@@ -595,33 +623,24 @@
     out_rows = shard // 8
     out_own = wo_ref.at[pl.ds(c * out_rows, out_rows)]
     down_own = wd_ref.at[pl.ds(c * down_rows, down_rows)]
-    strips = []
-    for i, weight in enumerate((wg_ref, wu_ref)):
-        for s in range(depth):
-            strips.append(
-                pltpu.make_async_copy(
-                    weight.at[:, lanes((s * 8 + c) * strip, strip)],
-                    gu_own.at[:, pl.ds((i * depth + s) * strip, strip)],
-                    parts.at[4 + i * depth + s],
-                )
-            )
+    strips = [
+        pltpu.make_async_copy(weight, whole.at[i], parts.at[4 + i]) for i, weight in enumerate((wg_ref, wu_ref))
+    ]
     for d in strips:
         d.start()
-    copies = [
-        pltpu.make_async_copy(out_own, wo_all.at[z], parts.at[0]),
-        pltpu.make_async_copy(down_own, down_all.at[z], parts.at[1]),
-        pltpu.make_async_copy(grad_ref, grad_all.at[c], parts.at[2]),
-    ]
+    ways = ((out_own, out_mine, ow_all.at[z, c]), (down_own, down_mine, down_all.at[z]), (grad_ref, grad_mine, grad_all.at[c]))
+    incoming = [pltpu.make_async_copy(a, b, parts.at[i]) for i, (a, b, _) in enumerate(ways)]
+    for d in incoming:
+        d.start()
     gains_ref[z] = gain_ref[...]
     infos_ref[c] = info_ref[...]
     bases[c] = base_ref[...]
 
-    own = lanes(z * shard, shard)
     count = 2 * HEAD_SIZE
-    w_ref[:count, own] = picked(wq_ref[...], c * count, count)
-    w_ref[count : count + HEAD_SIZE, own] = picked(wk_ref[...], c * HEAD_SIZE, HEAD_SIZE)
-    w_ref[count + HEAD_SIZE :, own] = picked(wv_ref[...], c * HEAD_SIZE, HEAD_SIZE)
-    line = Line(z, depth, lambda d: w_ref.at[:, lanes(d * shard, shard)], zsend, zrecv)
+    wz[z, :count] = picked(wq_ref[...], c * count, count)
+    wz[z, count : count + HEAD_SIZE] = picked(wk_ref[...], c * HEAD_SIZE, HEAD_SIZE)
+    wz[z, count + HEAD_SIZE :] = picked(wv_ref[...], c * HEAD_SIZE, HEAD_SIZE)
+    line = Line(z, depth, lambda d: wz.at[d], zsend, zrecv)
     line.step(0)
 
     x = x_ref[...].astype(F32)
@@ -634,9 +653,14 @@
     g = Gather(c, own_half(xs.at[c]), xs, row_half, send, recv)
     g.begin()
     out_line = Line(z, depth, lambda d: wo_all.at[d], osend, orecv, out_own)
+    down_line = Line(z, depth, lambda d: down_all.at[d], dsend, drecv, down_own)
     out_line.step(0)
-    for d in copies:
-        d.start()
+    copies = []
+    for i, (_, b, there) in enumerate(ways):
+        incoming[i].wait()
+        copies.append(pltpu.make_async_copy(b, there, parts.at[i]))
+        copies[-1].start()
+    wo_all[z] = out_mine[...]
 
     def keep(k):
         d = pltpu.make_async_copy(xs.at[flip(c, k)], all_ref.at[flip(c, k)], local.at[k])
@@ -677,6 +701,7 @@
     line.landed(0)
     line.step(1)
     g.near_half()
+    g2.begin_rest()
     out_line.landed(0)
     out_line.step(1)
     line.landed(1)
@@ -686,143 +711,58 @@
     keep(4)
     out_line.landed(1)
     out_line.step(2)
-    line.landed(2)
-    for d in strips:
+    for i, d in enumerate(strips):
         d.wait()
+        for f in range(depth):
+            gu_own[:, (i * depth + f) * strip : (i * depth + f + 1) * strip] = whole[i, :, lanes((f * 8 + c) * strip, strip)]
     gu_line = Line(z, depth, lambda d: gu_all.at[d], usend, urecv, gu_own)
-    down_line = Line(z, depth, lambda d: down_all.at[d], dsend, drecv, down_own)
     gu_line.step(0)
-    down_line.step(0)
     copies.append(pltpu.make_async_copy(gu_own, gu_all.at[z], parts.at[3]))
     copies[-1].start()
-    g2 = Gather(c, own_half(grad_ref), grad_all, row_half, send2, recv2)
-    g2.begin()
+    line.landed(2)
+    for f in range(depth):
+        w_ref[:, f * shard : (f + 1) * shard] = wz[f]
+    g.far()
+    g2.near_half()
     project(0)
-    g.far()
     project(2)
     project(4)
-    for channel, k in ((0, 1), (3, 3)):
+    for channel, k in ((0, 1), (3, 3), (4, 5)):
         g.paired(channel, k)
         keep(k)
         project(k)
-    g2.near_half()
-    g.paired(4, 5)
-    keep(5)
-    project(5)
     keep(6)
     project(6)
     g.paired(5, 7)
     keep(7)
     project(7)
-    g2.near_rest()
     out_line.landed(2)
-    gu_line.landed(0)
-    down_line.landed(0)
-    g2.far()
-    for channel, k in ((0, 1), (3, 3), (4, 5), (5, 7)):
-        g2.paired(channel, k)
-    for d in copies:
-        d.wait()
-    for d in sent:
-        d.wait_send()
-    line.sent((0, 1, 2))
-    out_line.sent((0, 1, 2))
-    gu_line.sent((0,))
-    down_line.sent((0,))
-    g.sent()
-    g2.sent()
-
-
-def first_part(x, gains, info, base, step, weights, grad, depth, cid):
-    rows, width = x.shape
-    shard = gains.shape[1]
-    columns = weights[4].shape[1]
-    down_rows = weights[6].shape[0] // 8
-    vm = pl.BlockSpec(memory_space=VMEM)
-    hbm = pl.BlockSpec(memory_space=ANY)
-    shape = jax.ShapeDtypeStruct
-    return pl.pallas_call(
-        first_kernel,
-        out_shape=(
-            shape((8, rows, width), BF16),
-            shape((8 * rows // BLOCK, 4 * HEAD_SIZE, BLOCK), BF16),
-            shape((4 * HEAD_SIZE, width), BF16),
-            shape((8 * rows // BLOCK, HEAD_SIZE, BLOCK), F32),
-            shape((depth,) + gains.shape, F32),
-            shape((8,) + info.shape, jnp.int32),
-            shape((depth, shard // 8, width), BF16),
-            shape((depth, shard, 2 * columns // 8), BF16),
-            shape((depth, down_rows, width), BF16),
-            shape((8, rows, width), BF16),
-        ),
-        in_specs=[vm] * 8 + [hbm] * 5,
-        out_specs=(hbm, vm, vm, vm, vm, vm, hbm, hbm, hbm, hbm),
-        scratch_shapes=[
-            VMEM((8, rows, width), BF16),
-            VMEM((shard, 2 * columns // 8), BF16),
-            VMEM((8,) + base.shape, F32),
-            DMA((depth,)),
-            DMA((depth,)),
-            DMA((8,)),
-            DMA((8,)),
-            DMA((8,)),
-            DMA((8,)),
-            DMA((8, 2)),
-            DMA((8, 2)),
-        ]
-        + [DMA((2, depth))] * 8
-        + [DMA((8, 2)), DMA((8, 2)), DMA((8,)), DMA((4 + 2 * depth,))],
-        compiler_params=params(cid),
-        name="first_part",
-    )(x, gains, info, base, step, *weights, grad)
-
-
-CHUNK = 512
-
-
-def whole_block(a):
-    return pl.BlockSpec(a.shape, lambda j, *_: (0,) * len(a.shape))
-
-
-def two_heads(ref, block):
-    return jnp.concatenate([ref[block, :HEAD_SIZE], ref[block, HEAD_SIZE : 2 * HEAD_SIZE]], 1)
-
-
-def causal(s, t, j):
-    key = t * CHUNK + lax.broadcasted_iota(jnp.int32, s.shape, 0)
-    query = j * BLOCK + lax.broadcasted_iota(jnp.int32, s.shape, 1) % BLOCK
-    return jnp.where(key <= query, s, -jnp.inf)
-
-
-def attend_kernel(
-    order_ref, qkv_ref, ow_ref, gu_in, down_in, low_ref, lse_ref, ow_all, gu_all, down_all,
-    keys, values, send, recv, local, usend, urecv, dsend, drecv,
-):
-    c = lax.axis_index("ctx")
-    z = lax.axis_index("fsdp")
-    depth = gu_all.shape[0]
-    others = [lax.rem(z + k, depth) for k in range(1, depth)]
-    greet([{"ctx": flip(c, k)} for k in (1, 2, 4)] + [{"fsdp": o} for o in others])
     few = depth // 2
-    g = Gather(
+    g3 = Gather(
         c,
-        lambda h: ow_ref.at[pl.ds(h * few, few)],
+        lambda h: wo_all.at[pl.ds(h * few, few)],
         ow_all,
         lambda ref, d, h: ref.at[pl.ds(h * few, few), d],
-        send,
-        recv,
-    )
-    here = pltpu.make_async_copy(ow_ref, ow_all.at[:, c], local)
-    here.start()
-    g.begin()
-    gu_line = Line(z, depth, lambda d: gu_all.at[d], usend, urecv)
-    down_line = Line(z, depth, lambda d: down_all.at[d], dsend, drecv)
-    gu_line.step(1)
-    down_line.step(1)
+        send3,
+        recv3,
+    )
+    for f in range(1, depth):
+        part = lax.rem(z + f, depth)
+        copies.append(pltpu.make_async_copy(wo_all.at[part], ow_all.at[part, c], parts.at[4 + f]))
+        copies[-1].start()
 
     blocks = qkv_ref.shape[0]
     per = CHUNK // BLOCK
     factor = HEAD_SIZE ** (-0.5) * math.log2(math.e)
+    small = pltpu.make_async_copy(infos_ref, infos, parts.at[8])
+    small.start()
+    small.wait()
+    starts = [infos[b // 2, 0, b % 2 * (LANES // 2)] for b in range(blocks)]
+    least = functools.reduce(jnp.minimum, starts)
+    ranks = [(start - least) // BLOCK for start in starts]
+    for i in range(blocks):
+        rank_ref[i] = ranks[i]
+        order_ref[i] = functools.reduce(jnp.maximum, [jnp.where(ranks[b] == i, b, 0) for b in range(blocks)])
     for b in range(blocks):
         there = slice(b * BLOCK, (b + 1) * BLOCK)
         keys[there, :] = qkv_ref[order_ref[b], 2 * HEAD_SIZE : 3 * HEAD_SIZE].T
@@ -859,52 +799,105 @@
             head = slice(h * HEAD_SIZE, (h + 1) * HEAD_SIZE)
             low_ref[j, head] = out[:, h * BLOCK : (h + 1) * BLOCK].astype(BF16)
 
-    turns = blocks // per
-    for turn in range(turns):
-
-        @pl.loop(turn * per, (turn + 1) * per)
+    def attend_blocks(first, count):
+        @pl.loop(first, first + count)
         def _(j):
-            attend_block(j, turn)
-
-        if turn == 1:
-            g.near_half()
-        if turn == 2:
-            g.near_rest()
-    g.far()
-    for channel, k in ((0, 1), (3, 3), (4, 5), (5, 7)):
-        g.paired(channel, k)
-    here.wait()
+            attend_block(j, first // per)
+
+    attend_blocks(0, per)
+    g2.near_rest()
+    g3.begin()
+    attend_blocks(per, per)
+    gu_line.landed(0)
+    gu_line.step(1)
+    down_line.step(0)
+    attend_blocks(2 * per, per // 2)
+    g2.far()
+    attend_blocks(2 * per + per // 2, per // 2)
+    g3.near_half()
+    attend_blocks(3 * per, per // 2)
+    g3.near_rest()
+    attend_blocks(3 * per + per // 2, per // 2)
+    g3.far()
+    for gather in (g2, g3):
+        for channel, k in ((0, 1), (3, 3), (4, 5), (5, 7)):
+            gather.paired(channel, k)
     gu_line.landed(1)
-    down_line.landed(1)
-    g.sent()
-    gu_line.sent((1,))
-    down_line.sent((1,))
-
-
-def attend(order, qkv, out_part, gate_up, down, cid):
-    blocks = qkv.shape[0]
-    tokens = blocks * BLOCK
-    depth, some, width = out_part.shape
-    outs = (
-        jax.ShapeDtypeStruct((blocks, 2 * HEAD_SIZE, BLOCK), BF16),
-        jax.ShapeDtypeStruct((blocks, 1, 2 * BLOCK), F32),
-        jax.ShapeDtypeStruct((depth, 8, some, width), BF16),
-        jax.ShapeDtypeStruct(gate_up.shape, BF16),
-        jax.ShapeDtypeStruct(down.shape, BF16),
-    )
+    down_line.landed(0)
+    for d in copies:
+        d.wait()
+    for d in sent:
+        d.wait_send()
+    line.sent((0, 1, 2))
+    out_line.sent((0, 1, 2))
+    gu_line.sent((0, 1))
+    down_line.sent((0,))
+    for gather in (g, g2, g3):
+        gather.sent()
+
+
+def first_part(positions, x, gains, freq, step, weights, grad, depth, cid):
+    rows, width = x.shape
+    shard = gains[0].shape[1]
+    small = (8, shard)
+    columns = weights[4].shape[1]
+    down_rows = weights[6].shape[0] // 8
+    blocks = 8 * rows // BLOCK
+    sm = pl.BlockSpec(memory_space=pltpu.SMEM)
     vm = pl.BlockSpec(memory_space=VMEM)
     hbm = pl.BlockSpec(memory_space=ANY)
+    shape = jax.ShapeDtypeStruct
     return pl.pallas_call(
-        attend_kernel,
-        out_shape=outs,
-        in_specs=[pl.BlockSpec(memory_space=pltpu.SMEM), vm, hbm, hbm, hbm],
-        out_specs=(vm, vm, hbm, hbm, hbm),
-        scratch_shapes=[VMEM((tokens, HEAD_SIZE), BF16), VMEM((HEAD_SIZE, tokens), BF16), DMA((8, 2)), DMA((8, 2)), DMA]
-        + [DMA((2, depth))] * 4,
-        input_output_aliases={3: 3, 4: 4},
+        first_kernel,
+        out_shape=(
+            shape((8, rows, width), BF16),
+            shape((8 * rows // BLOCK, 4 * HEAD_SIZE, BLOCK), BF16),
+            shape((4 * HEAD_SIZE, width), BF16),
+            shape((8 * rows // BLOCK, HEAD_SIZE, BLOCK), F32),
+            shape((depth,) + small, F32),
+            shape((blocks,), jnp.int32),
+            shape((blocks,), jnp.int32),
+            shape((blocks, 2 * HEAD_SIZE, BLOCK), BF16),
+            shape((blocks, 1, 2 * BLOCK), F32),
+            shape((depth, 8, shard // 8, width), BF16),
+            shape((depth, shard, 2 * columns // 8), BF16),
+            shape((depth, down_rows, width), BF16),
+            shape((8, rows, width), BF16),
+        ),
+        in_specs=[pl.BlockSpec(memory_space=pltpu.SMEM)] + [vm] * 8 + [hbm] * 5,
+        out_specs=(hbm, vm, vm, vm, vm, sm, sm, vm, vm, hbm, hbm, hbm, hbm),
+        scratch_shapes=[
+            VMEM((8, 8, LANES), jnp.int32),
+            pltpu.SMEM((8, 8, LANES), jnp.int32),
+            VMEM((depth, shard // 8, width), BF16),
+            VMEM((8 * rows, HEAD_SIZE), BF16),
+            VMEM((HEAD_SIZE, 8 * rows), BF16),
+            VMEM((8, rows, width), BF16),
+            VMEM((depth, 4 * HEAD_SIZE, shard), BF16),
+            VMEM((2, shard, columns), BF16),
+            VMEM((shard, 2 * columns // 8), BF16),
+            VMEM((shard // 8, width), BF16),
+            VMEM((down_rows, width), BF16),
+            VMEM((rows, width), BF16),
+            VMEM((8, HEAD_SIZE // 2, LANES), F32),
+            VMEM(small, F32),
+            VMEM((8, LANES), jnp.int32),
+            VMEM((HEAD_SIZE // 2, LANES), F32),
+            DMA((depth,)),
+            DMA((depth,)),
+            DMA((8,)),
+            DMA((8,)),
+            DMA((8,)),
+            DMA((8,)),
+            DMA((8, 2)),
+            DMA((8, 2)),
+        ]
+        + [DMA((2, depth))] * 8
+        + [DMA((8, 2))] * 4
+        + [DMA((8,)), DMA((9,))],
         compiler_params=params(cid),
-        name="attend",
-    )(order, qkv, out_part, gate_up, down)
+        name="first_part",
+    )(positions, x, *gains, freq, step, *weights, grad)
 
 
 class Scatter:
@@ -914,9 +907,9 @@
         self.c, self.p, self.first = c, p, first
         self.last, self.diagonal = last, diagonal
         self.s1, self.v1, self.s2, self.v2 = s1, v1, s2, v2
-        self.half = p.shape[1] // 2
+        self.half = first.shape[1] // 2 if p is None else p.shape[1] // 2
         self.pending = []
-        self.settled = False
+        self.summed = False
 
     @staticmethod
     def scratch(rows, width):
@@ -945,10 +938,14 @@
             self.go(remote(source, there, self.s1.at[j, q], self.v1.at[j, q], ctx=flip(self.c, 1)))
 
     def paired(self, j, q):
+        if self.summed:
+            return
         ref = self.first.at[j, self.sl(q)]
         remote(ref, ref, self.s1.at[j, q], self.v1.at[j, q], ctx=flip(self.c, 1)).wait_recv()
 
     def chip(self, j, q):
+        if self.summed:
+            return self.first[j, self.sl(q)].astype(F32)
         k = self.ORDER[j]
         return self.p[flip(self.c, k), self.sl(q)].astype(F32) + self.first[j, self.sl(q)].astype(F32)
 
@@ -1001,18 +998,17 @@
         self.onward(1, 1, True)
 
     def settle(self):
-        for q in (0, 1):
-            self.paired(3, q)
-            self.first[3, self.sl(q)] = self.chip(3, q).astype(BF16)
-        self.settled = True
+        for j in range(len(self.ORDER)):
+            for q in (0, 1):
+                self.paired(j, q)
+                self.first[j, self.sl(q)] = self.chip(j, q).astype(BF16)
+        self.summed = True
 
     def result(self, q):
-        if not self.settled:
-            self.paired(3, q)
+        self.paired(3, q)
         self.came(0, self.last.at[0, self.sl(q)], q, 2)
         self.came(1, self.last.at[1, self.sl(q)], q, 4)
-        chip = self.first[3, self.sl(q)].astype(F32) if self.settled else self.chip(3, q)
-        return chip + (
+        return self.chip(3, q) + (
             self.last[0, self.sl(q)].astype(F32) + self.last[1, self.sl(q)].astype(F32)
         )
 
@@ -1043,24 +1039,29 @@
 
 def middle_kernel(
     rank_ref, low_ref, x_ref, gains_ref, g_ref, ow_ref, gu_in, down_in,
-    mixed_ref, mgrad_ref, gsum_ref, do_ref, owg_ref, gug_ref, dg_ref, p1_ref, gu_all, down_all,
-    out_w, wgu, wd, grads, two, p2, act, dgu, stage, give, got,
-    first, last, diagonal, s1, v1, s2, v2,
-    esend, erecv, fsend, frecv, send, recv, usend, urecv, dsend, drecv, load, put, wput,
+    mixed_out, sums_ref, mgrad_ref, gsum_ref, do_ref, owg_ref, gug_ref, dg_ref, left_ref, right_ref, gu_all, down_all,
+    mixed_ref, p1, wgu, wd, grads, two, p2, act, dgu, give, got, *rest,
 ):
+    scatter_refs, layer_refs = rest[:7], rest[7:10]
+    esend, erecv, fsend, frecv, send, recv, usend, urecv, dsend, drecv, load, wput, hsend, hrecv = rest[10:]
     c = lax.axis_index("ctx")
     z = lax.axis_index("fsdp")
     depth, shard, both = gu_all.shape
     mine = both // 2
     rows, width = x_ref.shape
-    rows_of_out = out_w.shape[1]
+    out_rows = ow_ref.shape[1]
+    out_w = p1.at[:, pl.ds(0, out_rows)]
     others = [lax.rem(z + k, depth) for k in range(1, depth)]
     greet([{"ctx": flip(c, k)} for k in range(1, 8)] + [{"fsdp": o} for o in others])
     gu_line = Line(z, depth, lambda d: gu_all.at[d], usend, urecv)
     down_line = Line(z, depth, lambda d: down_all.at[d], dsend, drecv)
     gu_line.step(2)
-    down_line.step(2)
-    loads = [pltpu.make_async_copy(ow_ref, out_w, load.at[0]), pltpu.make_async_copy(g_ref, grads, load.at[1])]
+    down_line.step(1)
+    loads = [
+        pltpu.make_async_copy(ow_ref, out_w, load.at[0]),
+        pltpu.make_async_copy(g_ref, grads, load.at[1]),
+        pltpu.make_async_copy(x_ref, two.at[c], load.at[2]),
+    ]
     for d in loads:
         d.start()
 
@@ -1069,27 +1070,30 @@
     sent = exchange_start(c, give, got, esend, erecv)
     got[pl.ds(2 * c, 2)] = give[pl.ds(2 * c, 2)]
     loads[0].wait()
+    loads[2].wait()
     exchange_landed(c, got, esend, erecv)
-    x = lax.fori_loop(
-        0, 8, lambda i, total: total + contract(both_blocks(got, i), out_w[i], ((0,), (0,))), x_ref[...].astype(F32)
-    )
-    mixed_ref[...] = x
+    mixed_ref[...] = two[c].astype(F32)
+
+    @pl.loop(0, 8)
+    def _(i):
+        mixed_ref[...] += contract(both_blocks(got, i), p1[i, :out_rows], ((0,), (0,)))
+
     gain = jnp.concatenate([gains_ref[k, 4:5, :] for k in range(depth)], 1)
-    factor = lax.rsqrt(jnp.mean(x * x, -1, keepdims=True) + EPS)
-    two[c] = (x * factor * gain).astype(BF16)
+    halves = [pl.ds(q * (rows // 2), rows // 2) for q in (0, 1)]
+    for at in halves:
+        x = mixed_ref[at]
+        factor = lax.rsqrt(jnp.mean(x * x, -1, keepdims=True) + EPS)
+        two[c, at] = (x * factor * gain).astype(BF16)
     g = Gather(c, own_half(two.at[c]), two, row_half, send, recv)
     g.begin()
     loads[1].wait()
     gu_line.landed(2)
     weights = [pltpu.make_async_copy(gu_all, wgu, load.at[2])]
     weights[0].start()
-    down_line.landed(2)
-    weights.append(pltpu.make_async_copy(down_all, wd, load.at[3]))
-    weights[1].start()
-    for d in weights:
-        d.wait()
-
-    def block(d, slot):
+    down_line.landed(1)
+    down_line.step(2)
+
+    def block(d):
         up_w = wgu[...].reshape(width, both)
         down_w = wd[...].reshape(mine, width)
         gate_up = jnp.dot(two[d], up_w, preferred_element_type=F32)
@@ -1104,40 +1108,40 @@
         grad = jnp.concatenate([gate_grad, up_grad], 1).astype(BF16)
         dgu[d] = grad
         p2[d] = contract(grad, up_w, ((1,), (1,))).astype(BF16)
-        stage[slot] = jnp.dot(active, down_w, preferred_element_type=F32).astype(BF16)
-        pltpu.make_async_copy(stage.at[slot], p1_ref.at[d], put.at[slot]).start()
-
-    def drain(slot):
-        pltpu.make_async_copy(stage.at[slot], p1_ref.at[c], put.at[slot]).wait()
-
-    def pair(k, again):
+        p1[d] = jnp.dot(active, down_w, preferred_element_type=F32).astype(BF16)
+
+    def pair(k):
         d = flip(c, k)
         other = flip(c, 1 ^ k)
 
         @pl.loop(0, 2)
         def _(i):
-            if again:
-                drain(i)
-            block(other + i * (d - other), i)
-
-    scatter = Scatter(c, p2, first, last, diagonal, s1, v1, s2, v2)
-    g.paired(0, 1)
-    pair(0, False)
-    scatter.give(0)
+            block(other + i * (d - other))
+
+        scatter.give(k)
+
+    scatter = Scatter(c, p2, *scatter_refs)
+    layer = Scatter(c, p1, layer_refs[0], None, None, *layer_refs[1:], None, None)
     g.near_half()
     g.near_rest()
+    down_line.landed(2)
+    weights.append(pltpu.make_async_copy(down_all, wd, load.at[3]))
+    weights[1].start()
+    for d in weights:
+        d.wait()
+    g.paired(0, 1)
+    pair(0)
     g.paired(3, 3)
-    pair(2, True)
-    scatter.give(2)
+    pair(2)
     g.far()
     g.paired(5, 7)
-    pair(6, True)
-    scatter.give(6)
+    pair(6)
     g.paired(4, 5)
     scatter.far()
-    pair(4, True)
-    scatter.give(4)
+    pair(4)
     scatter.direct()
+    for k in Scatter.ORDER:
+        layer.give(k)
 
     puts = []
 
@@ -1153,8 +1157,30 @@
 
     wide(0)
     scatter.merged()
+    layer.settle()
+    keeps = [
+        pltpu.make_async_copy(layer.first, sums_ref, load.at[1]),
+        pltpu.make_async_copy(mixed_ref, mixed_out, load.at[2]),
+    ]
+    for d in keeps:
+        d.start()
+    layer.sent()
+    again = pltpu.make_async_copy(ow_ref, out_w, load.at[0])
+    again.start()
     for f in range(1, depth):
         wide(f)
+
+    hop_right = remote(wgu.at[depth - 1], left_ref, hsend.at[0], hrecv.at[0], fsdp=z + 1)
+    hop_left = remote(wgu.at[0], right_ref, hsend.at[1], hrecv.at[1], fsdp=z - 1)
+
+    @pl.when(z == 0)
+    def _():
+        hop_right.start()
+
+    @pl.when(z == depth - 1)
+    def _():
+        hop_left.start()
+
     strip = mine // depth
     for f in range(0, depth, 2):
         part = lambda i, total: total + contract(
@@ -1167,46 +1193,67 @@
     puts.append(pltpu.make_async_copy(wd, dg_ref, wput.at[depth]))
     puts[-1].start()
 
-    two_grad = jnp.concatenate([scatter.result(0), scatter.result(1)], 0)
-    x = mixed_ref[...]
-    factor = lax.rsqrt(jnp.mean(x * x, -1, keepdims=True) + EPS)
-    scaled = two_grad * gain
-    mixed_grad = (
-        grads[c].astype(F32)
-        + factor * scaled
-        - x * (factor * factor * factor) * jnp.mean(scaled * x, -1, keepdims=True)
-    )
-    gsum_ref[...] = jnp.broadcast_to(jnp.sum(two_grad * x * factor, 0, keepdims=True), gsum_ref.shape)
-    mgrad_ref[...] = mixed_grad
-    branch = mixed_grad.astype(BF16)
+    g.sent()
+    gain_sum = jnp.zeros((1, width), F32)
+    for q, at in enumerate(halves):
+        two_grad = scatter.result(q)
+        x = mixed_ref[at]
+        factor = lax.rsqrt(jnp.mean(x * x, -1, keepdims=True) + EPS)
+        gain_sum = gain_sum + jnp.sum(two_grad * x * factor, 0, keepdims=True)
+        scaled = two_grad * gain
+        mixed_grad = (
+            grads[c, at].astype(F32)
+            + factor * scaled
+            - x * (factor * factor * factor) * jnp.mean(scaled * x, -1, keepdims=True)
+        )
+        mgrad_ref[at] = mixed_grad
+        two[0, at] = mixed_grad.astype(BF16)
+    gsum_ref[...] = jnp.broadcast_to(gain_sum, gsum_ref.shape)
     for d in sent:
         d.wait_send()
+    again.wait()
     for i in range(8):
-        part = contract(out_w[i], branch, ((1,), (1,))).astype(BF16)
+        part = contract(p1[i, :out_rows], two[0], ((1,), (1,))).astype(BF16)
         give[2 * i] = part[:, :BLOCK]
         give[2 * i + 1] = part[:, BLOCK:]
     sent = exchange_start(c, give, do_ref, fsend, frecv)
     do_ref[pl.ds(2 * c, 2)] = give[pl.ds(2 * c, 2)]
-    for d in puts:
-        d.wait()
-    for i in (0, 1):
-        drain(i)
-    few = rows_of_out // depth
+    few = out_rows // depth
     for i in range(8):
-        part = jnp.dot(both_blocks(got, i), branch, preferred_element_type=F32).astype(BF16)
+        part = jnp.dot(both_blocks(got, i), two[0], preferred_element_type=F32).astype(BF16)
         f = i * depth // 8
         for t in range(depth):
-            out_w[i * depth % 8 + t, f * few : (f + 1) * few] = part[t * few : (t + 1) * few]
+            p1[i * depth % 8 + t, f * few : (f + 1) * few] = part[t * few : (t + 1) * few]
     out_put = pltpu.make_async_copy(out_w, owg_ref, load.at[0])
     out_put.start()
     exchange_landed(c, do_ref, fsend, frecv)
+    scatter.sent()
+
+    @pl.when(z == 0)
+    def _():
+        hop_right.wait_send()
+
+    @pl.when(z == depth - 1)
+    def _():
+        hop_left.wait_send()
+
+    @pl.when(z == 1)
+    def _():
+        remote(left_ref, left_ref, hsend.at[0], hrecv.at[0], fsdp=z - 1).wait_recv()
+
+    @pl.when(z == depth - 2)
+    def _():
+        remote(right_ref, right_ref, hsend.at[1], hrecv.at[1], fsdp=z + 1).wait_recv()
+
     out_put.wait()
+    for d in puts:
+        d.wait()
+    for d in keeps:
+        d.wait()
     for d in sent:
         d.wait_send()
-    scatter.sent()
-    g.sent()
     gu_line.sent((2,))
-    down_line.sent((2,))
+    down_line.sent((1, 2))
 
 
 def middle(rank, low, x, gains, grad_all, out_w, gate_up, down, cid):
@@ -1221,20 +1268,23 @@
         middle_kernel,
         out_shape=(
             shape((rows, width), F32),
+            shape((4, rows, width), BF16),
             shape((rows, width), F32),
             shape((8, width), F32),
             shape(heads, BF16),
             shape(out_w.shape, BF16),
             shape(gate_up.shape, BF16),
             shape(down.shape, BF16),
-            shape(block, BF16),
+            shape((shard, both), BF16),
+            shape((shard, both), BF16),
             shape(gate_up.shape, BF16),
             shape(down.shape, BF16),
         ),
-        in_specs=[pl.BlockSpec(memory_space=pltpu.SMEM), vm, vm, vm, hbm, hbm, hbm, hbm],
-        out_specs=(vm, vm, vm, vm, hbm, hbm, hbm, hbm, hbm, hbm),
+        in_specs=[pl.BlockSpec(memory_space=pltpu.SMEM), vm, hbm, vm, hbm, hbm, hbm, hbm],
+        out_specs=(hbm, hbm, vm, vm, vm, hbm, hbm, hbm, hbm, hbm, hbm, hbm),
         scratch_shapes=[
-            VMEM(out_w.shape, BF16),
+            VMEM((rows, width), F32),
+            VMEM(block, BF16),
             VMEM(gate_up.shape, BF16),
             VMEM(down.shape, BF16),
             VMEM(block, BF16),
@@ -1242,16 +1292,16 @@
             VMEM(block, BF16),
             VMEM((8, rows, both // 2), BF16),
             VMEM((8, rows, both), BF16),
-            VMEM((2, rows, width), BF16),
             VMEM(heads, BF16),
             VMEM(heads, BF16),
         ]
         + Scatter.scratch(rows, width)
+        + [VMEM((4, rows, width), BF16), DMA((4, 2)), DMA((4, 2))]
         + [DMA((8,))] * 4
         + [DMA((8, 2))] * 2
         + [DMA((2, depth))] * 4
-        + [DMA((4,)), DMA((2,)), DMA((depth + 1,))],
-        input_output_aliases={6: 8, 7: 9},
+        + [DMA((4,)), DMA((depth + 1,)), DMA((2,)), DMA((2,))],
+        input_output_aliases={6: 10, 7: 11},
         compiler_params=params(cid),
         name="middle",
     )(rank, low, x, gains, grad_all, out_w, gate_up, down)
@@ -1262,6 +1312,7 @@
         self.z, self.own, self.left, self.right = z, own, left, right
         self.send, self.recv = send, recv
         self.top = own.shape[0] - 1
+        self.begun = None
 
     @staticmethod
     def scratch(shape):
@@ -1274,6 +1325,9 @@
         return remote(self.own.at[part], there, self.send.at[way, s], self.recv.at[way, s], fsdp=to)
 
     def landed(self, way, s):
+        if s == 0 and self.begun:
+            self.begun[way].wait()
+            return
         ref = (self.left, self.right)[way].at[s]
         remote(ref, ref, self.send.at[way, s], self.recv.at[way, s], fsdp=self.z - 1 + 2 * way).wait_recv()
 
@@ -1319,7 +1373,7 @@
 
     def sent(self):
         z, top = self.z, self.top
-        for s in range(top):
+        for s in range(1 if self.begun else 0, top):
             for way in (0, 1):
                 place = z if way == 0 else top - z
                 part = top - s + z if way == 0 else s - top + z
@@ -1331,7 +1385,7 @@
 
 def back_kernel(
     order_ref, rank_ref, qkv_ref, o_ref, do_ref, lse_ref, table_ref, w_ref, gains_ref, gain_two_ref,
-    mixed_ref, mgrad_ref, x_ref, all_ref, p1_ref, owg_ref, gug_ref, dg_ref,
+    mgrad_ref, x_ref, mixed_ref, sums_ref, all_ref, owg_ref, gug_ref, dg_ref, left_ref, right_ref,
     layer_ref, input_ref, sum_ref, gu_all, down_all, q_all, o_all,
     keys, keys_t, values, dk, dv, dqn, dqkv, acc, xs, big, owg, gug, down, heads, outs,
     gain_rows, by_z, part_sum, by_c, first, last, diagonal, first2, last2, diagonal2, *rest,
@@ -1349,17 +1403,33 @@
     loads = [
         pltpu.make_async_copy(a, t, load.at[i])
         for i, (a, t) in enumerate(
-            ((gug_ref, gug), (p1_ref, big), (owg_ref, owg), (dg_ref, down), (mixed_ref, some), (mgrad_ref, some), (x_ref, xs.at[0]))
+            ((gug_ref, gug), (owg_ref, owg), (dg_ref, down), (mgrad_ref, some), (x_ref, xs.at[0]))
         )
     ]
-    for d in loads[:4]:
+    loads.append(pltpu.make_async_copy(sums_ref, first, load.at[7]))
+    loads.append(pltpu.make_async_copy(mixed_ref, some, load.at[8]))
+    for d in loads[:3] + loads[5:6]:
         d.start()
     gu_line, down_line, q_line, o_line = (
         LineScatter(z, a, *refs) for a, refs in zip((gug, down, heads, outs), lines)
     )
-    layer = Scatter(c, big, first, last, diagonal, *scatter_sems[0])
-    out = Scatter(c, owg, first2, last2, diagonal2, *scatter_sems[1])
-    one = Scatter(c, big, first, last, diagonal, *scatter_sems[2])
+    gu_line.begun = (
+        pltpu.make_async_copy(left_ref, gu_line.left.at[0], load.at[5]),
+        pltpu.make_async_copy(right_ref, gu_line.right.at[0], load.at[6]),
+    )
+
+    @pl.when(z == 1)
+    def _():
+        gu_line.begun[0].start()
+
+    @pl.when(z == depth - 2)
+    def _():
+        gu_line.begun[1].start()
+
+    layer = Scatter(c, None, first, last, diagonal, *scatter_sems[2])
+    layer.summed = True
+    out = Scatter(c, owg, first2, last2, diagonal2, *scatter_sems[0])
+    one = Scatter(c, big, first, last, diagonal, *scatter_sems[1])
     near = [flip(c, k) for k in (1, 2, 4)]
 
     blocks = qkv_ref.shape[0]
@@ -1376,17 +1446,15 @@
     dk[...] = jnp.zeros_like(dk)
     dv[...] = jnp.zeros_like(dv)
     loads[0].wait()
-    gu_line.step(0)
+    gu_line.step(1)
+    loads[2].wait()
+    down_line.step(0)
     loads[1].wait()
-    layer.give(6)
-    layer.give(2)
-    layer.give(4)
-    loads[2].wait()
-    out.give(6)
-    layer.give(0)
-    for k in (2, 4, 0):
+    for k in Scatter.ORDER:
         out.give(k)
-    loads[3].wait()
+    loads[5].wait()
+    layer.far()
+    layer.direct()
 
     def attend_block(j, last):
         block = order_ref[j]
@@ -1424,15 +1492,13 @@
             attend_block(j, turn)
 
         if turn == 0:
-            layer.far()
             out.far()
         if turn == 1:
-            layer.direct()
             out.direct()
         if turn == 2:
             layer.merged()
-            gu_line.step(1)
-            down_line.step(0)
+            gu_line.step(2)
+            down_line.step(1)
 
     for i in range(blocks):
         to = slice(i * BLOCK, (i + 1) * BLOCK)
@@ -1446,10 +1512,8 @@
     def x_load(d, slot):
         return pltpu.make_async_copy(all_ref.at[d], xs.at[slot], xload.at[slot])
 
+    out.merged()
     x_load(0, 0).start()
-    out.merged()
-    layer.settle()
-    layer.sent()
     acc[...] = jnp.zeros_like(acc)
     for d in range(8):
         slot = d % 2
@@ -1459,29 +1523,27 @@
         big[d] = contract(part, w_ref[...], ((0,), (0,))).astype(BF16)
         x_load(d, slot).wait()
         acc[...] += jnp.dot(part, xs[slot], preferred_element_type=F32)
-        if d == 3:
-            gu_line.step(2)
     for f in range(depth):
         heads[f] = acc[:, f * shard : (f + 1) * shard].astype(BF16)
+    loads[6].start()
     loads[4].start()
-    loads[6].start()
-    down_line.step(1)
     q_line.step(0)
-    loads[4].wait()
+    loads[6].wait()
     for q in (0, 1):
         at = pl.ds(q * (rows // 2), rows // 2)
         xs[1, at] = (acc[at] + layer.result(q)).astype(BF16)
-    loads[5].start()
+    loads[3].start()
     layer_put = pltpu.make_async_copy(xs.at[1], layer_ref, xload.at[1])
     layer_put.start()
+    layer.sent()
     for d in near:
         pl.semaphore_signal(free, inc=1, device_id={"ctx": d}, device_id_type=MESH)
     pl.semaphore_wait(free, len(near))
     for k in Scatter.ORDER:
         one.give(k)
-    one.far()
     outs[...] = jnp.concatenate([out.result(0), out.result(1)], 0).astype(BF16).reshape(outs.shape)
     o_line.step(0)
+    one.far()
     one.direct()
     gu_line.result()
     here = []
@@ -1501,19 +1563,25 @@
     one.merged()
 
     gain = jnp.concatenate([gains_ref[k, 0:1, :] for k in range(depth)], 1)
-    one_grad = jnp.concatenate([one.result(0), one.result(1)], 0)
     gathers[0].near_half()
-    loads[5].wait()
-    loads[6].wait()
+    q_line.step(2)
+    o_line.step(2)
+    loads[3].wait()
+    loads[4].wait()
     layer_put.wait()
-    x = xs[0].astype(F32)
-    norm = lax.rsqrt(jnp.mean(x * x, -1, keepdims=True) + EPS)
-    scaled = one_grad * gain
-    grad = norm * scaled - x * (norm * norm * norm) * jnp.mean(scaled * x, -1, keepdims=True)
-    xs[1] = (acc[:rows] + grad).astype(BF16)
+    gain_sum = jnp.zeros((1, width), F32)
+    for q in (0, 1):
+        at = pl.ds(q * (rows // 2), rows // 2)
+        one_grad = one.result(q)
+        x = xs[0, at].astype(F32)
+        norm = lax.rsqrt(jnp.mean(x * x, -1, keepdims=True) + EPS)
+        gain_sum = gain_sum + jnp.sum(one_grad * x * norm, 0, keepdims=True)
+        scaled = one_grad * gain
+        grad = norm * scaled - x * (norm * norm * norm) * jnp.mean(scaled * x, -1, keepdims=True)
+        xs[1, at] = (acc[at] + grad).astype(BF16)
     here.append(pltpu.make_async_copy(xs.at[1], input_ref, xload.at[0]))
     here[-1].start()
-    gain_rows[:4] = jnp.broadcast_to(jnp.sum(one_grad * x * norm, 0, keepdims=True), (4, width))
+    gain_rows[:4] = jnp.broadcast_to(gain_sum, (4, width))
     gain_rows[4:] = gain_two_ref[4:]
     sent = []
     for k, o in enumerate(others):
@@ -1521,11 +1589,13 @@
         d.start()
         sent.append(d)
     gathers[0].near_rest()
-    q_line.step(2)
-    o_line.step(2)
     down_line.result()
     spread(1, down.at[z], down_all)
     gathers[0].far()
+    q_line.result()
+    spread(2, heads.at[z], q_all)
+    o_line.result()
+    spread(3, outs.at[z], o_all)
 
     total = gain_rows[:, lanes(z * shard, shard)]
     for k in range(depth - 1):
@@ -1539,18 +1609,11 @@
         sent.append(d)
     by_c[c] = total
 
-    gathers[1].near_half()
-    q_line.result()
-    spread(2, heads.at[z], q_all)
-    gathers[1].near_rest()
-    o_line.result()
-    spread(3, outs.at[z], o_all)
-    gathers[1].far()
-    for g in gathers[2:]:
+    for g in gathers[1:]:
         g.near_half()
-    for g in gathers[2:]:
+    for g in gathers[1:]:
         g.near_rest()
-    for g in gathers[2:]:
+    for g in gathers[1:]:
         g.far()
     for g in gathers:
         for channel, k in ((0, 1), (3, 3), (4, 5), (5, 7)):
@@ -1614,48 +1677,66 @@
         + Scatter.scratch(out_rows, width)[:3]
         + scatter[3:] * 3
         + [r for a in lines for r in LineScatter.scratch(a)]
-        + [DMA((4, 8, 2)), DMA((4, 8, 2)), DMA((4,)), DMA((7,)), DMA((2,))]
+        + [DMA((4, 8, 2)), DMA((4, 8, 2)), DMA((4,)), DMA((9,)), DMA((2,))]
         + [DMA((depth,)), DMA((depth,)), DMA((8,)), DMA((8,)), pltpu.SemaphoreType.REGULAR],
         compiler_params=params(cid),
         name="back",
     )(order, rank, *arrays, *large)
 
 
-def widen_mlp(gate_up, down):
+def widen(gate_up, down, out, sums):
     _, shard, both = gate_up.shape
     mine = both // 2
-    depth = mine // LANES
+    strips = mine // LANES
     step = shard // 8
-
-    def kernel(a_ref, d_ref, gate_ref, up_ref, down_ref):
-        for i, out in enumerate((gate_ref, up_ref)):
+    _, rows, width = down.shape
+
+    def kernel(a_ref, d_ref, o_ref, s_ref, gate_ref, up_ref, down_ref, out_ref, one_ref, two_ref):
+        for i, target in enumerate((gate_ref, up_ref)):
             for c in range(8):
-                for s in range(depth):
-                    out[:, (s * 8 + c) * LANES : (s * 8 + c + 1) * LANES] = a_ref[
+                for s in range(strips):
+                    target[:, (s * 8 + c) * LANES : (s * 8 + c + 1) * LANES] = a_ref[
                         c, :, i * mine + s * LANES : i * mine + (s + 1) * LANES
                     ].astype(F32)
         down_ref[...] = d_ref[0].astype(F32)
-
-    _, rows, width = down.shape
+        out_ref[...] = o_ref[0].astype(F32)
+        one_ref[...] = s_ref[0]
+        two_ref[...] = s_ref[4]
+
     wide = jax.ShapeDtypeStruct((shard, 8 * mine), F32)
-    wide_spec = pl.BlockSpec((step, 8 * mine), lambda i: (i, 0))
+    gain = jax.ShapeDtypeStruct((shard,), F32)
+    by_rows = lambda n, columns: pl.BlockSpec((n, columns), lambda i: (i, 0))
+    by_device = lambda a: pl.BlockSpec((1,) + a.shape[1:], lambda i: (i, 0, 0))
     return pl.pallas_call(
         kernel,
         grid=(8,),
-        out_shape=(wide, wide, jax.ShapeDtypeStruct((8 * rows, width), F32)),
-        in_specs=[pl.BlockSpec((8, step, both), lambda i: (0, i, 0)), pl.BlockSpec((1, rows, width), lambda i: (i, 0, 0))],
-        out_specs=(wide_spec, wide_spec, pl.BlockSpec((rows, width), lambda i: (i, 0))),
+        out_shape=(
+            wide,
+            wide,
+            jax.ShapeDtypeStruct((8 * rows, width), F32),
+            jax.ShapeDtypeStruct((shard, width), F32),
+            gain,
+            gain,
+        ),
+        in_specs=[
+            pl.BlockSpec((8, step, both), lambda i: (0, i, 0)),
+            by_device(down),
+            by_device(out),
+            pl.BlockSpec(sums.shape, lambda i: (0, 0)),
+        ],
+        out_specs=(by_rows(step, 8 * mine), by_rows(step, 8 * mine), by_rows(rows, width), by_rows(step, width))
+        + (pl.BlockSpec((shard,), lambda i: (0,)),) * 2,
         compiler_params=pltpu.CompilerParams(vmem_limit_bytes=VMEM_BYTES),
-        name="widen_mlp",
-    )(gate_up, down)
-
-
-def widen_attention(qkv, out):
+        name="widen",
+    )(gate_up, down, out, sums)
+
+
+def widen_heads(qkv):
     shard = qkv.shape[2]
-    width = out.shape[2]
-
-    def kernel(a_ref, o_ref, q_out, k_out, v_out, out_out):
-        per_q = 2 * HEAD_SIZE
+    per_q = 2 * HEAD_SIZE
+    heads = 8 * HEAD_SIZE
+
+    def kernel(a_ref, q_out, k_out, v_out):
         for c in range(0, 8, 2):
             both = jnp.concatenate([a_ref[c + i, :per_q, :] for i in (0, 1)], 0)
             q_out[:, c * per_q : (c + 2) * per_q] = both.astype(F32).T
@@ -1663,21 +1744,18 @@
             for c in range(0, 8, 4):
                 four = jnp.concatenate([a_ref[c + i, first : first + HEAD_SIZE, :] for i in range(4)], 0)
                 target[:, c * HEAD_SIZE : (c + 4) * HEAD_SIZE] = four.astype(F32).T
-        for c in range(8):
-            rows = out.shape[1]
-            out_out[c * rows : (c + 1) * rows, :] = o_ref[c].astype(F32)
-
-    vm = pl.BlockSpec(memory_space=VMEM)
+
+    by_rows = lambda n: pl.BlockSpec((LANES, n), lambda i: (i, 0))
     shape = lambda n: jax.ShapeDtypeStruct((shard, n), F32)
-    heads = 8 * HEAD_SIZE
     return pl.pallas_call(
         kernel,
-        out_shape=(shape(2 * heads), shape(heads), shape(heads), shape(width)),
-        in_specs=[vm, vm],
-        out_specs=(vm, vm, vm, vm),
+        grid=(shard // LANES,),
+        out_shape=(shape(2 * heads), shape(heads), shape(heads)),
+        in_specs=[pl.BlockSpec((8, 4 * HEAD_SIZE, LANES), lambda i: (0, 0, i))],
+        out_specs=(by_rows(2 * heads), by_rows(heads), by_rows(heads)),
         compiler_params=pltpu.CompilerParams(vmem_limit_bytes=VMEM_BYTES),
-        name="widen_attention",
-    )(qkv, out)
+        name="widen_heads",
+    )(qkv)
 
 
 def in_plane(
@@ -1700,56 +1778,37 @@
     shard = width // depth
     half = HEAD_SIZE // 2
 
-    position = positions[0]
-    lane = lax.broadcasted_iota(jnp.int32, (8, LANES), 1)
-    info = jnp.where(lane < LANES // 2, position[0], position[BLOCK])
-    gains = jnp.concatenate(
-        [
-            jnp.broadcast_to(attn_gain.astype(F32)[None], (4, shard)),
-            jnp.broadcast_to(mlp_gain.astype(F32)[None], (4, shard)),
-        ],
-        0,
-    )
-    freq = THETA ** (-(jnp.arange(half, dtype=F32) * 2.0 / HEAD_SIZE))
-    start = freq[:, None] * info[:1].astype(F32)
-    quarter = lane[:1] // (LANES // 4)
-    base = jnp.where(quarter % 2 == 0, jnp.cos(start), jnp.sin(start))
-    inner = freq[:, None] * jnp.arange(BLOCK, dtype=F32)[None]
-    step = jnp.concatenate([jnp.cos(inner), jnp.sin(inner)], 0)
+    gains = (attn_gain.reshape(1, shard), mlp_gain.reshape(1, shard))
+    freq = np.float32(THETA) ** (-(np.arange(half, dtype=np.float32) * np.float32(2.0) / np.float32(HEAD_SIZE)))
+    inner = freq[:, None] * np.arange(BLOCK, dtype=np.float32)[None]
+    step = jnp.asarray(np.concatenate([np.cos(inner), np.sin(inner)], 0).astype(np.float32))
+    freq = jnp.asarray(np.broadcast_to(freq[:, None], (half, LANES)).astype(np.float32))
 
     hidden_low = hidden_in[0]
     weights = (w_query, key_projection, value_projection, w_out, w_gate, w_up, w_down)
     grad_low = out_grad[0]
-    (normed_all, qkv, qkv_w, table, gains_all, infos, out_part, gate_up_w, down_w, grad_all) = first_part(
-        hidden_low, gains, info, base, step, weights, grad_low, depth, 0
-    )
-    starts = infos[:, 0].reshape(plane, 2, LANES // 2)[:, :, 0].reshape(2 * plane)
-    rank = ((starts - jnp.min(starts)) // BLOCK).astype(jnp.int32)
-    blocks = 2 * plane
-    order = jnp.sum(
-        jnp.where(rank[None, :] == jnp.arange(blocks)[:, None], jnp.arange(blocks)[None, :], 0), 1
-    ).astype(jnp.int32)
-
-    attended_low, lse, out_w, gate_up_w, down_w = attend(order, qkv, out_part, gate_up_w, down_w, 1)
-    mixed, mixed_grad, gain_two_grad, do, out_wgrad, gate_up_wgrad, down_wgrad, down_sum, _, _ = middle(
+    (normed_all, qkv, qkv_w, table, gains_all, order, rank, attended_low, lse, out_w, gate_up_w, down_w, grad_all) = first_part(
+        positions, hidden_low, gains, freq, step, weights, grad_low, depth, 0
+    )
+    (mixed, down_sum, mixed_grad, gain_two_grad, do, out_wgrad, gate_up_wgrad, down_wgrad, left, right, _, _) = middle(
         rank, attended_low, hidden_low, gains_all, grad_all, out_w.reshape(plane, -1, width), gate_up_w, down_w, 2
     )
     arrays = (qkv, attended_low, do, lse, table, qkv_w, gains_all, gain_two_grad)
-    large = (mixed, mixed_grad, hidden_low, normed_all, down_sum, out_wgrad, gate_up_wgrad, down_wgrad)
+    large = (mixed_grad, hidden_low, mixed, down_sum, normed_all, out_wgrad, gate_up_wgrad, down_wgrad, left, right)
     layer_out, input_grad, gain_sums, gate_up_all, down_all, qkv_all, out_grads = back(
         order, rank, arrays, large, depth, 3
     )
-    gate_total, up_total, down_total = widen_mlp(gate_up_all, down_all)
-    query_total, key_total, value_total, out_total = widen_attention(qkv_all, out_grads)
+    query_total, key_total, value_total = widen_heads(qkv_all)
+    gate_total, up_total, down_total, out_total, gain_one, gain_two = widen(gate_up_all, down_all, out_grads, gain_sums)
     return (
         layer_out[None],
         input_grad[None],
-        gain_sums[0],
+        gain_one,
         query_total,
         key_total,
         value_total,
         out_total,
-        gain_sums[4],
+        gain_two,
         gate_total,
         up_total,
         down_total,

time: 392 us -> 367 us (0.936)
  Pallas kernels: 374 us -> 357 us
  other arithmetic: 5.34 us -> 0 us
    pallas_call x3 -> x2, Pallas kernels: 49 us -> 16.7 us  [the longest x1 12.2 us: widen(): pl.pallas_call(kernel, grid=(8,), out_shape=(wide, wide, jax.ShapeDtypeSt...]
    pallas_call x1, Pallas kernels: 69.4 us -> 90 us  [first_part(): pl.pallas_call(first_kernel, out_shape=(shape((8, rows, width), BF16), sh...]
    pallas_call x1, Pallas kernels: 151 us -> 141 us  [back(): pl.pallas_call(back_kernel, out_shape=[shape((rows, width), BF16), shape(...]
    pallas_call x1, Pallas kernels: 104 us -> 109 us  [middle(): pl.pallas_call(middle_kernel, out_shape=(shape((rows, width), F32), shape...]
where the time goes in v5:
time: 367 us; the launch traced here: 362 us
  Pallas kernels  357 us (97%)
  local copies, waits for them, and re-layouts  4.26 us (1%)
    pallas_call x1, Pallas kernels, back(): pl.pallas_call(back_kernel, out_shape=[shape((rows, width), BF16), shape(...  141 us
    pallas_call x1, Pallas kernels, middle(): pl.pallas_call(middle_kernel, out_shape=(shape((rows, width), F32), shape...  109 us
    pallas_call x1, Pallas kernels, first_part(): pl.pallas_call(first_kernel, out_shape=(shape((8, rows, width), BF16), sh...  90 us
    pallas_call x1, Pallas kernels, widen(): pl.pallas_call(kernel, grid=(8,), out_shape=(wide, wide, jax.ShapeDtypeSt...  12.2 us

profile of v5, /device:TPU:0, one launch (start us, length us, event | category | flops | bytes accessed | tf_op | source)
XLA Modules:
  0.0 362.4 jit_solution(1037038788783183916)
XLA Ops:
  0.6 1.2 reshape.31.gain_one_ref
  1.9 1.2 reshape.32.gain_two_ref
  3.1 90.0 %first_part.1 = (bf16[8,256,1536]{2,1,0:T(8,128)(2,1)}, bf16[16,384,128]{2,1,0:T(8,128)(2,1)}, bf16[384,1536]{1,0:T(8,128)(2,1)}, f32[16,96,128]{2,1,0:T(8,128)}...) custom-call(s32[1,256]{1,0:T(1,128)} %pos_ref.1, ...), custom_call_target="tpu_custom_call" | custom-call | tf_op jit(solution)/shard_map/first_part/pallas_call | solution.py:850
  93.1 109.5 %middle.1 = (f32[256,1536]{1,0:T(8,128)}, bf16[4,256,1536]{2,1,0:T(8,128)(2,1)}, f32[256,1536]{1,0:T(8,128)}, f32[8,1536]{1,0:T(8,128)}, bf16[16,192,128]{2,1,0:...) custom-call(s32[16]{0:T(128)} %get-tuple-element.51.rank_ref, ...), custom_call_target="tpu_custom_call", output_to_operand_aliasing={{10}: (6, {}), {11}: (7, {})} | custom-call | tf_op jit(solution)/shard_map/middle/pallas_call | solution.py:1267
  202.6 140.8 %back.1 = (bf16[256,1536]{1,0:T(8,128)(2,1)}, bf16[256,1536]{1,0:T(8,128)(2,1)}, f32[8,384]{1,0:T(8,128)}, bf16[8,384,1024]{2,1,0:T(8,128)(2,1)}, bf16[8,128,153...) custom-call(s32[16]{0:T(128)} %get-tuple-element.50.order_ref, ...), custom_call_target="tpu_custom_call" | custom-call | tf_op jit(solution)/shard_map/back/pallas_call | solution.py:1655
  343.4 4.5 %widen_heads.1 = (f32[384,1536]{1,0:T(8,128)}, f32[384,768]{1,0:T(8,128)}, f32[384,768]{1,0:T(8,128)}) custom-call(bf16[8,384,384]{2,1,0:T(8,128)(2,1)} %get-tuple-element.80.a_ref), custom_call_target="tpu_custom_call" | custom-call | tf_op jit(solution)/shard_map/widen_heads/pallas_call | solution.py:1750
  347.9 0.0 copy-start.1
  347.9 0.0 copy-start
  347.9 12.2 %widen.1 = (f32[384,4096]{1,0:T(8,128)}, f32[384,4096]{1,0:T(8,128)}, f32[1024,1536]{1,0:T(8,128)}, f32[384,1536]{1,0:T(8,128)}, f32[384]{0:T(512)}, /*index=5*/f32[384]{0:T(512)}) custom-call(bf16[8,384,1024]{2,1,0:T(8,128)(2,1)} %get-tuple-element.75.a_ref, bf16[8,128,1536]{2,1,0:T(8,128)(2,1)} %get-tuple-element.76.d_ref, ...), custom_call_target="tpu_custom_call" | custom-call | tf_op jit(solution)/shard_map/widen/pallas_call | solution.py:1710
  360.1 0.0 copy-done.1
  360.1 0.9 copy.31
  361.0 0.0 copy-done
  361.0 0.9 copy.32
Async XLA Ops:
  347.9 12.2 %copy-start.1 = (bf16[256,1536]{1,0:T(8,128)(2,1)S(1)}, bf16[256,1536]{1,0:T(8,128)(2,1)}, u32[]{:S(2)}) copy-start(bf16[256,1536]{1,0:T(8,128)(2,1)} %get-tuple-element.73) | copy-start | bytes 2359300
  347.9 13.1 %copy-start = (bf16[256,1536]{1,0:T(8,128)(2,1)S(1)}, bf16[256,1536]{1,0:T(8,128)(2,1)}, u32[]{:S(2)}) copy-start(bf16[256,1536]{1,0:T(8,128)(2,1)} %get-tuple-element.74) | copy-start | bytes 2359300
